TPU v7x, 128 devices: a whole 4x4x4 slice. The times are simulated.
128 devices in a mesh: row: 8 (over x, core), col: 16 (over y, z).
Axes of the slice: x: 4, y: 4, z: 4, core: 2. Of those that a mesh axis runs over, the one named last changes fastest.
Arguments:
- front: bfloat16 [24576, 24576], P('row', 'col'), may hold values from -6 to 6
- diag_inverse: bfloat16 [256, 256], replicated, as said below
- fill_pattern: int32 [384, 384], replicated, may hold values from 0 to 1, as said below
Outputs:
- updated: bfloat16 [24576, 24576], P('row', 'col')
Inputs may be any that keep to these rules, and one draw needn't show every extreme that they name: `fill_pattern`: symmetric, with ones on the diagonal. `diag_inverse`: lower triangular.
All inputs are finite; a program needn't handle non-finite values.
Results may differ from a plain program's by a relative error of at most 0.0045.
Values may be sent and summed in bfloat16 or wider, within the bound.
No kernel may reach another device: no remote copies, remote signals or barrier semaphores. Data moves between devices by JAX's collectives and lax.ppermute only.
A program may use at most 128 MiB of HBM per device.

v0:
```python
import jax
import jax.numpy as jnp
from jax import lax
from jax.sharding import PartitionSpec as P

B = 64
P_SIZE = 256


def broadcast(block, axis, owner):
    block = jnp.where(lax.axis_index(axis) == owner, block, jnp.zeros_like(block))
    return lax.psum(block, axis)


def body(front, diag_inverse, fill_pattern):
    rows, cols = front.shape
    n_row = lax.axis_size("row")
    n_col = lax.axis_size("col")
    block = B
    width = P_SIZE
    panel_blocks = width // block
    row_id = lax.axis_index("row")
    col_id = lax.axis_index("col")
    owner = col_id < panel_blocks
    first = jnp.minimum(col_id, panel_blocks - 1)
    contract = (((1,), (1,)), ((), ()))
    weights_part = lax.dynamic_slice_in_dim(diag_inverse, first * block, block, 1)
    term = lax.dot_general(
        front[:, :block], weights_part, contract, preferred_element_type=jnp.float32
    )
    term = jnp.where(owner, term, jnp.zeros_like(term))
    factor = lax.psum(term, "col").astype(jnp.bfloat16)
    ratio = n_col // n_row
    local_rows = rows // block
    local_cols = cols // block
    grouped = factor.reshape(local_cols, ratio, block, width)
    chosen = lax.dynamic_index_in_dim(grouped, col_id // n_row, 1, keepdims=False).reshape(
        cols, width
    )
    col_factor = broadcast(chosen, "row", col_id % n_row)
    product = lax.dot_general(factor, col_factor, contract, preferred_element_type=jnp.float32)
    pattern_grid = fill_pattern.reshape(local_rows, n_row, local_cols, n_col)
    picked = lax.dynamic_index_in_dim(pattern_grid, row_id, 1, keepdims=False)
    picked = lax.dynamic_index_in_dim(picked, col_id, 2, keepdims=False)
    row_global = jnp.arange(local_rows, dtype=jnp.int32) * n_row + row_id
    col_global = jnp.arange(local_cols, dtype=jnp.int32) * n_col + col_id
    keep = picked.astype(jnp.float32)
    keep = keep * (row_global >= panel_blocks).astype(jnp.float32)[:, None]
    keep = keep * (col_global >= panel_blocks).astype(jnp.float32)[None, :]
    spread = jnp.repeat(keep, block, axis=1)
    updated = (
        front.astype(jnp.float32).reshape(local_rows, block, cols)
        - product.reshape(local_rows, block, cols) * spread[:, None, :]
    )
    updated = updated.reshape(rows, cols).astype(jnp.bfloat16)
    panel_piece = lax.dynamic_slice_in_dim(factor, first * block, block, 1)
    leading = jnp.where(owner, panel_piece, updated[:, :block])
    return updated.at[:, :block].set(leading)


def solution(mesh):
    return jax.shard_map(
        body,
        mesh=mesh,
        in_specs=(P("row", "col"), P(), P()),
        out_specs=P("row", "col"),
        check_vma=False,
    )
```

profile of v0, /device:TPU:7, one launch (start us, length us, event | category | flops | bytes accessed | tf_op | source)
XLA Modules:
  0.0 205.0 jit_solution(7237751642170792720)
XLA Ops:
  6.5 0.0 copy-start
  6.5 0.0 all-reduce.3.cloned.1.call-start
  6.5 0.9 copy-done
  7.4 3.4 %fusion = f32[3072,256]{0,1:T(8,128)} fusion(pred[]{:T(512)S(6)} %lt.23, bf16[3072,1536]{1,0:T(8,128)(2,1)} %param.5, bf16[256,256]{1,0:T(8,128)(2,1)S(1)} %copy-done, s32[]{:T(128)S(6)} %select_n.62), kind=kOutput, calls=%fused_computation.2 | convolution fusion | flops 101449728 | bytes 3997701 | tf_op jit(solution)/shard_map/dot_general | solution.py:28
  10.8 87.0 %all-reduce.4 = bf16[3072,256]{0,1:T(8,128)(2,1)S(1)} all-reduce(f32[3072,256]{0,1:T(8,128)} %fusion), channel_id=1, replica_groups=mesh['row'=8,'col'=16] {'col'}, use_global_device_ids=true, to_apply=%region_0.1 | all-reduce | flops 786432 | bytes 4718592 | tf_op jit(solution)/shard_map/psum | solution.py:32
  97.9 0.7 copy.14
  98.6 1.0 dynamic-slice_select_fusion
  99.6 0.0 all-reduce.3.cloned.1.call-update
  99.6 0.0 copy-start.2
  99.6 12.7 %copy.13 = bf16[3072,1536]{0,1:T(8,128)(2,1)} copy(bf16[3072,1536]{1,0:T(8,128)(2,1)} %param.5) | data formatting | bytes 18874368 | tf_op args[0]
  112.3 0.0 copy-done.2
  112.3 2.9 %reshape.60 = s32[48,8,24,16]{3,2,1,0:T(8,128)} reshape(s32[384,384]{1,0:T(8,128)S(1)} %copy-done.2) | data formatting | bytes 1179648 | tf_op jit(solution)/shard_map/reshape | solution.py:42
  115.2 1.3 constant_dynamic-slice_fusion
  116.5 0.3 copy.19
  116.8 0.1 fusion.4
  116.9 0.1 copy.16
  117.0 0.2 broadcast_in_dim.13
  117.2 0.2 mul.58
  117.4 8.9 %mul.59 = f32[48,64,1536]{2,1,0:T(8,128)} broadcast(f32[48,1536]{1,0:T(8,128)S(1)} %mul.58), dimensions={0,2} | broadcast | bytes 19169280 | tf_op jit(solution)/shard_map/mul | solution.py:53
  126.2 18.7 %copy.17 = f32[3072,1536]{0,1:T(8,128)} copy(f32[3072,1536]{1,0:T(8,128)} %bitcast.11) | data formatting | bytes 37748736 | tf_op jit(solution)/shard_map/mul | solution.py:53
  144.9 0.7 compare_reduce_fusion
  145.6 22.5 %all-reduce.3.cloned.1.call-done = bf16[1536,256]{1,0:T(8,128)(2,1)} async-done(((bf16[1536,256]{1,0:T(8,128)(2,1)}), bf16[1536,256]{1,0:T(8,128)(2,1)}) %all-reduce.3.cloned.1.call-update) | async-done | bytes 786448 | tf_op jit(solution)/shard_map/psum | solution.py:12
  168.1 14.9 %subtract_convert_fusion = bf16[3072,1536]{0,1:T(8,128)(2,1)} fusion(f32[3072,1536]{0,1:T(8,128)} %copy.17, bf16[3072,1536]{0,1:T(8,128)(2,1)} %copy.13, bf16[1536,256]{1,0:T(8,128)(2,1)} %all-reduce.3.cloned.1.call-done, bf16[3072,256]{0,1:T(8,128)(2,1)S(1)} %all-reduce.4), kind=kOutput, calls=%fused_computation | convolution fusion | flops 2434793472 | bytes 40108032 | tf_op jit(solution)/shard_map/dot_general | solution.py:41
  183.0 0.0 copy-start.1
  183.0 2.6 %fusion.2 = bf16[3072,1536]{0,1:T(8,128)(2,1)} fusion(bf16[3072,1536]{0,1:T(8,128)(2,1)} %subtract_convert_fusion, bf16[3072,256]{0,1:T(8,128)(2,1)S(1)} %all-reduce.4, s32[]{:T(128)S(6)} %select_n.62, pred[]{:T(512)S(6)} %lt.23, pred[]{:T(512)} %compare_reduce_fusion), kind=kLoop, calls=%fused_computation.6 | loop fusion | flops 393216 | bytes 1180165 | tf_op jit(solution)/shard_map/scatter | solution.py:58
  185.5 12.6 %copy.18 = bf16[3072,1536]{1,0:T(8,128)(2,1)} copy(bf16[3072,1536]{0,1:T(8,128)(2,1)} %fusion.2) | data formatting | bytes 18874368 | tf_op jit(solution)/shard_map/scatter | solution.py:58
  198.1 0.0 copy-done.1
  (2 shorter events, 0.0 us)
Async XLA Ops:
  6.5 0.9 copy-start
  6.5 161.5 %all-reduce.3.cloned.1.call-start = ((), (), s32[]{:S(2)}) async-start(), calls=%async_computation | async-start | bytes 1572864 | tf_op jit(solution)/shard_map/psum | solution.py:12
  99.6 12.7 %copy-start.2 = (s32[384,384]{1,0:T(8,128)S(1)}, s32[384,384]{1,0:T(8,128)}, u32[]{:S(2)}) copy-start(s32[384,384]{1,0:T(8,128)} %param.7) | copy-start | bytes 1769476
  183.0 15.2 %copy-start.1 = (bf16[256,256]{1,0:T(8,128)(2,1)S(1)}, bf16[256,256]{1,0:T(8,128)(2,1)}, u32[]{:S(2)}) copy-start(bf16[256,256]{1,0:T(8,128)(2,1)} %param.6) | copy-start | bytes 393220
Sparse Core Ops, SparseCore 0:
  99.7 68.2 all-reduce.2
where the time goes:
time: 207 us; the launch traced here: 205 us
  blocking collectives  87 us (42%)
  local copies, waits for them, and re-layouts  59.4 us (29%)
  waiting for transfers between devices  22.5 us (11%)
  matrix products  18.3 us (9%)
  between operations  13.5 us (7%)
  other arithmetic  4.34 us (2%)
    psum x1, blocking collectives, body(): factor = lax.psum(term, 'col').astype(jnp.bfloat16)  87 us
    mul x3, local copies, waits for them, and re-layouts, body(): product.reshape(local_rows, block, cols) * spread[:, None, :]  27.7 us
    psum x1, waiting for transfers between devices, broadcast(): return lax.psum(block, axis)  22.5 us
    dot_general x1, matrix products, body(): lax.dot_general(factor, col_factor, contract, preferred_element_type=jnp....  14.9 us
    unnamed x8, local copies, waits for them, and re-layouts  13.8 us
    scatter x1, local copies, waits for them, and re-layouts, body(): return updated.at[:, :block].set(leading)  12.6 us
  transfers between devices with their start and end apart: 1, of which 1 were waited for; matrix products, arithmetic and copies ran while one was open for 22% of the time, Pallas kernels for 0%

commit v1 on v0

v1 whole, which is shorter than its diff:
```python
import functools

import jax
import jax.numpy as jnp
import numpy as np
from jax import lax
from jax.experimental import pallas as pl
from jax.experimental.pallas import tpu as pltpu
from jax.sharding import Mesh, PartitionSpec as P

BF16 = jnp.bfloat16
F32 = jnp.float32
B = 64
Q = 4
BLOCKS = 48
PAIRS = 24
HALF = 12
ROWS = HALF * B
COLS = 1536
WIDTH = 256
ALL = ("x", "core", "y", "z")
VMEM = pltpu.VMEM
NT = (((1,), (1,)), ((), ()))


def linear(x, core, y, z):
    return ((x * 2 + core) * 4 + y) * 4 + z


def quarter_of(y, z):
    return (z + 2 * (y // 2)) % 4


def spread_perm(step):
    pairs = []
    for x in range(4):
        for core in range(2):
            for j in range(4):
                target = [(1, j), (2, (j + 2) % 4), (3, (j + 2) % 4)][step]
                pairs.append((linear(x, core, 0, j), linear(x, core, *target)))
    return pairs


def column_perm(step):
    pairs = []
    for x in range(4):
        for core in range(2):
            r = 2 * x + core
            for y in range(4):
                for z in range(4):
                    q = quarter_of(y, z)
                    half = step if q < 2 else 1 - step
                    target = linear((y + x) % 4, q % 2, 2 * half + r // 4, r % 4)
                    pairs.append((linear(x, core, y, z), target))
    return pairs


def pack_kernel(front_ref, out_ref):
    flip = lax.axis_index("z") // 2
    for k in range(2):
        parity = jnp.bitwise_xor(k, flip)
        left = front_ref[:HALF, parity, :, :].reshape(ROWS, 128)
        right = front_ref[HALF:, parity, :, :].reshape(ROWS, 128)
        out_ref[k] = jnp.concatenate([left[:, :B], right[:, :B]], axis=1)


def pack(front4):
    return pl.pallas_call(
        pack_kernel,
        grid=(1,),
        out_shape=jax.ShapeDtypeStruct((2, ROWS, 128), BF16),
        in_specs=[pl.BlockSpec((PAIRS, 2, B, 128), lambda i: (0, 0, 0, 0))],
        out_specs=pl.BlockSpec((2, ROWS, 128), lambda i: (0, 0, 0)),
        compiler_params=pltpu.CompilerParams(vmem_limit_bytes=16 << 20),
    )(front4)


def choose_kernel(a_ref, b_ref, c_ref, d_ref, own_ref, first_ref, second_ref):
    y = lax.axis_index("y")
    for k, ref in enumerate((a_ref, b_ref, c_ref, d_ref)):

        @pl.when(y == k)
        def _():
            own_ref[...] = ref[...]
            first_ref[...] = ref[0]
            second_ref[...] = ref[1]


def choose(a, b, c, d):
    whole = pl.BlockSpec(memory_space=VMEM)
    return pl.pallas_call(
        choose_kernel,
        out_shape=(
            jax.ShapeDtypeStruct((2, ROWS, 128), BF16),
            jax.ShapeDtypeStruct((ROWS, 128), BF16),
            jax.ShapeDtypeStruct((ROWS, 128), BF16),
        ),
        in_specs=[whole] * 4,
        out_specs=(whole,) * 3,
        compiler_params=pltpu.CompilerParams(vmem_limit_bytes=16 << 20),
    )(a, b, c, d)


def prepare_kernel(diag_ref, pattern_ref, row_w_ref, col_w_ref, mask_ref):
    x, core = lax.axis_index("x"), lax.axis_index("core")
    y, z = lax.axis_index("y"), lax.axis_index("z")
    own = lax.rem(z + 2 * (y // 2), 4)
    diag = diag_ref[...]
    eye = (
        lax.broadcasted_iota(jnp.int32, (WIDTH, WIDTH), 0)
        == lax.broadcasted_iota(jnp.int32, (WIDTH, WIDTH), 1)
    ).astype(BF16)
    turned = lax.dot_general(eye, diag, NT, preferred_element_type=F32).astype(BF16)
    for q in range(Q):
        slot = lax.rem(q - own + 4, 4)
        part = turned[q * B : q * B + B, :]
        zero = jnp.zeros_like(part)
        row_w_ref[0, slot] = jnp.concatenate([part, zero], axis=0)
        row_w_ref[1, slot] = jnp.concatenate([zero, part], axis=0)
        half = y // 2
        other = jnp.where(q % 2 == core, 0, 2)
        late = jnp.where(q // 2 == half, 0, 1)
        part = diag[:, q * B : q * B + B]
        zero = jnp.zeros_like(part)
        col_w_ref[0, other + late] = jnp.concatenate([part, zero], axis=1)
        col_w_ref[1, other + late] = jnp.concatenate([zero, part], axis=1)
    row_id = x * 2 + core
    col_id = y * 4 + z
    count = pattern_ref.shape[0]
    rows = (
        lax.broadcasted_iota(jnp.int32, (BLOCKS, count), 0) * 8 + row_id
        == lax.broadcasted_iota(jnp.int32, (BLOCKS, count), 1)
    ).astype(BF16)
    cols = (
        lax.broadcasted_iota(jnp.int32, (count, COLS), 0)
        == lax.broadcasted_iota(jnp.int32, (count, COLS), 1) // B * 16 + col_id
    ).astype(BF16)
    picked = jnp.dot(
        rows, pattern_ref[...].astype(F32).astype(BF16), preferred_element_type=F32
    ).astype(BF16)
    keep = jnp.dot(picked, cols, preferred_element_type=F32)
    stored_row = lax.broadcasted_iota(jnp.int32, (BLOCKS, COLS), 0)
    stored_col = lax.broadcasted_iota(jnp.int32, (BLOCKS, COLS), 1) // B
    inside = (stored_row * 8 + row_id >= Q) & (stored_col * 16 + col_id >= Q)
    mask_ref[...] = jnp.where(inside, keep, 0.0)


def prepare(diag_inverse, fill_pattern):
    whole = pl.BlockSpec(memory_space=VMEM)
    return pl.pallas_call(
        prepare_kernel,
        out_shape=(
            jax.ShapeDtypeStruct((2, Q, 128, WIDTH), BF16),
            jax.ShapeDtypeStruct((2, Q, WIDTH, 128), BF16),
            jax.ShapeDtypeStruct((BLOCKS, COLS), F32),
        ),
        in_specs=[whole] * 2,
        out_specs=(whole,) * 3,
        compiler_params=pltpu.CompilerParams(vmem_limit_bytes=24 << 20),
    )(diag_inverse, fill_pattern)


TILE = 4
CHUNK = 512


def update_kernel(
    front_ref, p0, p1, p2, p3, g0, g1, g2, g3, row_w_ref, col_w_ref, mask_ref, out_ref, gt_ref
):
    parity, i = pl.program_id(0), pl.program_id(1)
    y, z = lax.axis_index("y"), lax.axis_index("z")
    col_id = y * 4 + z
    owner = col_id < Q
    own = lax.rem(z + 2 * (y // 2), 4)

    @pl.when((parity == 0) & (i == 0))
    def _():
        for u in range(2):
            total = jnp.zeros((WIDTH, ROWS), F32)
            for k, g in enumerate((g0, g1, g2, g3)):
                total += lax.dot_general(
                    col_w_ref[u, k], g[...], NT, preferred_element_type=F32
                )
            gt_ref[:, u * ROWS : (u + 1) * ROWS] = total.astype(BF16)

        @pl.when(owner)
        def _():
            lane = lax.broadcasted_iota(jnp.int32, (WIDTH, 128), 1)
            line = lax.broadcasted_iota(jnp.int32, (WIDTH, 128), 0)
            pick = (line == lane + col_id * B).astype(F32)
            old = gt_ref[:, :128].astype(F32)
            gt_ref[:, :128] = jnp.where(lane < B, pick, old).astype(BF16)

    u = i // (HALF // TILE)
    start = pl.multiple_of(lax.rem(i, HALF // TILE) * (TILE * B), TILE * B)
    total = jnp.zeros((TILE * B, WIDTH), F32)
    for k, p in enumerate((p0, p1, p2, p3)):
        q = lax.rem(own + k, 4)
        slot = jnp.bitwise_xor(parity, q // 2)
        total += jnp.dot(
            p[slot, pl.ds(start, TILE * B), :], row_w_ref[u, k], preferred_element_type=F32
        )
    factor = total.astype(BF16)
    lane = lax.broadcasted_iota(jnp.int32, (B, CHUNK), 1)
    for c in range(COLS // CHUNK):
        cols = slice(c * CHUNK, (c + 1) * CHUNK)
        product = jnp.dot(factor, gt_ref[:, cols], preferred_element_type=F32)
        for b in range(TILE):
            part = product[b * B : b * B + B]
            keep = mask_ref[pl.ds(2 * (TILE * i + b) + parity, 1), cols]
            new = front_ref[b, 0, :, cols].astype(F32) - part * keep
            if c == 0:
                new = jnp.where(owner & (lane < B), part, new)
            out_ref[b, 0, :, cols] = new.astype(BF16)


def update(front4, parts, columns, row_w, col_w, mask):
    whole = pl.BlockSpec(memory_space=VMEM)
    tile = pl.BlockSpec((TILE, 1, B, COLS), lambda p, i: (i, p, 0, 0))
    return pl.pallas_call(
        update_kernel,
        grid=(2, PAIRS // TILE),
        out_shape=jax.ShapeDtypeStruct((PAIRS, 2, B, COLS), BF16),
        in_specs=[tile] + [whole] * 11,
        out_specs=tile,
        scratch_shapes=[VMEM((WIDTH, COLS), BF16)],
        compiler_params=pltpu.CompilerParams(vmem_limit_bytes=32 << 20),
        cost_estimate=pl.CostEstimate(
            flops=2 * 3072 * 1536 * 256, bytes_accessed=4 * 3072 * 1536, transcendentals=0
        ),
    )(front4, *parts, *columns, row_w, col_w, mask)


def body(front, diag_inverse, fill_pattern):
    front4 = front.reshape(PAIRS, 2, B, COLS)
    packed = pack(front4)
    row_w, col_w, mask = prepare(diag_inverse, fill_pattern)
    spread = [lax.ppermute(packed, ALL, spread_perm(k)) for k in range(3)]
    own, first, second = choose(packed, *spread)
    g0 = lax.ppermute(first, ALL, column_perm(0))
    g1 = lax.ppermute(second, ALL, column_perm(1))
    z_next = lax.ppermute(own, "z", [((i + 1) % 4, i) for i in range(4)])
    z_prev = lax.ppermute(own, "z", [(i, (i + 1) % 4) for i in range(4)])
    y_pair = lax.ppermute(own, "y", [(1, 2), (2, 1), (3, 0), (0, 3)])
    swap = [(0, 1), (1, 0)]
    g2 = lax.ppermute(g0, "core", swap)
    g3 = lax.ppermute(g1, "core", swap)
    out = update(
        front4, (own, z_next, y_pair, z_prev), (g0, g1, g2, g3), row_w, col_w, mask
    )
    return out.reshape(front.shape)


def solution(mesh):
    fine = Mesh(mesh.devices.reshape(4, 2, 4, 4), ALL)
    spec = P(("x", "core"), ("y", "z"))
    return jax.shard_map(
        body,
        mesh=fine,
        in_specs=(spec, P(), P()),
        out_specs=spec,
        check_vma=False,
    )
```

time: 207 us -> 71.3 us (0.34)
  blocking collectives: 87 us -> 0 us
  local copies, waits for them, and re-layouts: 59.4 us -> 3.69 us
  starting transfers between devices: 0.01 us -> 27.9 us
  matrix products: 18.3 us -> 0 us
  Pallas kernels: 0 us -> 13.9 us
  between operations: 13.5 us -> 0.07 us
  other arithmetic: 4.34 us -> 0 us
  waiting for transfers between devices: 22.5 us -> 25.6 us
    psum x1 -> x0, blocking collectives: 87 us -> none  [body(): factor = lax.psum(term, 'col').astype(jnp.bfloat16)]
    ppermute x0 -> x10, starting transfers between devices: none -> 27.9 us  [the longest x3 10.9 us: body(): spread = [lax.ppermute(packed, ALL, spread_perm(k)) for k in range(3)]]
    mul x4 -> x0, local copies, waits for them, and re-layouts: 27.8 us -> none  [the longest x3 27.7 us: body(): product.reshape(local_rows, block, cols) * spread[:, None, :]]
    ppermute x0 -> x10, waiting for transfers between devices: none -> 25.6 us  [the longest x3 14.8 us: body(): spread = [lax.ppermute(packed, ALL, spread_perm(k)) for k in range(3)]]
    psum x1 -> x0, waiting for transfers between devices: 22.5 us -> none  [broadcast(): return lax.psum(block, axis)]
    dot_general x2 -> x0, matrix products: 18.3 us -> none  [the longest x1 14.9 us: body(): lax.dot_general(factor, col_factor, contract, preferred_element_type=jnp....]
    pallas_call x0 -> x4, Pallas kernels: none -> 13.9 us  [the longest x1 13 us: update(): pl.pallas_call(update_kernel, grid=(2, PAIRS // TILE), out_shape=jax.Shap...]
    scatter x1 -> x0, local copies, waits for them, and re-layouts: 12.6 us -> none  [body(): return updated.at[:, :block].set(leading)]
  transfers between devices with their start and end apart: 1 -> 10, of which waited for: 1 -> 7; matrix products, arithmetic and copies ran while one was open for 22% -> 0% of each run, Pallas kernels for 0% -> 1%
where the time goes in v1:
time: 71.3 us; the launch traced here: 71.1 us
  starting transfers between devices  27.9 us (39%)
  waiting for transfers between devices  25.6 us (36%)
  Pallas kernels  13.9 us (19%)
  local copies, waits for them, and re-layouts  3.69 us (5%)
    ppermute x3, waiting for transfers between devices, body(): spread = [lax.ppermute(packed, ALL, spread_perm(k)) for k in range(3)]  14.8 us
    pallas_call x1, Pallas kernels, update(): pl.pallas_call(update_kernel, grid=(2, PAIRS // TILE), out_shape=jax.Shap...  13 us
    ppermute x3, starting transfers between devices, body(): spread = [lax.ppermute(packed, ALL, spread_perm(k)) for k in range(3)]  10.9 us
    ppermute x1, starting transfers between devices, body(): g0 = lax.ppermute(first, ALL, column_perm(0))  5.69 us
    ppermute x1, waiting for transfers between devices, body(): y_pair = lax.ppermute(own, 'y', [(1, 2), (2, 1), (3, 0), (0, 3)])  5.34 us
    unnamed x8, local copies, waits for them, and re-layouts  3.69 us
    ppermute x1, waiting for transfers between devices, body(): g0 = lax.ppermute(first, ALL, column_perm(0))  3.45 us
    ppermute x1, starting transfers between devices, body(): z_next = lax.ppermute(own, 'z', [((i + 1) % 4, i) for i in range(4)])  2.58 us
  transfers between devices with their start and end apart: 10, of which 7 were waited for; matrix products, arithmetic and copies ran while one was open for 0% of the time, Pallas kernels for 1%

profile of v1, /device:TPU:7, one launch (start us, length us, event | category | flops | bytes accessed | tf_op | source)
XLA Modules:
  0.0 71.1 jit_solution(6360622647178304248)
XLA Ops:
  0.0 0.0 copy-start
  0.0 3.7 %copy-done = bf16[3072,1536]{1,0:T(8,128)(2,1)S(1)} copy-done((bf16[3072,1536]{1,0:T(8,128)(2,1)S(1)}, bf16[3072,1536]{1,0:T(8,128)(2,1)}, u32[]{:S(2)}) %copy-start) | copy-done | bytes 9437208
  3.7 0.0 copy-start.2
  3.7 0.0 copy-start.3
  3.7 0.0 copy-start.1
  3.7 0.3 shard_map.37.a_ref
  4.0 8.2 %collective-permute-start.2 = (bf16[2,768,128]{2,1,0:T(8,128)(2,1)S(1)}, bf16[2,768,128]{2,1,0:T(8,128)(2,1)S(1)}, u32[]{:S(2)}, u32[]{:S(2)}) collective-permute-start(bf16[2,768,128]{2,1,0:T(8,128)(2,1)S(1)} %shard_map.37.a_ref), channel_id=1, source_target_pairs={{0,14},{1,15},{2,12},{3,13},{16,30},{17,31},{18,28},{19,29},{32,46... | collective-permute-start | bytes 1179656 | tf_op jit(solution)/shard_map/ppermute | solution.py:238
  12.2 1.3 %collective-permute-start.1 = (bf16[2,768,128]{2,1,0:T(8,128)(2,1)S(1)}, bf16[2,768,128]{2,1,0:T(8,128)(2,1)S(1)}, u32[]{:S(2)}, u32[]{:S(2)}) collective-permute-start(bf16[2,768,128]{2,1,0:T(8,128)(2,1)S(1)} %shard_map.37.a_ref), channel_id=1, source_target_pairs={{0,10},{1,11},{2,8},{3,9},{16,26},{17,27},{18,24},{19,25},{32,42},... | collective-permute-start | bytes 1179656 | tf_op jit(solution)/shard_map/ppermute | solution.py:238
  13.6 1.3 %collective-permute-start = (bf16[2,768,128]{2,1,0:T(8,128)(2,1)S(1)}, bf16[2,768,128]{2,1,0:T(8,128)(2,1)S(1)}, u32[]{:S(2)}, u32[]{:S(2)}) collective-permute-start(bf16[2,768,128]{2,1,0:T(8,128)(2,1)S(1)} %shard_map.37.a_ref), channel_id=1, source_target_pairs={{0,4},{1,5},{2,6},{3,7},{16,20},{17,21},{18,22},{19,23},{32,36},{3... | collective-permute-start | bytes 1179656 | tf_op jit(solution)/shard_map/ppermute | solution.py:238
  14.9 5.1 %collective-permute-done.2.d_ref = bf16[2,768,128]{2,1,0:T(8,128)(2,1)S(1)} collective-permute-done((bf16[2,768,128]{2,1,0:T(8,128)(2,1)S(1)}, bf16[2,768,128]{2,1,0:T(8,128)(2,1)S(1)}, u32[]{:S(2)}, u32[]{:S(2)}) %collective-permute-start.2) | collective-permute-done | bytes 393248 | tf_op jit(solution)/shard_map/ppermute | solution.py:238
  20.0 1.3 %collective-permute-done.1.c_ref = bf16[2,768,128]{2,1,0:T(8,128)(2,1)S(1)} collective-permute-done((bf16[2,768,128]{2,1,0:T(8,128)(2,1)S(1)}, bf16[2,768,128]{2,1,0:T(8,128)(2,1)S(1)}, u32[]{:S(2)}, u32[]{:S(2)}) %collective-permute-start.1) | collective-permute-done | bytes 393248 | tf_op jit(solution)/shard_map/ppermute | solution.py:238
  21.3 8.4 %collective-permute-done.b_ref = bf16[2,768,128]{2,1,0:T(8,128)(2,1)S(1)} collective-permute-done((bf16[2,768,128]{2,1,0:T(8,128)(2,1)S(1)}, bf16[2,768,128]{2,1,0:T(8,128)(2,1)S(1)}, u32[]{:S(2)}, u32[]{:S(2)}) %collective-permute-start) | collective-permute-done | bytes 393248 | tf_op jit(solution)/shard_map/ppermute | solution.py:238
  29.7 0.1 shard_map.38
  29.9 5.7 %collective-permute-start.6 = (bf16[768,128]{1,0:T(8,128)(2,1)S(1)}, bf16[768,128]{1,0:T(8,128)(2,1)S(1)}, u32[]{:S(2)}, u32[]{:S(2)}) collective-permute-start(bf16[768,128]{1,0:T(8,128)(2,1)S(1)} %get-tuple-element.12), channel_id=1, source_target_pairs={{0,0},{1,16},{2,8},{3,24},{4,32},{5,48},{6,40},{7,56},{8,72},{9,88... | collective-permute-start | bytes 589832 | tf_op jit(solution)/shard_map/ppermute | solution.py:240
  35.5 2.4 %collective-permute-start.7 = (bf16[768,128]{1,0:T(8,128)(2,1)S(1)}, bf16[768,128]{1,0:T(8,128)(2,1)S(1)}, u32[]{:S(2)}, u32[]{:S(2)}) collective-permute-start(bf16[768,128]{1,0:T(8,128)(2,1)S(1)} %get-tuple-element.13), channel_id=1, source_target_pairs={{0,8},{1,24},{2,0},{3,16},{4,40},{5,56},{6,32},{7,48},{8,64},{9,80... | collective-permute-start | bytes 589832 | tf_op jit(solution)/shard_map/ppermute | solution.py:241
  37.9 1.4 %collective-permute-start.5 = (bf16[2,768,128]{2,1,0:T(8,128)(2,1)S(1)}, bf16[2,768,128]{2,1,0:T(8,128)(2,1)S(1)}, u32[]{:S(2)}, u32[]{:S(2)}) collective-permute-start(bf16[2,768,128]{2,1,0:T(8,128)(2,1)S(1)} %get-tuple-element.11.p0), channel_id=1, source_target_pairs={{0,1},{1,2},{2,3},{3,0},{4,5},{5,6},{6,7},{7,4},{8,9},{9,10},{10,1... | collective-permute-start | bytes 1179656 | tf_op jit(solution)/shard_map/ppermute | solution.py:243
  39.3 1.0 %collective-permute-start.4 = (bf16[2,768,128]{2,1,0:T(8,128)(2,1)S(1)}, bf16[2,768,128]{2,1,0:T(8,128)(2,1)S(1)}, u32[]{:S(2)}, u32[]{:S(2)}) collective-permute-start(bf16[2,768,128]{2,1,0:T(8,128)(2,1)S(1)} %get-tuple-element.11.p0), channel_id=1, source_target_pairs={{4,8},{8,4},{12,0},{0,12},{5,9},{9,5},{13,1},{1,13},{6,10},{10,6},... | collective-permute-start | bytes 1179656 | tf_op jit(solution)/shard_map/ppermute | solution.py:244
  40.3 2.6 %collective-permute-start.3 = (bf16[2,768,128]{2,1,0:T(8,128)(2,1)S(1)}, bf16[2,768,128]{2,1,0:T(8,128)(2,1)S(1)}, u32[]{:S(2)}, u32[]{:S(2)}) collective-permute-start(bf16[2,768,128]{2,1,0:T(8,128)(2,1)S(1)} %get-tuple-element.11.p0), channel_id=1, source_target_pairs={{1,0},{2,1},{3,2},{0,3},{5,4},{6,5},{7,6},{4,7},{9,8},{10,9},{11,1... | collective-permute-start | bytes 1179656 | tf_op jit(solution)/shard_map/ppermute | solution.py:242
  42.9 3.5 %collective-permute-done.6.g0 = bf16[768,128]{1,0:T(8,128)(2,1)S(1)} collective-permute-done((bf16[768,128]{1,0:T(8,128)(2,1)S(1)}, bf16[768,128]{1,0:T(8,128)(2,1)S(1)}, u32[]{:S(2)}, u32[]{:S(2)}) %collective-permute-start.6) | collective-permute-done | bytes 196640 | tf_op jit(solution)/shard_map/ppermute | solution.py:240
  46.3 2.2 %collective-permute-start.8 = (bf16[768,128]{1,0:T(8,128)(2,1)S(1)}, bf16[768,128]{1,0:T(8,128)(2,1)S(1)}, u32[]{:S(2)}, u32[]{:S(2)}) collective-permute-start(bf16[768,128]{1,0:T(8,128)(2,1)S(1)} %collective-permute-done.6.g0), channel_id=1, source_target_pairs={{0,16},{16,0},{1,17},{17,1},{2,18},{18,2},{3,19},{19,3},{4,20},{20... | collective-permute-start | bytes 589832 | tf_op jit(solution)/shard_map/ppermute | solution.py:246
  48.5 0.0 collective-permute-done.7.g1
  48.5 1.8 %collective-permute-start.9 = (bf16[768,128]{1,0:T(8,128)(2,1)S(1)}, bf16[768,128]{1,0:T(8,128)(2,1)S(1)}, u32[]{:S(2)}, u32[]{:S(2)}) collective-permute-start(bf16[768,128]{1,0:T(8,128)(2,1)S(1)} %collective-permute-done.7.g1), channel_id=1, source_target_pairs={{0,16},{16,0},{1,17},{17,1},{2,18},{18,2},{3,19},{19,3},{4,20},{20... | collective-permute-start | bytes 589832 | tf_op jit(solution)/shard_map/ppermute | solution.py:247
  50.3 0.0 copy-done.2
  50.3 0.0 copy-done.3
  50.3 0.5 shard_map.39
  50.9 0.0 collective-permute-done.8.g2
  50.9 0.5 collective-permute-done.9.g3
  51.4 1.4 %collective-permute-done.5.p3 = bf16[2,768,128]{2,1,0:T(8,128)(2,1)S(1)} collective-permute-done((bf16[2,768,128]{2,1,0:T(8,128)(2,1)S(1)}, bf16[2,768,128]{2,1,0:T(8,128)(2,1)S(1)}, u32[]{:S(2)}, u32[]{:S(2)}) %collective-permute-start.5) | collective-permute-done | bytes 393248 | tf_op jit(solution)/shard_map/ppermute | solution.py:243
  52.8 5.3 %collective-permute-done.4.p2 = bf16[2,768,128]{2,1,0:T(8,128)(2,1)S(1)} collective-permute-done((bf16[2,768,128]{2,1,0:T(8,128)(2,1)S(1)}, bf16[2,768,128]{2,1,0:T(8,128)(2,1)S(1)}, u32[]{:S(2)}, u32[]{:S(2)}) %collective-permute-start.4) | collective-permute-done | bytes 393248 | tf_op jit(solution)/shard_map/ppermute | solution.py:244
  58.1 0.0 collective-permute-done.3.p1
  58.1 0.0 copy-done.1
  58.2 13.0 %shard_map.40 = bf16[24,2,64,1536]{3,2,1,0:T(8,128)(2,1)} custom-call(bf16[24,2,64,1536]{3,2,1,0:T(8,128)(2,1)S(1)} %bitcast.3, bf16[2,768,128]{2,1,0:T(8,128)(2,1)S(1)} %get-tuple-element.11.p0, bf16[2,768,128]{2,1,0:T(8,128)(2,1)S(1)} %collective-permute-done.3.p1, bf16[2,768,128]{2,1,0:T(8,128)(2,1)S(1)} %collective-permute-done.4.p2, ...), custom_call_target="tpu_custom_call" | custom-call | flops 2415919104 | bytes 18874368 | tf_op jit(solution)/shard_map/pallas_call | solution.py:220
Async XLA Ops:
  0.0 3.7 %copy-start = (bf16[3072,1536]{1,0:T(8,128)(2,1)S(1)}, bf16[3072,1536]{1,0:T(8,128)(2,1)}, u32[]{:S(2)}) copy-start(bf16[3072,1536]{1,0:T(8,128)(2,1)} %param.3) | copy-start | bytes 28311556
  3.7 46.6 %copy-start.2 = (s32[384,384]{1,0:T(8,128)S(1)}, s32[384,384]{1,0:T(8,128)}, u32[]{:S(2)}) copy-start(s32[384,384]{1,0:T(8,128)} %pattern_ref.1) | copy-start | bytes 1769476
  3.7 46.6 %copy-start.3 = (bf16[256,256]{1,0:T(8,128)(2,1)S(1)}, bf16[256,256]{1,0:T(8,128)(2,1)}, u32[]{:S(2)}) copy-start(bf16[256,256]{1,0:T(8,128)(2,1)} %diag_ref.1) | copy-start | bytes 393220
  3.7 54.5 %copy-start.1 = (bf16[3072,1536]{1,0:T(8,128)(2,1)S(1)}, bf16[3072,1536]{1,0:T(8,128)(2,1)}, u32[]{:S(2)}) copy-start(bf16[3072,1536]{1,0:T(8,128)(2,1)} %param.3) | copy-start | bytes 28311556
  4.0 16.0 %collective-permute-start.2 = (bf16[2,768,128]{2,1,0:T(8,128)(2,1)S(1)}, bf16[2,768,128]{2,1,0:T(8,128)(2,1)S(1)}, u32[]{:S(2)}, u32[]{:S(2)}) collective-permute-start(bf16[2,768,128]{2,1,0:T(8,128)(2,1)S(1)} %shard_map.37.a_ref), channel_id=1, source_target_pairs={{0,14},{1,15},{2,12},{3,13},{16,30},{17,31},{18,28},{19,29},{32,46... | collective-permute-start | bytes 1179656 | tf_op jit(solution)/shard_map/ppermute | solution.py:238
  12.2 9.1 %collective-permute-start.1 = (bf16[2,768,128]{2,1,0:T(8,128)(2,1)S(1)}, bf16[2,768,128]{2,1,0:T(8,128)(2,1)S(1)}, u32[]{:S(2)}, u32[]{:S(2)}) collective-permute-start(bf16[2,768,128]{2,1,0:T(8,128)(2,1)S(1)} %shard_map.37.a_ref), channel_id=1, source_target_pairs={{0,10},{1,11},{2,8},{3,9},{16,26},{17,27},{18,24},{19,25},{32,42},... | collective-permute-start | bytes 1179656 | tf_op jit(solution)/shard_map/ppermute | solution.py:238
  13.6 16.2 %collective-permute-start = (bf16[2,768,128]{2,1,0:T(8,128)(2,1)S(1)}, bf16[2,768,128]{2,1,0:T(8,128)(2,1)S(1)}, u32[]{:S(2)}, u32[]{:S(2)}) collective-permute-start(bf16[2,768,128]{2,1,0:T(8,128)(2,1)S(1)} %shard_map.37.a_ref), channel_id=1, source_target_pairs={{0,4},{1,5},{2,6},{3,7},{16,20},{17,21},{18,22},{19,23},{32,36},{3... | collective-permute-start | bytes 1179656 | tf_op jit(solution)/shard_map/ppermute | solution.py:238
  29.9 16.5 %collective-permute-start.6 = (bf16[768,128]{1,0:T(8,128)(2,1)S(1)}, bf16[768,128]{1,0:T(8,128)(2,1)S(1)}, u32[]{:S(2)}, u32[]{:S(2)}) collective-permute-start(bf16[768,128]{1,0:T(8,128)(2,1)S(1)} %get-tuple-element.12), channel_id=1, source_target_pairs={{0,0},{1,16},{2,8},{3,24},{4,32},{5,48},{6,40},{7,56},{8,72},{9,88... | collective-permute-start | bytes 589832 | tf_op jit(solution)/shard_map/ppermute | solution.py:240
  35.5 12.9 %collective-permute-start.7 = (bf16[768,128]{1,0:T(8,128)(2,1)S(1)}, bf16[768,128]{1,0:T(8,128)(2,1)S(1)}, u32[]{:S(2)}, u32[]{:S(2)}) collective-permute-start(bf16[768,128]{1,0:T(8,128)(2,1)S(1)} %get-tuple-element.13), channel_id=1, source_target_pairs={{0,8},{1,24},{2,0},{3,16},{4,40},{5,56},{6,32},{7,48},{8,64},{9,80... | collective-permute-start | bytes 589832 | tf_op jit(solution)/shard_map/ppermute | solution.py:241
  37.9 14.9 %collective-permute-start.5 = (bf16[2,768,128]{2,1,0:T(8,128)(2,1)S(1)}, bf16[2,768,128]{2,1,0:T(8,128)(2,1)S(1)}, u32[]{:S(2)}, u32[]{:S(2)}) collective-permute-start(bf16[2,768,128]{2,1,0:T(8,128)(2,1)S(1)} %get-tuple-element.11.p0), channel_id=1, source_target_pairs={{0,1},{1,2},{2,3},{3,0},{4,5},{5,6},{6,7},{7,4},{8,9},{9,10},{10,1... | collective-permute-start | bytes 1179656 | tf_op jit(solution)/shard_map/ppermute | solution.py:243
  39.3 18.8 %collective-permute-start.4 = (bf16[2,768,128]{2,1,0:T(8,128)(2,1)S(1)}, bf16[2,768,128]{2,1,0:T(8,128)(2,1)S(1)}, u32[]{:S(2)}, u32[]{:S(2)}) collective-permute-start(bf16[2,768,128]{2,1,0:T(8,128)(2,1)S(1)} %get-tuple-element.11.p0), channel_id=1, source_target_pairs={{4,8},{8,4},{12,0},{0,12},{5,9},{9,5},{13,1},{1,13},{6,10},{10,6},... | collective-permute-start | bytes 1179656 | tf_op jit(solution)/shard_map/ppermute | solution.py:244
  40.3 17.8 %collective-permute-start.3 = (bf16[2,768,128]{2,1,0:T(8,128)(2,1)S(1)}, bf16[2,768,128]{2,1,0:T(8,128)(2,1)S(1)}, u32[]{:S(2)}, u32[]{:S(2)}) collective-permute-start(bf16[2,768,128]{2,1,0:T(8,128)(2,1)S(1)} %get-tuple-element.11.p0), channel_id=1, source_target_pairs={{1,0},{2,1},{3,2},{0,3},{5,4},{6,5},{7,6},{4,7},{9,8},{10,9},{11,1... | collective-permute-start | bytes 1179656 | tf_op jit(solution)/shard_map/ppermute | solution.py:242
  46.3 4.5 %collective-permute-start.8 = (bf16[768,128]{1,0:T(8,128)(2,1)S(1)}, bf16[768,128]{1,0:T(8,128)(2,1)S(1)}, u32[]{:S(2)}, u32[]{:S(2)}) collective-permute-start(bf16[768,128]{1,0:T(8,128)(2,1)S(1)} %collective-permute-done.6.g0), channel_id=1, source_target_pairs={{0,16},{16,0},{1,17},{17,1},{2,18},{18,2},{3,19},{19,3},{4,20},{20... | collective-permute-start | bytes 589832 | tf_op jit(solution)/shard_map/ppermute | solution.py:246
  48.5 2.9 %collective-permute-start.9 = (bf16[768,128]{1,0:T(8,128)(2,1)S(1)}, bf16[768,128]{1,0:T(8,128)(2,1)S(1)}, u32[]{:S(2)}, u32[]{:S(2)}) collective-permute-start(bf16[768,128]{1,0:T(8,128)(2,1)S(1)} %collective-permute-done.7.g1), channel_id=1, source_target_pairs={{0,16},{16,0},{1,17},{17,1},{2,18},{18,2},{3,19},{19,3},{4,20},{20... | collective-permute-start | bytes 589832 | tf_op jit(solution)/shard_map/ppermute | solution.py:247

commit v2 on v1

--- a/solution.py
+++ b/solution.py
@@ -55,24 +55,24 @@
     return pairs
 
 
-def pack_kernel(front_ref, out_ref):
+def pack_kernel(panel_ref, out_ref):
     flip = lax.axis_index("z") // 2
     for k in range(2):
         parity = jnp.bitwise_xor(k, flip)
-        left = front_ref[:HALF, parity, :, :].reshape(ROWS, 128)
-        right = front_ref[HALF:, parity, :, :].reshape(ROWS, 128)
+        left = panel_ref[:HALF, parity, :, :].reshape(ROWS, 128)
+        right = panel_ref[HALF:, parity, :, :].reshape(ROWS, 128)
         out_ref[k] = jnp.concatenate([left[:, :B], right[:, :B]], axis=1)
 
 
-def pack(front4):
+def pack(panel4):
+    whole = pl.BlockSpec(memory_space=VMEM)
     return pl.pallas_call(
         pack_kernel,
-        grid=(1,),
         out_shape=jax.ShapeDtypeStruct((2, ROWS, 128), BF16),
-        in_specs=[pl.BlockSpec((PAIRS, 2, B, 128), lambda i: (0, 0, 0, 0))],
-        out_specs=pl.BlockSpec((2, ROWS, 128), lambda i: (0, 0, 0)),
+        in_specs=[whole],
+        out_specs=whole,
         compiler_params=pltpu.CompilerParams(vmem_limit_bytes=16 << 20),
-    )(front4)
+    )(panel4)
 
 
 def choose_kernel(a_ref, b_ref, c_ref, d_ref, own_ref, first_ref, second_ref):
@@ -101,7 +101,20 @@
     )(a, b, c, d)
 
 
-def prepare_kernel(diag_ref, pattern_ref, row_w_ref, col_w_ref, mask_ref):
+STAGES = 4
+
+
+def prepare_kernel(
+    front_ref, diag_ref, pattern_ref, row_w_ref, col_w_ref, mask_ref, stay_ref, sems
+):
+    span = PAIRS // STAGES
+    copies = []
+    for k in range(STAGES):
+        part = pl.ds(k * span, span)
+        copies.append(
+            pltpu.make_async_copy(front_ref.at[part], stay_ref.at[part], sems.at[k])
+        )
+        copies[-1].start()
     x, core = lax.axis_index("x"), lax.axis_index("core")
     y, z = lax.axis_index("y"), lax.axis_index("z")
     own = lax.rem(z + 2 * (y // 2), 4)
@@ -143,9 +156,11 @@
     stored_col = lax.broadcasted_iota(jnp.int32, (BLOCKS, COLS), 1) // B
     inside = (stored_row * 8 + row_id >= Q) & (stored_col * 16 + col_id >= Q)
     mask_ref[...] = jnp.where(inside, keep, 0.0)
-
-
-def prepare(diag_inverse, fill_pattern):
+    for copy in copies:
+        copy.wait()
+
+
+def prepare(front4, diag_inverse, fill_pattern):
     whole = pl.BlockSpec(memory_space=VMEM)
     return pl.pallas_call(
         prepare_kernel,
@@ -153,88 +168,103 @@
             jax.ShapeDtypeStruct((2, Q, 128, WIDTH), BF16),
             jax.ShapeDtypeStruct((2, Q, WIDTH, 128), BF16),
             jax.ShapeDtypeStruct((BLOCKS, COLS), F32),
-        ),
-        in_specs=[whole] * 2,
-        out_specs=(whole,) * 3,
-        compiler_params=pltpu.CompilerParams(vmem_limit_bytes=24 << 20),
-    )(diag_inverse, fill_pattern)
-
-
-TILE = 4
+            jax.ShapeDtypeStruct(front4.shape, BF16),
+        ),
+        in_specs=[pl.BlockSpec(memory_space=pltpu.HBM), whole, whole],
+        out_specs=(whole,) * 4,
+        scratch_shapes=[pltpu.SemaphoreType.DMA((STAGES,))],
+        compiler_params=pltpu.CompilerParams(vmem_limit_bytes=41 << 20),
+        cost_estimate=pl.CostEstimate(
+            flops=0, bytes_accessed=2 * 3072 * 1536 * 2, transcendentals=0
+        ),
+    )(front4, diag_inverse, fill_pattern)
+
+
+def column_kernel(g0, g1, g2, g3, col_w_ref, out_ref):
+    col_id = lax.axis_index("y") * 4 + lax.axis_index("z")
+    for u in range(2):
+        total = jnp.zeros((WIDTH, ROWS), F32)
+        for k, g in enumerate((g0, g1, g2, g3)):
+            total += lax.dot_general(col_w_ref[u, k], g[...], NT, preferred_element_type=F32)
+        out_ref[:, u * ROWS : (u + 1) * ROWS] = total.astype(BF16)
+
+    @pl.when(col_id < Q)
+    def _():
+        lane = lax.broadcasted_iota(jnp.int32, (WIDTH, 128), 1)
+        line = lax.broadcasted_iota(jnp.int32, (WIDTH, 128), 0)
+        pick = (line == lane + col_id * B).astype(F32)
+        old = out_ref[:, :128].astype(F32)
+        out_ref[:, :128] = jnp.where(lane < B, pick, old).astype(BF16)
+
+
+def column_factor(columns, col_w):
+    whole = pl.BlockSpec(memory_space=VMEM)
+    return pl.pallas_call(
+        column_kernel,
+        out_shape=jax.ShapeDtypeStruct((WIDTH, COLS), BF16),
+        in_specs=[whole] * 5,
+        out_specs=whole,
+        compiler_params=pltpu.CompilerParams(vmem_limit_bytes=16 << 20),
+        cost_estimate=pl.CostEstimate(
+            flops=2 * COLS * 256 * 512, bytes_accessed=2 * COLS * 768, transcendentals=0
+        ),
+    )(*columns, col_w)
+
+
 CHUNK = 512
 
 
-def update_kernel(
-    front_ref, p0, p1, p2, p3, g0, g1, g2, g3, row_w_ref, col_w_ref, mask_ref, out_ref, gt_ref
-):
-    parity, i = pl.program_id(0), pl.program_id(1)
+def update_kernel(front_ref, p0, p1, p2, p3, gt_ref, row_w_ref, mask_ref, out_ref):
+    parity, u = pl.program_id(0), pl.program_id(1)
     y, z = lax.axis_index("y"), lax.axis_index("z")
-    col_id = y * 4 + z
-    owner = col_id < Q
+    owner = y * 4 + z < Q
     own = lax.rem(z + 2 * (y // 2), 4)
-
-    @pl.when((parity == 0) & (i == 0))
-    def _():
-        for u in range(2):
-            total = jnp.zeros((WIDTH, ROWS), F32)
-            for k, g in enumerate((g0, g1, g2, g3)):
-                total += lax.dot_general(
-                    col_w_ref[u, k], g[...], NT, preferred_element_type=F32
-                )
-            gt_ref[:, u * ROWS : (u + 1) * ROWS] = total.astype(BF16)
-
-        @pl.when(owner)
-        def _():
-            lane = lax.broadcasted_iota(jnp.int32, (WIDTH, 128), 1)
-            line = lax.broadcasted_iota(jnp.int32, (WIDTH, 128), 0)
-            pick = (line == lane + col_id * B).astype(F32)
-            old = gt_ref[:, :128].astype(F32)
-            gt_ref[:, :128] = jnp.where(lane < B, pick, old).astype(BF16)
-
-    u = i // (HALF // TILE)
-    start = pl.multiple_of(lax.rem(i, HALF // TILE) * (TILE * B), TILE * B)
-    total = jnp.zeros((TILE * B, WIDTH), F32)
+    parts = []
     for k, p in enumerate((p0, p1, p2, p3)):
         q = lax.rem(own + k, 4)
-        slot = jnp.bitwise_xor(parity, q // 2)
-        total += jnp.dot(
-            p[slot, pl.ds(start, TILE * B), :], row_w_ref[u, k], preferred_element_type=F32
+        parts.append(p[jnp.bitwise_xor(parity, q // 2)])
+    factor = jnp.dot(
+        jnp.concatenate(parts, axis=1),
+        row_w_ref[u].reshape(Q * 128, WIDTH),
+        preferred_element_type=F32,
+    ).astype(BF16)
+    lane = lax.broadcasted_iota(jnp.int32, (B, 128), 1)
+    for c in range(COLS // CHUNK):
+        product = jnp.dot(
+            factor, gt_ref[:, c * CHUNK : (c + 1) * CHUNK], preferred_element_type=F32
         )
-    factor = total.astype(BF16)
-    lane = lax.broadcasted_iota(jnp.int32, (B, CHUNK), 1)
-    for c in range(COLS // CHUNK):
-        cols = slice(c * CHUNK, (c + 1) * CHUNK)
-        product = jnp.dot(factor, gt_ref[:, cols], preferred_element_type=F32)
-        for b in range(TILE):
-            part = product[b * B : b * B + B]
-            keep = mask_ref[pl.ds(2 * (TILE * i + b) + parity, 1), cols]
-            new = front_ref[b, 0, :, cols].astype(F32) - part * keep
-            if c == 0:
-                new = jnp.where(owner & (lane < B), part, new)
-            out_ref[b, 0, :, cols] = new.astype(BF16)
-
-
-def update(front4, parts, columns, row_w, col_w, mask):
-    whole = pl.BlockSpec(memory_space=VMEM)
-    tile = pl.BlockSpec((TILE, 1, B, COLS), lambda p, i: (i, p, 0, 0))
+        for b in range(HALF):
+            t = HALF * u + b
+            keeps = mask_ref[pl.ds(2 * t + parity, 1), c * CHUNK : (c + 1) * CHUNK]
+            for first, last in ((0, 128), (128, CHUNK)) if c == 0 else ((0, CHUNK),):
+                cols = slice(c * CHUNK + first, c * CHUNK + last)
+                part = product[b * B : b * B + B, first:last]
+                keep = keeps[:, first:last]
+                new = front_ref[t, parity, :, cols].astype(F32) - part * keep
+                if cols.stop == 128:
+                    new = jnp.where(owner & (lane < B), part, new)
+                out_ref[b, 0, :, cols] = new.astype(BF16)
+
+
+def update(front4, parts, columns, row_w, mask):
+    whole = pl.BlockSpec(memory_space=VMEM)
     return pl.pallas_call(
         update_kernel,
-        grid=(2, PAIRS // TILE),
+        grid=(2, 2),
         out_shape=jax.ShapeDtypeStruct((PAIRS, 2, B, COLS), BF16),
-        in_specs=[tile] + [whole] * 11,
-        out_specs=tile,
-        scratch_shapes=[VMEM((WIDTH, COLS), BF16)],
-        compiler_params=pltpu.CompilerParams(vmem_limit_bytes=32 << 20),
+        in_specs=[whole] * 8,
+        out_specs=pl.BlockSpec((HALF, 1, B, COLS), lambda p, u: (u, p, 0, 0)),
+        compiler_params=pltpu.CompilerParams(vmem_limit_bytes=20 << 20),
         cost_estimate=pl.CostEstimate(
             flops=2 * 3072 * 1536 * 256, bytes_accessed=4 * 3072 * 1536, transcendentals=0
         ),
-    )(front4, *parts, *columns, row_w, col_w, mask)
+    )(front4, *parts, columns, row_w, mask)
 
 
 def body(front, diag_inverse, fill_pattern):
     front4 = front.reshape(PAIRS, 2, B, COLS)
-    packed = pack(front4)
-    row_w, col_w, mask = prepare(diag_inverse, fill_pattern)
+    packed = pack(lax.slice(front, (0, 0), (front.shape[0], 128)).reshape(PAIRS, 2, B, 128))
+    row_w, col_w, mask, stay = prepare(front4, diag_inverse, fill_pattern)
     spread = [lax.ppermute(packed, ALL, spread_perm(k)) for k in range(3)]
     own, first, second = choose(packed, *spread)
     g0 = lax.ppermute(first, ALL, column_perm(0))
@@ -245,9 +275,8 @@
     swap = [(0, 1), (1, 0)]
     g2 = lax.ppermute(g0, "core", swap)
     g3 = lax.ppermute(g1, "core", swap)
-    out = update(
-        front4, (own, z_next, y_pair, z_prev), (g0, g1, g2, g3), row_w, col_w, mask
-    )
+    columns = column_factor((g0, g1, g2, g3), col_w)
+    out = update(stay, (own, z_next, y_pair, z_prev), columns, row_w, mask)
     return out.reshape(front.shape)
 
 

time: 71.3 us -> 62.3 us (0.87)
  waiting for transfers between devices: 25.6 us -> 19.2 us
  Pallas kernels: 13.9 us -> 12 us
    pallas_call x2 -> x3, Pallas kernels: 13.3 us -> 7.9 us  [the longest x1 6.73 us: update(): pl.pallas_call(update_kernel, grid=(2, 2), out_shape=jax.ShapeDtypeStruct...]
    ppermute x1, waiting for transfers between devices: 5.34 us -> 0.85 us  [body(): y_pair = lax.ppermute(own, 'y', [(1, 2), (2, 1), (3, 0), (0, 3)])]
    pallas_call x1, Pallas kernels: 0.53 us -> 3.97 us  [prepare(): pl.pallas_call(prepare_kernel, out_shape=(jax.ShapeDtypeStruct((2, Q, 128...]
    unnamed x8 -> x4, local copies, waits for them, and re-layouts: 3.69 us -> 1.97 us
    ppermute x1, waiting for transfers between devices: 1.42 us -> 0.01 us  [body(): z_prev = lax.ppermute(own, 'z', [(i, (i + 1) % 4) for i in range(4)])]
    slice x0 -> x1, local copies, waits for them, and re-layouts: none -> 1.18 us  [body(): lax.slice(front, (0, 0), (front.shape[0], 128)).reshape(PAIRS, 2, B, 128)]
  transfers between devices with their start and end apart: 10 -> 10, of which waited for: 7 -> 5; matrix products, arithmetic and copies ran while one was open for 0% -> 0% of each run, Pallas kernels for 1% -> 8%
where the time goes in v2:
time: 62.3 us; the launch traced here: 62 us
  starting transfers between devices  27.6 us (44%)
  waiting for transfers between devices  19.2 us (31%)
  Pallas kernels  12 us (19%)
  local copies, waits for them, and re-layouts  3.15 us (5%)
    ppermute x3, waiting for transfers between devices, body(): spread = [lax.ppermute(packed, ALL, spread_perm(k)) for k in range(3)]  14.8 us
    ppermute x3, starting transfers between devices, body(): spread = [lax.ppermute(packed, ALL, spread_perm(k)) for k in range(3)]  10.6 us
    pallas_call x1, Pallas kernels, update(): pl.pallas_call(update_kernel, grid=(2, 2), out_shape=jax.ShapeDtypeStruct...  6.73 us
    ppermute x1, starting transfers between devices, body(): g0 = lax.ppermute(first, ALL, column_perm(0))  5.69 us
    pallas_call x1, Pallas kernels, prepare(): pl.pallas_call(prepare_kernel, out_shape=(jax.ShapeDtypeStruct((2, Q, 128...  3.97 us
    ppermute x1, waiting for transfers between devices, body(): g0 = lax.ppermute(first, ALL, column_perm(0))  3.45 us
    ppermute x1, starting transfers between devices, body(): z_next = lax.ppermute(own, 'z', [((i + 1) % 4, i) for i in range(4)])  2.58 us
    ppermute x1, starting transfers between devices, body(): g1 = lax.ppermute(second, ALL, column_perm(1))  2.35 us
  transfers between devices with their start and end apart: 10, of which 5 were waited for; matrix products, arithmetic and copies ran while one was open for 0% of the time, Pallas kernels for 8%

profile of v2, /device:TPU:7, one launch (start us, length us, event | category | flops | bytes accessed | tf_op | source)
XLA Modules:
  0.0 62.0 jit_solution(11056260106124455975)
XLA Ops:
  0.0 1.2 %slice.3 = bf16[3072,128]{1,0:T(8,128)(2,1)S(1)} slice(bf16[3072,1536]{1,0:T(8,128)(2,1)} %param.3), slice={[0:3072], [0:128]} | slice | bytes 1572864 | tf_op jit(solution)/shard_map/slice | solution.py:266
  1.2 0.2 shard_map.38.a_ref
  1.4 8.0 %collective-permute-start.2 = (bf16[2,768,128]{2,1,0:T(8,128)(2,1)S(1)}, bf16[2,768,128]{2,1,0:T(8,128)(2,1)S(1)}, u32[]{:S(2)}, u32[]{:S(2)}) collective-permute-start(bf16[2,768,128]{2,1,0:T(8,128)(2,1)S(1)} %shard_map.38.a_ref), channel_id=1, source_target_pairs={{0,14},{1,15},{2,12},{3,13},{16,30},{17,31},{18,28},{19,29},{32,46... | collective-permute-start | bytes 1179656 | tf_op jit(solution)/shard_map/ppermute | solution.py:268
  9.4 1.3 %collective-permute-start.1 = (bf16[2,768,128]{2,1,0:T(8,128)(2,1)S(1)}, bf16[2,768,128]{2,1,0:T(8,128)(2,1)S(1)}, u32[]{:S(2)}, u32[]{:S(2)}) collective-permute-start(bf16[2,768,128]{2,1,0:T(8,128)(2,1)S(1)} %shard_map.38.a_ref), channel_id=1, source_target_pairs={{0,10},{1,11},{2,8},{3,9},{16,26},{17,27},{18,24},{19,25},{32,42},... | collective-permute-start | bytes 1179656 | tf_op jit(solution)/shard_map/ppermute | solution.py:268
  10.7 1.3 %collective-permute-start = (bf16[2,768,128]{2,1,0:T(8,128)(2,1)S(1)}, bf16[2,768,128]{2,1,0:T(8,128)(2,1)S(1)}, u32[]{:S(2)}, u32[]{:S(2)}) collective-permute-start(bf16[2,768,128]{2,1,0:T(8,128)(2,1)S(1)} %shard_map.38.a_ref), channel_id=1, source_target_pairs={{0,4},{1,5},{2,6},{3,7},{16,20},{17,21},{18,22},{19,23},{32,36},{3... | collective-permute-start | bytes 1179656 | tf_op jit(solution)/shard_map/ppermute | solution.py:268
  12.0 5.1 %collective-permute-done.2.d_ref = bf16[2,768,128]{2,1,0:T(8,128)(2,1)S(1)} collective-permute-done((bf16[2,768,128]{2,1,0:T(8,128)(2,1)S(1)}, bf16[2,768,128]{2,1,0:T(8,128)(2,1)S(1)}, u32[]{:S(2)}, u32[]{:S(2)}) %collective-permute-start.2) | collective-permute-done | bytes 393248 | tf_op jit(solution)/shard_map/ppermute | solution.py:268
  17.1 1.3 %collective-permute-done.1.c_ref = bf16[2,768,128]{2,1,0:T(8,128)(2,1)S(1)} collective-permute-done((bf16[2,768,128]{2,1,0:T(8,128)(2,1)S(1)}, bf16[2,768,128]{2,1,0:T(8,128)(2,1)S(1)}, u32[]{:S(2)}, u32[]{:S(2)}) %collective-permute-start.1) | collective-permute-done | bytes 393248 | tf_op jit(solution)/shard_map/ppermute | solution.py:268
  18.4 8.4 %collective-permute-done.b_ref = bf16[2,768,128]{2,1,0:T(8,128)(2,1)S(1)} collective-permute-done((bf16[2,768,128]{2,1,0:T(8,128)(2,1)S(1)}, bf16[2,768,128]{2,1,0:T(8,128)(2,1)S(1)}, u32[]{:S(2)}, u32[]{:S(2)}) %collective-permute-start) | collective-permute-done | bytes 393248 | tf_op jit(solution)/shard_map/ppermute | solution.py:268
  26.8 0.1 shard_map.39
  27.0 5.7 %collective-permute-start.6 = (bf16[768,128]{1,0:T(8,128)(2,1)S(1)}, bf16[768,128]{1,0:T(8,128)(2,1)S(1)}, u32[]{:S(2)}, u32[]{:S(2)}) collective-permute-start(bf16[768,128]{1,0:T(8,128)(2,1)S(1)} %get-tuple-element.14), channel_id=1, source_target_pairs={{0,0},{1,16},{2,8},{3,24},{4,32},{5,48},{6,40},{7,56},{8,72},{9,88... | collective-permute-start | bytes 589832 | tf_op jit(solution)/shard_map/ppermute | solution.py:270
  32.7 2.4 %collective-permute-start.7 = (bf16[768,128]{1,0:T(8,128)(2,1)S(1)}, bf16[768,128]{1,0:T(8,128)(2,1)S(1)}, u32[]{:S(2)}, u32[]{:S(2)}) collective-permute-start(bf16[768,128]{1,0:T(8,128)(2,1)S(1)} %get-tuple-element.15), channel_id=1, source_target_pairs={{0,8},{1,24},{2,0},{3,16},{4,40},{5,56},{6,32},{7,48},{8,64},{9,80... | collective-permute-start | bytes 589832 | tf_op jit(solution)/shard_map/ppermute | solution.py:271
  35.0 1.4 %collective-permute-start.5 = (bf16[2,768,128]{2,1,0:T(8,128)(2,1)S(1)}, bf16[2,768,128]{2,1,0:T(8,128)(2,1)S(1)}, u32[]{:S(2)}, u32[]{:S(2)}) collective-permute-start(bf16[2,768,128]{2,1,0:T(8,128)(2,1)S(1)} %get-tuple-element.13.p0), channel_id=1, source_target_pairs={{0,1},{1,2},{2,3},{3,0},{4,5},{5,6},{6,7},{7,4},{8,9},{9,10},{10,1... | collective-permute-start | bytes 1179656 | tf_op jit(solution)/shard_map/ppermute | solution.py:273
  36.4 1.0 %collective-permute-start.4 = (bf16[2,768,128]{2,1,0:T(8,128)(2,1)S(1)}, bf16[2,768,128]{2,1,0:T(8,128)(2,1)S(1)}, u32[]{:S(2)}, u32[]{:S(2)}) collective-permute-start(bf16[2,768,128]{2,1,0:T(8,128)(2,1)S(1)} %get-tuple-element.13.p0), channel_id=1, source_target_pairs={{4,8},{8,4},{12,0},{0,12},{5,9},{9,5},{13,1},{1,13},{6,10},{10,6},... | collective-permute-start | bytes 1179656 | tf_op jit(solution)/shard_map/ppermute | solution.py:274
  37.4 2.6 %collective-permute-start.3 = (bf16[2,768,128]{2,1,0:T(8,128)(2,1)S(1)}, bf16[2,768,128]{2,1,0:T(8,128)(2,1)S(1)}, u32[]{:S(2)}, u32[]{:S(2)}) collective-permute-start(bf16[2,768,128]{2,1,0:T(8,128)(2,1)S(1)} %get-tuple-element.13.p0), channel_id=1, source_target_pairs={{1,0},{2,1},{3,2},{0,3},{5,4},{6,5},{7,6},{4,7},{9,8},{10,9},{11,1... | collective-permute-start | bytes 1179656 | tf_op jit(solution)/shard_map/ppermute | solution.py:272
  40.0 3.5 %collective-permute-done.6.g0 = bf16[768,128]{1,0:T(8,128)(2,1)S(1)} collective-permute-done((bf16[768,128]{1,0:T(8,128)(2,1)S(1)}, bf16[768,128]{1,0:T(8,128)(2,1)S(1)}, u32[]{:S(2)}, u32[]{:S(2)}) %collective-permute-start.6) | collective-permute-done | bytes 196640 | tf_op jit(solution)/shard_map/ppermute | solution.py:270
  43.4 2.2 %collective-permute-start.8 = (bf16[768,128]{1,0:T(8,128)(2,1)S(1)}, bf16[768,128]{1,0:T(8,128)(2,1)S(1)}, u32[]{:S(2)}, u32[]{:S(2)}) collective-permute-start(bf16[768,128]{1,0:T(8,128)(2,1)S(1)} %collective-permute-done.6.g0), channel_id=1, source_target_pairs={{0,16},{16,0},{1,17},{17,1},{2,18},{18,2},{3,19},{19,3},{4,20},{20... | collective-permute-start | bytes 589832 | tf_op jit(solution)/shard_map/ppermute | solution.py:276
  45.6 0.0 collective-permute-done.7.g1
  45.6 1.8 %collective-permute-start.9 = (bf16[768,128]{1,0:T(8,128)(2,1)S(1)}, bf16[768,128]{1,0:T(8,128)(2,1)S(1)}, u32[]{:S(2)}, u32[]{:S(2)}) collective-permute-start(bf16[768,128]{1,0:T(8,128)(2,1)S(1)} %collective-permute-done.7.g1), channel_id=1, source_target_pairs={{0,16},{16,0},{1,17},{17,1},{2,18},{18,2},{3,19},{19,3},{4,20},{20... | collective-permute-start | bytes 589832 | tf_op jit(solution)/shard_map/ppermute | solution.py:277
  47.4 0.0 copy-start
  47.4 1.1 %copy-done = s32[384,384]{1,0:T(8,128)S(1)} copy-done((s32[384,384]{1,0:T(8,128)S(1)}, s32[384,384]{1,0:T(8,128)}, u32[]{:S(2)}) %copy-start) | copy-done | bytes 589848
  48.5 0.0 copy-start.1
  48.5 0.9 %copy-done.1 = bf16[256,256]{1,0:T(8,128)(2,1)S(1)} copy-done((bf16[256,256]{1,0:T(8,128)(2,1)S(1)}, bf16[256,256]{1,0:T(8,128)(2,1)}, u32[]{:S(2)}) %copy-start.1) | copy-done | bytes 131096
  49.4 4.0 %shard_map.37 = (bf16[2,4,128,256]{3,2,1,0:T(8,128)(2,1)S(1)}, bf16[2,4,256,128]{3,2,1,0:T(8,128)(2,1)S(1)}, f32[48,1536]{1,0:T(8,128)S(1)}, bf16[24,2,64,1536]{3,2,1,0:T(8,128)(2,1)S(1)}) custom-call(bf16[24,2,64,1536]{3,2,1,0:T(8,128)(2,1)} %bitcast.4, bf16[256,256]{1,0:T(8,128)(2,1)S(1)} %copy-done.1, s32[384,384]{1,0:T(8,128)S(1)} %copy-done), custom_call_target="tpu_custom_call" | custom-call | bytes 18874368 | tf_op jit(solution)/shard_map/pallas_call | solution.py:165
  53.4 0.0 collective-permute-done.8.g2
  53.4 0.0 collective-permute-done.9.g3
  53.4 1.0 %shard_map.40.gt_ref = bf16[256,1536]{1,0:T(8,128)(2,1)S(1)} custom-call(bf16[768,128]{1,0:T(8,128)(2,1)S(1)} %collective-permute-done.6.g0, bf16[768,128]{1,0:T(8,128)(2,1)S(1)} %collective-permute-done.7.g1, bf16[768,128]{1,0:T(8,128)(2,1)S(1)} %collective-permute-done.8.g2, bf16[768,128]{1,0:T(8,128)(2,1)S(1)} %collective-permute-done.9.g3, ...), custom_call_target="tpu_custom_call" | custom-call | flops 402653184 | bytes 2359296 | tf_op jit(solution)/shard_map/pallas_call | solution.py:202
  54.4 0.0 collective-permute-done.5.p3
  54.4 0.9 %collective-permute-done.4.p2 = bf16[2,768,128]{2,1,0:T(8,128)(2,1)S(1)} collective-permute-done((bf16[2,768,128]{2,1,0:T(8,128)(2,1)S(1)}, bf16[2,768,128]{2,1,0:T(8,128)(2,1)S(1)}, u32[]{:S(2)}, u32[]{:S(2)}) %collective-permute-start.4) | collective-permute-done | bytes 393248 | tf_op jit(solution)/shard_map/ppermute | solution.py:274
  55.3 0.0 collective-permute-done.3.p1
  55.3 6.7 %shard_map.41 = bf16[24,2,64,1536]{3,2,1,0:T(8,128)(2,1)} custom-call(bf16[24,2,64,1536]{3,2,1,0:T(8,128)(2,1)S(1)} %get-tuple-element.12.front_ref, bf16[2,768,128]{2,1,0:T(8,128)(2,1)S(1)} %get-tuple-element.13.p0, bf16[2,768,128]{2,1,0:T(8,128)(2,1)S(1)} %collective-permute-done.3.p1, bf16[2,768,128]{2,1,0:T(8,128)(2,1)S(1)} %collective-permute-done.4.p2, ...), custom_call_target="tpu_custom_call" | custom-call | flops 2415919104 | bytes 18874368 | tf_op jit(solution)/shard_map/pallas_call | solution.py:251
Async XLA Ops:
  1.4 15.7 %collective-permute-start.2 = (bf16[2,768,128]{2,1,0:T(8,128)(2,1)S(1)}, bf16[2,768,128]{2,1,0:T(8,128)(2,1)S(1)}, u32[]{:S(2)}, u32[]{:S(2)}) collective-permute-start(bf16[2,768,128]{2,1,0:T(8,128)(2,1)S(1)} %shard_map.38.a_ref), channel_id=1, source_target_pairs={{0,14},{1,15},{2,12},{3,13},{16,30},{17,31},{18,28},{19,29},{32,46... | collective-permute-start | bytes 1179656 | tf_op jit(solution)/shard_map/ppermute | solution.py:268
  9.4 9.1 %collective-permute-start.1 = (bf16[2,768,128]{2,1,0:T(8,128)(2,1)S(1)}, bf16[2,768,128]{2,1,0:T(8,128)(2,1)S(1)}, u32[]{:S(2)}, u32[]{:S(2)}) collective-permute-start(bf16[2,768,128]{2,1,0:T(8,128)(2,1)S(1)} %shard_map.38.a_ref), channel_id=1, source_target_pairs={{0,10},{1,11},{2,8},{3,9},{16,26},{17,27},{18,24},{19,25},{32,42},... | collective-permute-start | bytes 1179656 | tf_op jit(solution)/shard_map/ppermute | solution.py:268
  10.7 16.2 %collective-permute-start = (bf16[2,768,128]{2,1,0:T(8,128)(2,1)S(1)}, bf16[2,768,128]{2,1,0:T(8,128)(2,1)S(1)}, u32[]{:S(2)}, u32[]{:S(2)}) collective-permute-start(bf16[2,768,128]{2,1,0:T(8,128)(2,1)S(1)} %shard_map.38.a_ref), channel_id=1, source_target_pairs={{0,4},{1,5},{2,6},{3,7},{16,20},{17,21},{18,22},{19,23},{32,36},{3... | collective-permute-start | bytes 1179656 | tf_op jit(solution)/shard_map/ppermute | solution.py:268
  27.0 16.5 %collective-permute-start.6 = (bf16[768,128]{1,0:T(8,128)(2,1)S(1)}, bf16[768,128]{1,0:T(8,128)(2,1)S(1)}, u32[]{:S(2)}, u32[]{:S(2)}) collective-permute-start(bf16[768,128]{1,0:T(8,128)(2,1)S(1)} %get-tuple-element.14), channel_id=1, source_target_pairs={{0,0},{1,16},{2,8},{3,24},{4,32},{5,48},{6,40},{7,56},{8,72},{9,88... | collective-permute-start | bytes 589832 | tf_op jit(solution)/shard_map/ppermute | solution.py:270
  32.7 12.9 %collective-permute-start.7 = (bf16[768,128]{1,0:T(8,128)(2,1)S(1)}, bf16[768,128]{1,0:T(8,128)(2,1)S(1)}, u32[]{:S(2)}, u32[]{:S(2)}) collective-permute-start(bf16[768,128]{1,0:T(8,128)(2,1)S(1)} %get-tuple-element.15), channel_id=1, source_target_pairs={{0,8},{1,24},{2,0},{3,16},{4,40},{5,56},{6,32},{7,48},{8,64},{9,80... | collective-permute-start | bytes 589832 | tf_op jit(solution)/shard_map/ppermute | solution.py:271
  35.0 19.4 %collective-permute-start.5 = (bf16[2,768,128]{2,1,0:T(8,128)(2,1)S(1)}, bf16[2,768,128]{2,1,0:T(8,128)(2,1)S(1)}, u32[]{:S(2)}, u32[]{:S(2)}) collective-permute-start(bf16[2,768,128]{2,1,0:T(8,128)(2,1)S(1)} %get-tuple-element.13.p0), channel_id=1, source_target_pairs={{0,1},{1,2},{2,3},{3,0},{4,5},{5,6},{6,7},{7,4},{8,9},{9,10},{10,1... | collective-permute-start | bytes 1179656 | tf_op jit(solution)/shard_map/ppermute | solution.py:273
  36.4 18.8 %collective-permute-start.4 = (bf16[2,768,128]{2,1,0:T(8,128)(2,1)S(1)}, bf16[2,768,128]{2,1,0:T(8,128)(2,1)S(1)}, u32[]{:S(2)}, u32[]{:S(2)}) collective-permute-start(bf16[2,768,128]{2,1,0:T(8,128)(2,1)S(1)} %get-tuple-element.13.p0), channel_id=1, source_target_pairs={{4,8},{8,4},{12,0},{0,12},{5,9},{9,5},{13,1},{1,13},{6,10},{10,6},... | collective-permute-start | bytes 1179656 | tf_op jit(solution)/shard_map/ppermute | solution.py:274
  37.4 17.8 %collective-permute-start.3 = (bf16[2,768,128]{2,1,0:T(8,128)(2,1)S(1)}, bf16[2,768,128]{2,1,0:T(8,128)(2,1)S(1)}, u32[]{:S(2)}, u32[]{:S(2)}) collective-permute-start(bf16[2,768,128]{2,1,0:T(8,128)(2,1)S(1)} %get-tuple-element.13.p0), channel_id=1, source_target_pairs={{1,0},{2,1},{3,2},{0,3},{5,4},{6,5},{7,6},{4,7},{9,8},{10,9},{11,1... | collective-permute-start | bytes 1179656 | tf_op jit(solution)/shard_map/ppermute | solution.py:272
  43.4 9.9 %collective-permute-start.8 = (bf16[768,128]{1,0:T(8,128)(2,1)S(1)}, bf16[768,128]{1,0:T(8,128)(2,1)S(1)}, u32[]{:S(2)}, u32[]{:S(2)}) collective-permute-start(bf16[768,128]{1,0:T(8,128)(2,1)S(1)} %collective-permute-done.6.g0), channel_id=1, source_target_pairs={{0,16},{16,0},{1,17},{17,1},{2,18},{18,2},{3,19},{19,3},{4,20},{20... | collective-permute-start | bytes 589832 | tf_op jit(solution)/shard_map/ppermute | solution.py:276
  45.6 7.8 %collective-permute-start.9 = (bf16[768,128]{1,0:T(8,128)(2,1)S(1)}, bf16[768,128]{1,0:T(8,128)(2,1)S(1)}, u32[]{:S(2)}, u32[]{:S(2)}) collective-permute-start(bf16[768,128]{1,0:T(8,128)(2,1)S(1)} %collective-permute-done.7.g1), channel_id=1, source_target_pairs={{0,16},{16,0},{1,17},{17,1},{2,18},{18,2},{3,19},{19,3},{4,20},{20... | collective-permute-start | bytes 589832 | tf_op jit(solution)/shard_map/ppermute | solution.py:277
  47.4 1.1 %copy-start = (s32[384,384]{1,0:T(8,128)S(1)}, s32[384,384]{1,0:T(8,128)}, u32[]{:S(2)}) copy-start(s32[384,384]{1,0:T(8,128)} %pattern_ref.1) | copy-start | bytes 1769476
  48.5 0.9 %copy-start.1 = (bf16[256,256]{1,0:T(8,128)(2,1)S(1)}, bf16[256,256]{1,0:T(8,128)(2,1)}, u32[]{:S(2)}) copy-start(bf16[256,256]{1,0:T(8,128)(2,1)} %diag_ref.1) | copy-start | bytes 393220

commit v3 on v2

--- a/solution.py
+++ b/solution.py
@@ -1,8 +1,5 @@
-import functools
-
 import jax
 import jax.numpy as jnp
-import numpy as np
 from jax import lax
 from jax.experimental import pallas as pl
 from jax.experimental.pallas import tpu as pltpu
@@ -48,55 +45,71 @@
             r = 2 * x + core
             for y in range(4):
                 for z in range(4):
-                    q = quarter_of(y, z)
-                    half = step if q < 2 else 1 - step
-                    target = linear((y + x) % 4, q % 2, 2 * half + r // 4, r % 4)
+                    q, half, far = quarter_of(y, z), y % 2, y // 2
+                    near = (step == 0) == (q < 2)
+                    to_x = (x + far + (0 if near else 2)) % 4
+                    target = linear(to_x, q % 2, 2 * half + r // 4, r % 4)
                     pairs.append((linear(x, core, y, z), target))
     return pairs
 
 
-def pack_kernel(panel_ref, out_ref):
-    flip = lax.axis_index("z") // 2
-    for k in range(2):
-        parity = jnp.bitwise_xor(k, flip)
+def shift_perm(first, second):
+    pairs = []
+    for x in range(4):
+        for core in range(2):
+            dy, dz = (first, second)[core]
+            for y in range(4):
+                for z in range(4):
+                    source = linear(x, core, (y + dy) % 4, (z + dz) % 4)
+                    pairs.append((source, linear(x, core, y, z)))
+    return pairs
+
+
+OFFSETS = (
+    ((0, 1), (0, 1)),
+    ((2, 0), (0, 2)),
+    ((0, -1), (0, -1)),
+    ((1, 0), (1, 0)),
+    ((-1, -1), (-1, -1)),
+    ((-1, 0), (-1, 0)),
+    ((-1, 1), (1, -1)),
+)
+
+
+def pack_kernel(panel_ref, even_ref, odd_ref):
+    for parity, ref in enumerate((even_ref, odd_ref)):
         left = panel_ref[:HALF, parity, :, :].reshape(ROWS, 128)
         right = panel_ref[HALF:, parity, :, :].reshape(ROWS, 128)
-        out_ref[k] = jnp.concatenate([left[:, :B], right[:, :B]], axis=1)
+        ref[...] = jnp.concatenate([left[:, :B], right[:, :B]], axis=1)
 
 
 def pack(panel4):
     whole = pl.BlockSpec(memory_space=VMEM)
     return pl.pallas_call(
         pack_kernel,
-        out_shape=jax.ShapeDtypeStruct((2, ROWS, 128), BF16),
+        out_shape=(jax.ShapeDtypeStruct((ROWS, 128), BF16),) * 2,
         in_specs=[whole],
-        out_specs=whole,
+        out_specs=(whole,) * 2,
         compiler_params=pltpu.CompilerParams(vmem_limit_bytes=16 << 20),
     )(panel4)
 
 
-def choose_kernel(a_ref, b_ref, c_ref, d_ref, own_ref, first_ref, second_ref):
+def choose_kernel(a_ref, b_ref, c_ref, d_ref, own_ref):
     y = lax.axis_index("y")
     for k, ref in enumerate((a_ref, b_ref, c_ref, d_ref)):
 
         @pl.when(y == k)
         def _():
             own_ref[...] = ref[...]
-            first_ref[...] = ref[0]
-            second_ref[...] = ref[1]
 
 
 def choose(a, b, c, d):
     whole = pl.BlockSpec(memory_space=VMEM)
     return pl.pallas_call(
         choose_kernel,
-        out_shape=(
-            jax.ShapeDtypeStruct((2, ROWS, 128), BF16),
-            jax.ShapeDtypeStruct((ROWS, 128), BF16),
-            jax.ShapeDtypeStruct((ROWS, 128), BF16),
-        ),
+        out_shape=jax.ShapeDtypeStruct((ROWS, 128), BF16),
         in_specs=[whole] * 4,
-        out_specs=(whole,) * 3,
+        out_specs=whole,
         compiler_params=pltpu.CompilerParams(vmem_limit_bytes=16 << 20),
     )(a, b, c, d)
 
@@ -124,13 +137,16 @@
         == lax.broadcasted_iota(jnp.int32, (WIDTH, WIDTH), 1)
     ).astype(BF16)
     turned = lax.dot_general(eye, diag, NT, preferred_element_type=F32).astype(BF16)
+    bases = (own, lax.rem(own + 2 * lax.rem(y, 2), 4))
+    source_x = 2 * lax.rem(y, 2) + z // 2
+    half = lax.rem(x - source_x + 4, 4) // 2
     for q in range(Q):
-        slot = lax.rem(q - own + 4, 4)
         part = turned[q * B : q * B + B, :]
         zero = jnp.zeros_like(part)
-        row_w_ref[0, slot] = jnp.concatenate([part, zero], axis=0)
-        row_w_ref[1, slot] = jnp.concatenate([zero, part], axis=0)
-        half = y // 2
+        for kind, base in enumerate(bases):
+            slot = lax.rem(q - base + 4, 4)
+            row_w_ref[kind, 0, slot] = jnp.concatenate([part, zero], axis=0)
+            row_w_ref[kind, 1, slot] = jnp.concatenate([zero, part], axis=0)
         other = jnp.where(q % 2 == core, 0, 2)
         late = jnp.where(q // 2 == half, 0, 1)
         part = diag[:, q * B : q * B + B]
@@ -165,7 +181,7 @@
     return pl.pallas_call(
         prepare_kernel,
         out_shape=(
-            jax.ShapeDtypeStruct((2, Q, 128, WIDTH), BF16),
+            jax.ShapeDtypeStruct((2, 2, Q, 128, WIDTH), BF16),
             jax.ShapeDtypeStruct((2, Q, WIDTH, 128), BF16),
             jax.ShapeDtypeStruct((BLOCKS, COLS), F32),
             jax.ShapeDtypeStruct(front4.shape, BF16),
@@ -214,20 +230,23 @@
 CHUNK = 512
 
 
-def update_kernel(front_ref, p0, p1, p2, p3, gt_ref, row_w_ref, mask_ref, out_ref):
+def update_kernel(front_ref, *refs):
+    parts, (gt_ref, row_w_ref, mask_ref, out_ref, factor_ref) = refs[:8], refs[8:]
     parity, u = pl.program_id(0), pl.program_id(1)
     y, z = lax.axis_index("y"), lax.axis_index("z")
     owner = y * 4 + z < Q
-    own = lax.rem(z + 2 * (y // 2), 4)
-    parts = []
-    for k, p in enumerate((p0, p1, p2, p3)):
-        q = lax.rem(own + k, 4)
-        parts.append(p[jnp.bitwise_xor(parity, q // 2)])
-    factor = jnp.dot(
-        jnp.concatenate(parts, axis=1),
-        row_w_ref[u].reshape(Q * 128, WIDTH),
-        preferred_element_type=F32,
-    ).astype(BF16)
+    for kind in range(2):
+
+        @pl.when(lax.rem(y + kind, 2) == parity)
+        def _():
+            four = [p[...] for p in parts[4 * kind : 4 * kind + 4]]
+            factor_ref[...] = jnp.dot(
+                jnp.concatenate(four, axis=1),
+                row_w_ref[kind, u].reshape(Q * 128, WIDTH),
+                preferred_element_type=F32,
+            ).astype(BF16)
+
+    factor = factor_ref[...]
     lane = lax.broadcasted_iota(jnp.int32, (B, 128), 1)
     for c in range(COLS // CHUNK):
         product = jnp.dot(
@@ -252,7 +271,8 @@
         update_kernel,
         grid=(2, 2),
         out_shape=jax.ShapeDtypeStruct((PAIRS, 2, B, COLS), BF16),
-        in_specs=[whole] * 8,
+        in_specs=[whole] * 12,
+        scratch_shapes=[VMEM((ROWS, WIDTH), BF16)],
         out_specs=pl.BlockSpec((HALF, 1, B, COLS), lambda p, u: (u, p, 0, 0)),
         compiler_params=pltpu.CompilerParams(vmem_limit_bytes=20 << 20),
         cost_estimate=pl.CostEstimate(
@@ -263,20 +283,20 @@
 
 def body(front, diag_inverse, fill_pattern):
     front4 = front.reshape(PAIRS, 2, B, COLS)
-    packed = pack(lax.slice(front, (0, 0), (front.shape[0], 128)).reshape(PAIRS, 2, B, 128))
+    even, odd = pack(lax.slice(front, (0, 0), (front.shape[0], 128)).reshape(PAIRS, 2, B, 128))
     row_w, col_w, mask, stay = prepare(front4, diag_inverse, fill_pattern)
-    spread = [lax.ppermute(packed, ALL, spread_perm(k)) for k in range(3)]
-    own, first, second = choose(packed, *spread)
-    g0 = lax.ppermute(first, ALL, column_perm(0))
-    g1 = lax.ppermute(second, ALL, column_perm(1))
-    z_next = lax.ppermute(own, "z", [((i + 1) % 4, i) for i in range(4)])
-    z_prev = lax.ppermute(own, "z", [(i, (i + 1) % 4) for i in range(4)])
-    y_pair = lax.ppermute(own, "y", [(1, 2), (2, 1), (3, 0), (0, 3)])
+    spread = [
+        lax.ppermute(part, ALL, spread_perm(k)) for k, part in enumerate((odd, even, odd))
+    ]
+    own = choose(even, *spread)
+    g0 = lax.ppermute(own, ALL, column_perm(0))
+    g1 = lax.ppermute(own, ALL, column_perm(1))
+    parts = [own] + [lax.ppermute(own, ALL, shift_perm(*offsets)) for offsets in OFFSETS]
     swap = [(0, 1), (1, 0)]
     g2 = lax.ppermute(g0, "core", swap)
     g3 = lax.ppermute(g1, "core", swap)
     columns = column_factor((g0, g1, g2, g3), col_w)
-    out = update(stay, (own, z_next, y_pair, z_prev), columns, row_w, mask)
+    out = update(stay, parts, columns, row_w, mask)
     return out.reshape(front.shape)
 
 

time: 62.3 us -> 60.9 us (0.978)
  the two profiles are of different devices: /device:TPU:7 before, /device:TPU:21 now
where the time goes in v3:
time: 60.9 us; the launch traced here: 60.6 us
  waiting for transfers between devices  23.1 us (38%)
  starting transfers between devices  22.8 us (37%)
  Pallas kernels  11.5 us (19%)
  local copies, waits for them, and re-layouts  3.15 us (5%)
    ppermute x1, starting transfers between devices, body(): g1 = lax.ppermute(own, ALL, column_perm(1))  9.83 us
    ppermute x3, waiting for transfers between devices, body(): lax.ppermute(part, ALL, spread_perm(k))  8.91 us
    ppermute x1, waiting for transfers between devices, body(): g0 = lax.ppermute(own, ALL, column_perm(0))  8.56 us
    pallas_call x1, Pallas kernels, update(): pl.pallas_call(update_kernel, grid=(2, 2), out_shape=jax.ShapeDtypeStruct...  6.36 us
    ppermute x7, starting transfers between devices, body(): lax.ppermute(own, ALL, shift_perm(*offsets))  5.38 us
    pallas_call x1, Pallas kernels, prepare(): pl.pallas_call(prepare_kernel, out_shape=(jax.ShapeDtypeStruct((2, 2, Q,...  3.98 us
    ppermute x7, waiting for transfers between devices, body(): lax.ppermute(own, ALL, shift_perm(*offsets))  3.27 us
    ppermute x3, starting transfers between devices, body(): lax.ppermute(part, ALL, spread_perm(k))  2.64 us
  transfers between devices with their start and end apart: 14, of which 4 were waited for; matrix products, arithmetic and copies ran while one was open for 0% of the time, Pallas kernels for 8%

profile of v3, /device:TPU:21, one launch (start us, length us, event | category | flops | bytes accessed | tf_op | source)
XLA Modules:
  0.0 60.6 jit_solution(14700651628019958245)
XLA Ops:
  0.0 1.2 %slice.3 = bf16[3072,128]{1,0:T(8,128)(2,1)S(1)} slice(bf16[3072,1536]{1,0:T(8,128)(2,1)} %param.3), slice={[0:3072], [0:128]} | slice | bytes 1572864 | tf_op jit(solution)/shard_map/slice | solution.py:286
  1.2 0.2 shard_map.38
  1.4 1.3 %collective-permute-start.1 = (bf16[768,128]{1,0:T(8,128)(2,1)S(1)}, bf16[768,128]{1,0:T(8,128)(2,1)S(1)}, u32[]{:S(2)}, u32[]{:S(2)}) collective-permute-start(bf16[768,128]{1,0:T(8,128)(2,1)S(1)} %get-tuple-element.12.a_ref), channel_id=1, source_target_pairs={{0,10},{1,11},{2,8},{3,9},{16,26},{17,27},{18,24},{19,25},{32,42},... | collective-permute-start | bytes 589832 | tf_op jit(solution)/shard_map/ppermute | solution.py:289
  2.7 0.7 %collective-permute-start.2 = (bf16[768,128]{1,0:T(8,128)(2,1)S(1)}, bf16[768,128]{1,0:T(8,128)(2,1)S(1)}, u32[]{:S(2)}, u32[]{:S(2)}) collective-permute-start(bf16[768,128]{1,0:T(8,128)(2,1)S(1)} %get-tuple-element.13), channel_id=1, source_target_pairs={{0,14},{1,15},{2,12},{3,13},{16,30},{17,31},{18,28},{19,29},{32,46... | collective-permute-start | bytes 589832 | tf_op jit(solution)/shard_map/ppermute | solution.py:289
  3.3 0.7 %collective-permute-start = (bf16[768,128]{1,0:T(8,128)(2,1)S(1)}, bf16[768,128]{1,0:T(8,128)(2,1)S(1)}, u32[]{:S(2)}, u32[]{:S(2)}) collective-permute-start(bf16[768,128]{1,0:T(8,128)(2,1)S(1)} %get-tuple-element.13), channel_id=1, source_target_pairs={{0,4},{1,5},{2,6},{3,7},{16,20},{17,21},{18,22},{19,23},{32,36},{3... | collective-permute-start | bytes 589832 | tf_op jit(solution)/shard_map/ppermute | solution.py:289
  4.0 8.9 %collective-permute-done.1.c_ref = bf16[768,128]{1,0:T(8,128)(2,1)S(1)} collective-permute-done((bf16[768,128]{1,0:T(8,128)(2,1)S(1)}, bf16[768,128]{1,0:T(8,128)(2,1)S(1)}, u32[]{:S(2)}, u32[]{:S(2)}) %collective-permute-start.1) | collective-permute-done | bytes 196640 | tf_op jit(solution)/shard_map/ppermute | solution.py:289
  12.9 0.0 collective-permute-done.2.d_ref
  12.9 0.0 collective-permute-done.b_ref
  13.0 9.8 %collective-permute-start.11 = (bf16[768,128]{1,0:T(8,128)(2,1)S(1)}, bf16[768,128]{1,0:T(8,128)(2,1)S(1)}, u32[]{:S(2)}, u32[]{:S(2)}) collective-permute-start(bf16[768,128]{1,0:T(8,128)(2,1)S(1)} %shard_map.39.refs_0_), channel_id=1, source_target_pairs={{0,64},{1,80},{2,0},{3,16},{4,72},{5,88},{6,8},{7,24},{8,32},{9,48... | collective-permute-start | bytes 589832 | tf_op jit(solution)/shard_map/ppermute | solution.py:293
  22.8 1.9 %collective-permute-start.10 = (bf16[768,128]{1,0:T(8,128)(2,1)S(1)}, bf16[768,128]{1,0:T(8,128)(2,1)S(1)}, u32[]{:S(2)}, u32[]{:S(2)}) collective-permute-start(bf16[768,128]{1,0:T(8,128)(2,1)S(1)} %shard_map.39.refs_0_), channel_id=1, source_target_pairs={{0,0},{1,16},{2,64},{3,80},{4,8},{5,24},{6,72},{7,88},{8,96},{9,11... | collective-permute-start | bytes 589832 | tf_op jit(solution)/shard_map/ppermute | solution.py:292
  24.7 0.1 collective-permute-start.9
  24.8 0.3 collective-permute-start.8
  25.1 2.3 %collective-permute-done.11.g1 = bf16[768,128]{1,0:T(8,128)(2,1)S(1)} collective-permute-done((bf16[768,128]{1,0:T(8,128)(2,1)S(1)}, bf16[768,128]{1,0:T(8,128)(2,1)S(1)}, u32[]{:S(2)}, u32[]{:S(2)}) %collective-permute-start.11) | collective-permute-done | bytes 196640 | tf_op jit(solution)/shard_map/ppermute | solution.py:293
  27.4 2.4 %collective-permute-start.13 = (bf16[768,128]{1,0:T(8,128)(2,1)S(1)}, bf16[768,128]{1,0:T(8,128)(2,1)S(1)}, u32[]{:S(2)}, u32[]{:S(2)}) collective-permute-start(bf16[768,128]{1,0:T(8,128)(2,1)S(1)} %collective-permute-done.11.g1), channel_id=1, source_target_pairs={{0,16},{16,0},{1,17},{17,1},{2,18},{18,2},{3,19},{19,3},{4,20},{20... | collective-permute-start | bytes 589832 | tf_op jit(solution)/shard_map/ppermute | solution.py:297
  29.8 8.6 %collective-permute-done.10.g0 = bf16[768,128]{1,0:T(8,128)(2,1)S(1)} collective-permute-done((bf16[768,128]{1,0:T(8,128)(2,1)S(1)}, bf16[768,128]{1,0:T(8,128)(2,1)S(1)}, u32[]{:S(2)}, u32[]{:S(2)}) %collective-permute-start.10) | collective-permute-done | bytes 196640 | tf_op jit(solution)/shard_map/ppermute | solution.py:292
  38.4 0.6 %collective-permute-start.12 = (bf16[768,128]{1,0:T(8,128)(2,1)S(1)}, bf16[768,128]{1,0:T(8,128)(2,1)S(1)}, u32[]{:S(2)}, u32[]{:S(2)}) collective-permute-start(bf16[768,128]{1,0:T(8,128)(2,1)S(1)} %collective-permute-done.10.g0), channel_id=1, source_target_pairs={{0,16},{16,0},{1,17},{17,1},{2,18},{18,2},{3,19},{19,3},{4,20},{20... | collective-permute-start | bytes 589832 | tf_op jit(solution)/shard_map/ppermute | solution.py:296
  39.0 0.0 collective-permute-start.7
  39.0 0.0 collective-permute-done.9.refs_7_
  39.0 0.0 collective-permute-start.6
  39.0 0.0 collective-permute-done.8.refs_6_
  39.0 0.1 collective-permute-start.5
  39.1 0.0 collective-permute-done.13.g3
  39.1 4.9 %collective-permute-start.4 = (bf16[768,128]{1,0:T(8,128)(2,1)S(1)}, bf16[768,128]{1,0:T(8,128)(2,1)S(1)}, u32[]{:S(2)}, u32[]{:S(2)}) collective-permute-start(bf16[768,128]{1,0:T(8,128)(2,1)S(1)} %shard_map.39.refs_0_), channel_id=1, source_target_pairs={{8,0},{9,1},{10,2},{11,3},{12,4},{13,5},{14,6},{15,7},{0,8},{1,9},... | collective-permute-start | bytes 589832 | tf_op jit(solution)/shard_map/ppermute | solution.py:294
  44.0 0.0 collective-permute-done.12.g2
  44.1 1.1 %copy-done = s32[384,384]{1,0:T(8,128)S(1)} copy-done((s32[384,384]{1,0:T(8,128)S(1)}, s32[384,384]{1,0:T(8,128)}, u32[]{:S(2)}) %copy-start) | copy-done | bytes 589848
  45.1 0.9 %copy-done.1 = bf16[256,256]{1,0:T(8,128)(2,1)S(1)} copy-done((bf16[256,256]{1,0:T(8,128)(2,1)S(1)}, bf16[256,256]{1,0:T(8,128)(2,1)}, u32[]{:S(2)}) %copy-start.1) | copy-done | bytes 131096
  46.0 4.0 %shard_map.37 = (bf16[2,2,4,128,256]{4,3,2,1,0:T(8,128)(2,1)S(1)}, bf16[2,4,256,128]{3,2,1,0:T(8,128)(2,1)S(1)}, f32[48,1536]{1,0:T(8,128)S(1)}, bf16[24,2,64,1536]{3,2,1,0:T(8,128)(2,1)S(1)}) custom-call(bf16[24,2,64,1536]{3,2,1,0:T(8,128)(2,1)} %bitcast.4, bf16[256,256]{1,0:T(8,128)(2,1)S(1)} %copy-done.1, s32[384,384]{1,0:T(8,128)S(1)} %copy-done), custom_call_target="tpu_custom_call" | custom-call | bytes 18874368 | tf_op jit(solution)/shard_map/pallas_call | solution.py:181
  50.0 1.0 %shard_map.40.refs_8_ = bf16[256,1536]{1,0:T(8,128)(2,1)S(1)} custom-call(bf16[768,128]{1,0:T(8,128)(2,1)S(1)} %collective-permute-done.10.g0, bf16[768,128]{1,0:T(8,128)(2,1)S(1)} %collective-permute-done.11.g1, bf16[768,128]{1,0:T(8,128)(2,1)S(1)} %collective-permute-done.12.g2, bf16[768,128]{1,0:T(8,128)(2,1)S(1)} %collective-permute-done.13.g3, ...), custom_call_target="tpu_custom_call" | custom-call | flops 402653184 | bytes 2359296 | tf_op jit(solution)/shard_map/pallas_call | solution.py:218
  51.0 0.0 collective-permute-done.7.refs_5_
  51.0 3.3 %collective-permute-done.5.refs_3_ = bf16[768,128]{1,0:T(8,128)(2,1)S(1)} collective-permute-done((bf16[768,128]{1,0:T(8,128)(2,1)S(1)}, bf16[768,128]{1,0:T(8,128)(2,1)S(1)}, u32[]{:S(2)}, u32[]{:S(2)}) %collective-permute-start.5) | collective-permute-done | bytes 196640 | tf_op jit(solution)/shard_map/ppermute | solution.py:294
  54.3 0.0 collective-permute-done.3.refs_1_
  54.3 6.4 %shard_map.41 = bf16[24,2,64,1536]{3,2,1,0:T(8,128)(2,1)} custom-call(bf16[24,2,64,1536]{3,2,1,0:T(8,128)(2,1)S(1)} %get-tuple-element.11.front_ref, bf16[768,128]{1,0:T(8,128)(2,1)S(1)} %shard_map.39.refs_0_, bf16[768,128]{1,0:T(8,128)(2,1)S(1)} %collective-permute-done.3.refs_1_, bf16[768,128]{1,0:T(8,128)(2,1)S(1)} %collective-permute-done.4.refs_2_, ...), custom_call_target="tpu_custom_call" | custom-call | flops 2415919104 | bytes 18874368 | tf_op jit(solution)/shard_map/pallas_call | solution.py:270
  (6 shorter events, 0.0 us)
Async XLA Ops:
  1.4 11.6 %collective-permute-start.1 = (bf16[768,128]{1,0:T(8,128)(2,1)S(1)}, bf16[768,128]{1,0:T(8,128)(2,1)S(1)}, u32[]{:S(2)}, u32[]{:S(2)}) collective-permute-start(bf16[768,128]{1,0:T(8,128)(2,1)S(1)} %get-tuple-element.12.a_ref), channel_id=1, source_target_pairs={{0,10},{1,11},{2,8},{3,9},{16,26},{17,27},{18,24},{19,25},{32,42},... | collective-permute-start | bytes 589832 | tf_op jit(solution)/shard_map/ppermute | solution.py:289
  2.7 10.3 %collective-permute-start.2 = (bf16[768,128]{1,0:T(8,128)(2,1)S(1)}, bf16[768,128]{1,0:T(8,128)(2,1)S(1)}, u32[]{:S(2)}, u32[]{:S(2)}) collective-permute-start(bf16[768,128]{1,0:T(8,128)(2,1)S(1)} %get-tuple-element.13), channel_id=1, source_target_pairs={{0,14},{1,15},{2,12},{3,13},{16,30},{17,31},{18,28},{19,29},{32,46... | collective-permute-start | bytes 589832 | tf_op jit(solution)/shard_map/ppermute | solution.py:289
  3.3 9.6 %collective-permute-start = (bf16[768,128]{1,0:T(8,128)(2,1)S(1)}, bf16[768,128]{1,0:T(8,128)(2,1)S(1)}, u32[]{:S(2)}, u32[]{:S(2)}) collective-permute-start(bf16[768,128]{1,0:T(8,128)(2,1)S(1)} %get-tuple-element.13), channel_id=1, source_target_pairs={{0,4},{1,5},{2,6},{3,7},{16,20},{17,21},{18,22},{19,23},{32,36},{3... | collective-permute-start | bytes 589832 | tf_op jit(solution)/shard_map/ppermute | solution.py:289
  13.0 14.5 %collective-permute-start.11 = (bf16[768,128]{1,0:T(8,128)(2,1)S(1)}, bf16[768,128]{1,0:T(8,128)(2,1)S(1)}, u32[]{:S(2)}, u32[]{:S(2)}) collective-permute-start(bf16[768,128]{1,0:T(8,128)(2,1)S(1)} %shard_map.39.refs_0_), channel_id=1, source_target_pairs={{0,64},{1,80},{2,0},{3,16},{4,72},{5,88},{6,8},{7,24},{8,32},{9,48... | collective-permute-start | bytes 589832 | tf_op jit(solution)/shard_map/ppermute | solution.py:293
  22.8 15.6 %collective-permute-start.10 = (bf16[768,128]{1,0:T(8,128)(2,1)S(1)}, bf16[768,128]{1,0:T(8,128)(2,1)S(1)}, u32[]{:S(2)}, u32[]{:S(2)}) collective-permute-start(bf16[768,128]{1,0:T(8,128)(2,1)S(1)} %shard_map.39.refs_0_), channel_id=1, source_target_pairs={{0,0},{1,16},{2,64},{3,80},{4,8},{5,24},{6,72},{7,88},{8,96},{9,11... | collective-permute-start | bytes 589832 | tf_op jit(solution)/shard_map/ppermute | solution.py:292
  24.7 14.3 %collective-permute-start.9 = (bf16[768,128]{1,0:T(8,128)(2,1)S(1)}, bf16[768,128]{1,0:T(8,128)(2,1)S(1)}, u32[]{:S(2)}, u32[]{:S(2)}) collective-permute-start(bf16[768,128]{1,0:T(8,128)(2,1)S(1)} %shard_map.39.refs_0_), channel_id=1, source_target_pairs={{13,0},{14,1},{15,2},{12,3},{1,4},{2,5},{3,6},{0,7},{5,8},{6,9},{7... | collective-permute-start | bytes 589832 | tf_op jit(solution)/shard_map/ppermute | solution.py:294
  24.8 14.2 %collective-permute-start.8 = (bf16[768,128]{1,0:T(8,128)(2,1)S(1)}, bf16[768,128]{1,0:T(8,128)(2,1)S(1)}, u32[]{:S(2)}, u32[]{:S(2)}) collective-permute-start(bf16[768,128]{1,0:T(8,128)(2,1)S(1)} %shard_map.39.refs_0_), channel_id=1, source_target_pairs={{12,0},{13,1},{14,2},{15,3},{0,4},{1,5},{2,6},{3,7},{4,8},{5,9},{6... | collective-permute-start | bytes 589832 | tf_op jit(solution)/shard_map/ppermute | solution.py:294
  27.4 11.7 %collective-permute-start.13 = (bf16[768,128]{1,0:T(8,128)(2,1)S(1)}, bf16[768,128]{1,0:T(8,128)(2,1)S(1)}, u32[]{:S(2)}, u32[]{:S(2)}) collective-permute-start(bf16[768,128]{1,0:T(8,128)(2,1)S(1)} %collective-permute-done.11.g1), channel_id=1, source_target_pairs={{0,16},{16,0},{1,17},{17,1},{2,18},{18,2},{3,19},{19,3},{4,20},{20... | collective-permute-start | bytes 589832 | tf_op jit(solution)/shard_map/ppermute | solution.py:297
  38.4 5.7 %collective-permute-start.12 = (bf16[768,128]{1,0:T(8,128)(2,1)S(1)}, bf16[768,128]{1,0:T(8,128)(2,1)S(1)}, u32[]{:S(2)}, u32[]{:S(2)}) collective-permute-start(bf16[768,128]{1,0:T(8,128)(2,1)S(1)} %collective-permute-done.10.g0), channel_id=1, source_target_pairs={{0,16},{16,0},{1,17},{17,1},{2,18},{18,2},{3,19},{19,3},{4,20},{20... | collective-permute-start | bytes 589832 | tf_op jit(solution)/shard_map/ppermute | solution.py:296
  39.0 12.0 %collective-permute-start.7 = (bf16[768,128]{1,0:T(8,128)(2,1)S(1)}, bf16[768,128]{1,0:T(8,128)(2,1)S(1)}, u32[]{:S(2)}, u32[]{:S(2)}) collective-permute-start(bf16[768,128]{1,0:T(8,128)(2,1)S(1)} %shard_map.39.refs_0_), channel_id=1, source_target_pairs={{15,0},{12,1},{13,2},{14,3},{3,4},{0,5},{1,6},{2,7},{7,8},{4,9},{5... | collective-permute-start | bytes 589832 | tf_op jit(solution)/shard_map/ppermute | solution.py:294
  39.0 12.0 %collective-permute-start.6 = (bf16[768,128]{1,0:T(8,128)(2,1)S(1)}, bf16[768,128]{1,0:T(8,128)(2,1)S(1)}, u32[]{:S(2)}, u32[]{:S(2)}) collective-permute-start(bf16[768,128]{1,0:T(8,128)(2,1)S(1)} %shard_map.39.refs_0_), channel_id=1, source_target_pairs={{4,0},{5,1},{6,2},{7,3},{8,4},{9,5},{10,6},{11,7},{12,8},{13,9},{1... | collective-permute-start | bytes 589832 | tf_op jit(solution)/shard_map/ppermute | solution.py:294
  39.0 15.3 %collective-permute-start.5 = (bf16[768,128]{1,0:T(8,128)(2,1)S(1)}, bf16[768,128]{1,0:T(8,128)(2,1)S(1)}, u32[]{:S(2)}, u32[]{:S(2)}) collective-permute-start(bf16[768,128]{1,0:T(8,128)(2,1)S(1)} %shard_map.39.refs_0_), channel_id=1, source_target_pairs={{3,0},{0,1},{1,2},{2,3},{7,4},{4,5},{5,6},{6,7},{11,8},{8,9},{9,10... | collective-permute-start | bytes 589832 | tf_op jit(solution)/shard_map/ppermute | solution.py:294
  39.1 15.2 %collective-permute-start.4 = (bf16[768,128]{1,0:T(8,128)(2,1)S(1)}, bf16[768,128]{1,0:T(8,128)(2,1)S(1)}, u32[]{:S(2)}, u32[]{:S(2)}) collective-permute-start(bf16[768,128]{1,0:T(8,128)(2,1)S(1)} %shard_map.39.refs_0_), channel_id=1, source_target_pairs={{8,0},{9,1},{10,2},{11,3},{12,4},{13,5},{14,6},{15,7},{0,8},{1,9},... | collective-permute-start | bytes 589832 | tf_op jit(solution)/shard_map/ppermute | solution.py:294
  44.0 10.2 %collective-permute-start.3 = (bf16[768,128]{1,0:T(8,128)(2,1)S(1)}, bf16[768,128]{1,0:T(8,128)(2,1)S(1)}, u32[]{:S(2)}, u32[]{:S(2)}) collective-permute-start(bf16[768,128]{1,0:T(8,128)(2,1)S(1)} %shard_map.39.refs_0_), channel_id=1, source_target_pairs={{1,0},{2,1},{3,2},{0,3},{5,4},{6,5},{7,6},{4,7},{9,8},{10,9},{11,1... | collective-permute-start | bytes 589832 | tf_op jit(solution)/shard_map/ppermute | solution.py:294
  44.0 1.1 %copy-start = (s32[384,384]{1,0:T(8,128)S(1)}, s32[384,384]{1,0:T(8,128)}, u32[]{:S(2)}) copy-start(s32[384,384]{1,0:T(8,128)} %pattern_ref.1) | copy-start | bytes 1769476
  45.1 0.9 %copy-start.1 = (bf16[256,256]{1,0:T(8,128)(2,1)S(1)}, bf16[256,256]{1,0:T(8,128)(2,1)}, u32[]{:S(2)}) copy-start(bf16[256,256]{1,0:T(8,128)(2,1)} %diag_ref.1) | copy-start | bytes 393220

commit v4 on v3

--- a/solution.py
+++ b/solution.py
@@ -70,9 +70,9 @@
     ((2, 0), (0, 2)),
     ((0, -1), (0, -1)),
     ((1, 0), (1, 0)),
-    ((-1, -1), (-1, -1)),
+    ((1, 1), (1, 1)),
     ((-1, 0), (-1, 0)),
-    ((-1, 1), (1, -1)),
+    ((1, -1), (-1, 1)),
 )
 
 

time: 60.9 us -> 59 us (0.969)
  the two profiles are of different devices: /device:TPU:21 before, /device:TPU:5 now
where the time goes in v4:
time: 59 us; the launch traced here: 58.7 us
  starting transfers between devices  33 us (56%)
  Pallas kernels  11.5 us (19%)
  waiting for transfers between devices  10.9 us (18%)
  local copies, waits for them, and re-layouts  3.15 us (5%)
    ppermute x7, starting transfers between devices, body(): lax.ppermute(own, ALL, shift_perm(*offsets))  11.5 us
    ppermute x3, starting transfers between devices, body(): lax.ppermute(part, ALL, spread_perm(k))  10.7 us
    pallas_call x1, Pallas kernels, update(): pl.pallas_call(update_kernel, grid=(2, 2), out_shape=jax.ShapeDtypeStruct...  6.32 us
    ppermute x1, starting transfers between devices, body(): g1 = lax.ppermute(own, ALL, column_perm(1))  5.93 us
    ppermute x1, waiting for transfers between devices, body(): g0 = lax.ppermute(own, ALL, column_perm(0))  5.54 us
    ppermute x3, waiting for transfers between devices, body(): lax.ppermute(part, ALL, spread_perm(k))  5.13 us
    pallas_call x1, Pallas kernels, prepare(): pl.pallas_call(prepare_kernel, out_shape=(jax.ShapeDtypeStruct((2, 2, Q,...  3.98 us
    ppermute x1, starting transfers between devices, body(): g2 = lax.ppermute(g0, 'core', swap)  2.84 us
  transfers between devices with their start and end apart: 14, of which 5 were waited for; matrix products, arithmetic and copies ran while one was open for 0% of the time, Pallas kernels for 8%

profile of v4, /device:TPU:5, one launch (start us, length us, event | category | flops | bytes accessed | tf_op | source)
XLA Modules:
  0.0 58.7 jit_solution(16095265263410857650)
XLA Ops:
  0.0 1.2 %slice.3 = bf16[3072,128]{1,0:T(8,128)(2,1)S(1)} slice(bf16[3072,1536]{1,0:T(8,128)(2,1)} %param.3), slice={[0:3072], [0:128]} | slice | bytes 1572864 | tf_op jit(solution)/shard_map/slice | solution.py:286
  1.2 0.2 shard_map.38
  1.4 8.1 %collective-permute-start.1 = (bf16[768,128]{1,0:T(8,128)(2,1)S(1)}, bf16[768,128]{1,0:T(8,128)(2,1)S(1)}, u32[]{:S(2)}, u32[]{:S(2)}) collective-permute-start(bf16[768,128]{1,0:T(8,128)(2,1)S(1)} %get-tuple-element.12.a_ref), channel_id=1, source_target_pairs={{0,10},{1,11},{2,8},{3,9},{16,26},{17,27},{18,24},{19,25},{32,42},... | collective-permute-start | bytes 589832 | tf_op jit(solution)/shard_map/ppermute | solution.py:289
  9.5 1.3 %collective-permute-start.2 = (bf16[768,128]{1,0:T(8,128)(2,1)S(1)}, bf16[768,128]{1,0:T(8,128)(2,1)S(1)}, u32[]{:S(2)}, u32[]{:S(2)}) collective-permute-start(bf16[768,128]{1,0:T(8,128)(2,1)S(1)} %get-tuple-element.13), channel_id=1, source_target_pairs={{0,14},{1,15},{2,12},{3,13},{16,30},{17,31},{18,28},{19,29},{32,46... | collective-permute-start | bytes 589832 | tf_op jit(solution)/shard_map/ppermute | solution.py:289
  10.8 1.3 %collective-permute-start = (bf16[768,128]{1,0:T(8,128)(2,1)S(1)}, bf16[768,128]{1,0:T(8,128)(2,1)S(1)}, u32[]{:S(2)}, u32[]{:S(2)}) collective-permute-start(bf16[768,128]{1,0:T(8,128)(2,1)S(1)} %get-tuple-element.13), channel_id=1, source_target_pairs={{0,4},{1,5},{2,6},{3,7},{16,20},{17,21},{18,22},{19,23},{32,36},{3... | collective-permute-start | bytes 589832 | tf_op jit(solution)/shard_map/ppermute | solution.py:289
  12.1 0.9 %collective-permute-done.1.c_ref = bf16[768,128]{1,0:T(8,128)(2,1)S(1)} collective-permute-done((bf16[768,128]{1,0:T(8,128)(2,1)S(1)}, bf16[768,128]{1,0:T(8,128)(2,1)S(1)}, u32[]{:S(2)}, u32[]{:S(2)}) %collective-permute-start.1) | collective-permute-done | bytes 196640 | tf_op jit(solution)/shard_map/ppermute | solution.py:289
  13.1 1.3 %collective-permute-done.2.d_ref = bf16[768,128]{1,0:T(8,128)(2,1)S(1)} collective-permute-done((bf16[768,128]{1,0:T(8,128)(2,1)S(1)}, bf16[768,128]{1,0:T(8,128)(2,1)S(1)}, u32[]{:S(2)}, u32[]{:S(2)}) %collective-permute-start.2) | collective-permute-done | bytes 196640 | tf_op jit(solution)/shard_map/ppermute | solution.py:289
  14.4 2.9 %collective-permute-done.b_ref = bf16[768,128]{1,0:T(8,128)(2,1)S(1)} collective-permute-done((bf16[768,128]{1,0:T(8,128)(2,1)S(1)}, bf16[768,128]{1,0:T(8,128)(2,1)S(1)}, u32[]{:S(2)}, u32[]{:S(2)}) %collective-permute-start) | collective-permute-done | bytes 196640 | tf_op jit(solution)/shard_map/ppermute | solution.py:289
  17.3 5.9 %collective-permute-start.11 = (bf16[768,128]{1,0:T(8,128)(2,1)S(1)}, bf16[768,128]{1,0:T(8,128)(2,1)S(1)}, u32[]{:S(2)}, u32[]{:S(2)}) collective-permute-start(bf16[768,128]{1,0:T(8,128)(2,1)S(1)} %shard_map.39.refs_0_), channel_id=1, source_target_pairs={{0,64},{1,80},{2,0},{3,16},{4,72},{5,88},{6,8},{7,24},{8,32},{9,48... | collective-permute-start | bytes 589832 | tf_op jit(solution)/shard_map/ppermute | solution.py:293
  23.2 2.0 %collective-permute-start.10 = (bf16[768,128]{1,0:T(8,128)(2,1)S(1)}, bf16[768,128]{1,0:T(8,128)(2,1)S(1)}, u32[]{:S(2)}, u32[]{:S(2)}) collective-permute-start(bf16[768,128]{1,0:T(8,128)(2,1)S(1)} %shard_map.39.refs_0_), channel_id=1, source_target_pairs={{0,0},{1,16},{2,64},{3,80},{4,8},{5,24},{6,72},{7,88},{8,96},{9,11... | collective-permute-start | bytes 589832 | tf_op jit(solution)/shard_map/ppermute | solution.py:292
  25.2 0.1 collective-permute-start.9
  25.3 4.9 %collective-permute-start.8 = (bf16[768,128]{1,0:T(8,128)(2,1)S(1)}, bf16[768,128]{1,0:T(8,128)(2,1)S(1)}, u32[]{:S(2)}, u32[]{:S(2)}) collective-permute-start(bf16[768,128]{1,0:T(8,128)(2,1)S(1)} %shard_map.39.refs_0_), channel_id=1, source_target_pairs={{12,0},{13,1},{14,2},{15,3},{0,4},{1,5},{2,6},{3,7},{4,8},{5,9},{6... | collective-permute-start | bytes 589832 | tf_op jit(solution)/shard_map/ppermute | solution.py:294
  30.2 0.0 collective-permute-done.11.g1
  30.2 0.0 collective-permute-start.13
  30.2 5.5 %collective-permute-done.10.g0 = bf16[768,128]{1,0:T(8,128)(2,1)S(1)} collective-permute-done((bf16[768,128]{1,0:T(8,128)(2,1)S(1)}, bf16[768,128]{1,0:T(8,128)(2,1)S(1)}, u32[]{:S(2)}, u32[]{:S(2)}) %collective-permute-start.10) | collective-permute-done | bytes 196640 | tf_op jit(solution)/shard_map/ppermute | solution.py:292
  35.7 2.8 %collective-permute-start.12 = (bf16[768,128]{1,0:T(8,128)(2,1)S(1)}, bf16[768,128]{1,0:T(8,128)(2,1)S(1)}, u32[]{:S(2)}, u32[]{:S(2)}) collective-permute-start(bf16[768,128]{1,0:T(8,128)(2,1)S(1)} %collective-permute-done.10.g0), channel_id=1, source_target_pairs={{0,16},{16,0},{1,17},{17,1},{2,18},{18,2},{3,19},{19,3},{4,20},{20... | collective-permute-start | bytes 589832 | tf_op jit(solution)/shard_map/ppermute | solution.py:296
  38.6 0.0 collective-permute-start.7
  38.6 0.0 collective-permute-done.9.refs_7_
  38.6 0.0 collective-permute-start.6
  38.6 0.0 collective-permute-done.8.refs_6_
  38.6 4.1 %collective-permute-start.5 = (bf16[768,128]{1,0:T(8,128)(2,1)S(1)}, bf16[768,128]{1,0:T(8,128)(2,1)S(1)}, u32[]{:S(2)}, u32[]{:S(2)}) collective-permute-start(bf16[768,128]{1,0:T(8,128)(2,1)S(1)} %shard_map.39.refs_0_), channel_id=1, source_target_pairs={{3,0},{0,1},{1,2},{2,3},{7,4},{4,5},{5,6},{6,7},{11,8},{8,9},{9,10... | collective-permute-start | bytes 589832 | tf_op jit(solution)/shard_map/ppermute | solution.py:294
  42.7 0.0 collective-permute-done.13.g3
  42.7 0.0 collective-permute-start.4
  42.7 0.0 collective-permute-done.12.g2
  42.7 2.5 %collective-permute-start.3 = (bf16[768,128]{1,0:T(8,128)(2,1)S(1)}, bf16[768,128]{1,0:T(8,128)(2,1)S(1)}, u32[]{:S(2)}, u32[]{:S(2)}) collective-permute-start(bf16[768,128]{1,0:T(8,128)(2,1)S(1)} %shard_map.39.refs_0_), channel_id=1, source_target_pairs={{1,0},{2,1},{3,2},{0,3},{5,4},{6,5},{7,6},{4,7},{9,8},{10,9},{11,1... | collective-permute-start | bytes 589832 | tf_op jit(solution)/shard_map/ppermute | solution.py:294
  45.2 1.1 %copy-done = s32[384,384]{1,0:T(8,128)S(1)} copy-done((s32[384,384]{1,0:T(8,128)S(1)}, s32[384,384]{1,0:T(8,128)}, u32[]{:S(2)}) %copy-start) | copy-done | bytes 589848
  46.3 0.9 %copy-done.1 = bf16[256,256]{1,0:T(8,128)(2,1)S(1)} copy-done((bf16[256,256]{1,0:T(8,128)(2,1)S(1)}, bf16[256,256]{1,0:T(8,128)(2,1)}, u32[]{:S(2)}) %copy-start.1) | copy-done | bytes 131096
  47.2 4.0 %shard_map.37 = (bf16[2,2,4,128,256]{4,3,2,1,0:T(8,128)(2,1)S(1)}, bf16[2,4,256,128]{3,2,1,0:T(8,128)(2,1)S(1)}, f32[48,1536]{1,0:T(8,128)S(1)}, bf16[24,2,64,1536]{3,2,1,0:T(8,128)(2,1)S(1)}) custom-call(bf16[24,2,64,1536]{3,2,1,0:T(8,128)(2,1)} %bitcast.4, bf16[256,256]{1,0:T(8,128)(2,1)S(1)} %copy-done.1, s32[384,384]{1,0:T(8,128)S(1)} %copy-done), custom_call_target="tpu_custom_call" | custom-call | bytes 18874368 | tf_op jit(solution)/shard_map/pallas_call | solution.py:181
  51.2 1.0 %shard_map.40.refs_8_ = bf16[256,1536]{1,0:T(8,128)(2,1)S(1)} custom-call(bf16[768,128]{1,0:T(8,128)(2,1)S(1)} %collective-permute-done.10.g0, bf16[768,128]{1,0:T(8,128)(2,1)S(1)} %collective-permute-done.11.g1, bf16[768,128]{1,0:T(8,128)(2,1)S(1)} %collective-permute-done.12.g2, bf16[768,128]{1,0:T(8,128)(2,1)S(1)} %collective-permute-done.13.g3, ...), custom_call_target="tpu_custom_call" | custom-call | flops 402653184 | bytes 2359296 | tf_op jit(solution)/shard_map/pallas_call | solution.py:218
  52.2 0.0 collective-permute-done.6.refs_4_
  52.2 0.2 collective-permute-done.3.refs_1_
  52.4 6.3 %shard_map.41 = bf16[24,2,64,1536]{3,2,1,0:T(8,128)(2,1)} custom-call(bf16[24,2,64,1536]{3,2,1,0:T(8,128)(2,1)S(1)} %get-tuple-element.11.front_ref, bf16[768,128]{1,0:T(8,128)(2,1)S(1)} %shard_map.39.refs_0_, bf16[768,128]{1,0:T(8,128)(2,1)S(1)} %collective-permute-done.3.refs_1_, bf16[768,128]{1,0:T(8,128)(2,1)S(1)} %collective-permute-done.4.refs_2_, ...), custom_call_target="tpu_custom_call" | custom-call | flops 2415919104 | bytes 18874368 | tf_op jit(solution)/shard_map/pallas_call | solution.py:270
  (6 shorter events, 0.0 us)
Async XLA Ops:
  1.4 11.7 %collective-permute-start.1 = (bf16[768,128]{1,0:T(8,128)(2,1)S(1)}, bf16[768,128]{1,0:T(8,128)(2,1)S(1)}, u32[]{:S(2)}, u32[]{:S(2)}) collective-permute-start(bf16[768,128]{1,0:T(8,128)(2,1)S(1)} %get-tuple-element.12.a_ref), channel_id=1, source_target_pairs={{0,10},{1,11},{2,8},{3,9},{16,26},{17,27},{18,24},{19,25},{32,42},... | collective-permute-start | bytes 589832 | tf_op jit(solution)/shard_map/ppermute | solution.py:289
  9.5 4.8 %collective-permute-start.2 = (bf16[768,128]{1,0:T(8,128)(2,1)S(1)}, bf16[768,128]{1,0:T(8,128)(2,1)S(1)}, u32[]{:S(2)}, u32[]{:S(2)}) collective-permute-start(bf16[768,128]{1,0:T(8,128)(2,1)S(1)} %get-tuple-element.13), channel_id=1, source_target_pairs={{0,14},{1,15},{2,12},{3,13},{16,30},{17,31},{18,28},{19,29},{32,46... | collective-permute-start | bytes 589832 | tf_op jit(solution)/shard_map/ppermute | solution.py:289
  10.8 6.4 %collective-permute-start = (bf16[768,128]{1,0:T(8,128)(2,1)S(1)}, bf16[768,128]{1,0:T(8,128)(2,1)S(1)}, u32[]{:S(2)}, u32[]{:S(2)}) collective-permute-start(bf16[768,128]{1,0:T(8,128)(2,1)S(1)} %get-tuple-element.13), channel_id=1, source_target_pairs={{0,4},{1,5},{2,6},{3,7},{16,20},{17,21},{18,22},{19,23},{32,36},{3... | collective-permute-start | bytes 589832 | tf_op jit(solution)/shard_map/ppermute | solution.py:289
  17.3 12.9 %collective-permute-start.11 = (bf16[768,128]{1,0:T(8,128)(2,1)S(1)}, bf16[768,128]{1,0:T(8,128)(2,1)S(1)}, u32[]{:S(2)}, u32[]{:S(2)}) collective-permute-start(bf16[768,128]{1,0:T(8,128)(2,1)S(1)} %shard_map.39.refs_0_), channel_id=1, source_target_pairs={{0,64},{1,80},{2,0},{3,16},{4,72},{5,88},{6,8},{7,24},{8,32},{9,48... | collective-permute-start | bytes 589832 | tf_op jit(solution)/shard_map/ppermute | solution.py:293
  23.2 12.5 %collective-permute-start.10 = (bf16[768,128]{1,0:T(8,128)(2,1)S(1)}, bf16[768,128]{1,0:T(8,128)(2,1)S(1)}, u32[]{:S(2)}, u32[]{:S(2)}) collective-permute-start(bf16[768,128]{1,0:T(8,128)(2,1)S(1)} %shard_map.39.refs_0_), channel_id=1, source_target_pairs={{0,0},{1,16},{2,64},{3,80},{4,8},{5,24},{6,72},{7,88},{8,96},{9,11... | collective-permute-start | bytes 589832 | tf_op jit(solution)/shard_map/ppermute | solution.py:292
  25.2 13.3 %collective-permute-start.9 = (bf16[768,128]{1,0:T(8,128)(2,1)S(1)}, bf16[768,128]{1,0:T(8,128)(2,1)S(1)}, u32[]{:S(2)}, u32[]{:S(2)}) collective-permute-start(bf16[768,128]{1,0:T(8,128)(2,1)S(1)} %shard_map.39.refs_0_), channel_id=1, source_target_pairs={{7,0},{4,1},{5,2},{6,3},{11,4},{8,5},{9,6},{10,7},{15,8},{12,9},{1... | collective-permute-start | bytes 589832 | tf_op jit(solution)/shard_map/ppermute | solution.py:294
  25.3 13.3 %collective-permute-start.8 = (bf16[768,128]{1,0:T(8,128)(2,1)S(1)}, bf16[768,128]{1,0:T(8,128)(2,1)S(1)}, u32[]{:S(2)}, u32[]{:S(2)}) collective-permute-start(bf16[768,128]{1,0:T(8,128)(2,1)S(1)} %shard_map.39.refs_0_), channel_id=1, source_target_pairs={{12,0},{13,1},{14,2},{15,3},{0,4},{1,5},{2,6},{3,7},{4,8},{5,9},{6... | collective-permute-start | bytes 589832 | tf_op jit(solution)/shard_map/ppermute | solution.py:294
  30.2 12.5 %collective-permute-start.13 = (bf16[768,128]{1,0:T(8,128)(2,1)S(1)}, bf16[768,128]{1,0:T(8,128)(2,1)S(1)}, u32[]{:S(2)}, u32[]{:S(2)}) collective-permute-start(bf16[768,128]{1,0:T(8,128)(2,1)S(1)} %collective-permute-done.11.g1), channel_id=1, source_target_pairs={{0,16},{16,0},{1,17},{17,1},{2,18},{18,2},{3,19},{19,3},{4,20},{20... | collective-permute-start | bytes 589832 | tf_op jit(solution)/shard_map/ppermute | solution.py:297
  35.7 7.0 %collective-permute-start.12 = (bf16[768,128]{1,0:T(8,128)(2,1)S(1)}, bf16[768,128]{1,0:T(8,128)(2,1)S(1)}, u32[]{:S(2)}, u32[]{:S(2)}) collective-permute-start(bf16[768,128]{1,0:T(8,128)(2,1)S(1)} %collective-permute-done.10.g0), channel_id=1, source_target_pairs={{0,16},{16,0},{1,17},{17,1},{2,18},{18,2},{3,19},{19,3},{4,20},{20... | collective-permute-start | bytes 589832 | tf_op jit(solution)/shard_map/ppermute | solution.py:296
  38.6 13.6 %collective-permute-start.7 = (bf16[768,128]{1,0:T(8,128)(2,1)S(1)}, bf16[768,128]{1,0:T(8,128)(2,1)S(1)}, u32[]{:S(2)}, u32[]{:S(2)}) collective-permute-start(bf16[768,128]{1,0:T(8,128)(2,1)S(1)} %shard_map.39.refs_0_), channel_id=1, source_target_pairs={{5,0},{6,1},{7,2},{4,3},{9,4},{10,5},{11,6},{8,7},{13,8},{14,9},{1... | collective-permute-start | bytes 589832 | tf_op jit(solution)/shard_map/ppermute | solution.py:294
  38.6 13.6 %collective-permute-start.6 = (bf16[768,128]{1,0:T(8,128)(2,1)S(1)}, bf16[768,128]{1,0:T(8,128)(2,1)S(1)}, u32[]{:S(2)}, u32[]{:S(2)}) collective-permute-start(bf16[768,128]{1,0:T(8,128)(2,1)S(1)} %shard_map.39.refs_0_), channel_id=1, source_target_pairs={{4,0},{5,1},{6,2},{7,3},{8,4},{9,5},{10,6},{11,7},{12,8},{13,9},{1... | collective-permute-start | bytes 589832 | tf_op jit(solution)/shard_map/ppermute | solution.py:294
  38.6 13.6 %collective-permute-start.5 = (bf16[768,128]{1,0:T(8,128)(2,1)S(1)}, bf16[768,128]{1,0:T(8,128)(2,1)S(1)}, u32[]{:S(2)}, u32[]{:S(2)}) collective-permute-start(bf16[768,128]{1,0:T(8,128)(2,1)S(1)} %shard_map.39.refs_0_), channel_id=1, source_target_pairs={{3,0},{0,1},{1,2},{2,3},{7,4},{4,5},{5,6},{6,7},{11,8},{8,9},{9,10... | collective-permute-start | bytes 589832 | tf_op jit(solution)/shard_map/ppermute | solution.py:294
  42.7 9.5 %collective-permute-start.4 = (bf16[768,128]{1,0:T(8,128)(2,1)S(1)}, bf16[768,128]{1,0:T(8,128)(2,1)S(1)}, u32[]{:S(2)}, u32[]{:S(2)}) collective-permute-start(bf16[768,128]{1,0:T(8,128)(2,1)S(1)} %shard_map.39.refs_0_), channel_id=1, source_target_pairs={{8,0},{9,1},{10,2},{11,3},{12,4},{13,5},{14,6},{15,7},{0,8},{1,9},... | collective-permute-start | bytes 589832 | tf_op jit(solution)/shard_map/ppermute | solution.py:294
  42.7 9.7 %collective-permute-start.3 = (bf16[768,128]{1,0:T(8,128)(2,1)S(1)}, bf16[768,128]{1,0:T(8,128)(2,1)S(1)}, u32[]{:S(2)}, u32[]{:S(2)}) collective-permute-start(bf16[768,128]{1,0:T(8,128)(2,1)S(1)} %shard_map.39.refs_0_), channel_id=1, source_target_pairs={{1,0},{2,1},{3,2},{0,3},{5,4},{6,5},{7,6},{4,7},{9,8},{10,9},{11,1... | collective-permute-start | bytes 589832 | tf_op jit(solution)/shard_map/ppermute | solution.py:294
  45.2 1.1 %copy-start = (s32[384,384]{1,0:T(8,128)S(1)}, s32[384,384]{1,0:T(8,128)}, u32[]{:S(2)}) copy-start(s32[384,384]{1,0:T(8,128)} %pattern_ref.1) | copy-start | bytes 1769476
  46.3 0.9 %copy-start.1 = (bf16[256,256]{1,0:T(8,128)(2,1)S(1)}, bf16[256,256]{1,0:T(8,128)(2,1)}, u32[]{:S(2)}) copy-start(bf16[256,256]{1,0:T(8,128)(2,1)} %diag_ref.1) | copy-start | bytes 393220

commit v5 on v4

--- a/solution.py
+++ b/solution.py
@@ -38,42 +38,17 @@
     return pairs
 
 
-def column_perm(step):
+def column_perm():
     pairs = []
     for x in range(4):
         for core in range(2):
             r = 2 * x + core
             for y in range(4):
                 for z in range(4):
-                    q, half, far = quarter_of(y, z), y % 2, y // 2
-                    near = (step == 0) == (q < 2)
-                    to_x = (x + far + (0 if near else 2)) % 4
-                    target = linear(to_x, q % 2, 2 * half + r // 4, r % 4)
+                    to_x = (x + 2 * (y // 2) + z % 2) % 4
+                    target = linear(to_x, quarter_of(y, z) // 2, 2 * (y % 2) + r // 4, r % 4)
                     pairs.append((linear(x, core, y, z), target))
     return pairs
-
-
-def shift_perm(first, second):
-    pairs = []
-    for x in range(4):
-        for core in range(2):
-            dy, dz = (first, second)[core]
-            for y in range(4):
-                for z in range(4):
-                    source = linear(x, core, (y + dy) % 4, (z + dz) % 4)
-                    pairs.append((source, linear(x, core, y, z)))
-    return pairs
-
-
-OFFSETS = (
-    ((0, 1), (0, 1)),
-    ((2, 0), (0, 2)),
-    ((0, -1), (0, -1)),
-    ((1, 0), (1, 0)),
-    ((1, 1), (1, 1)),
-    ((-1, 0), (-1, 0)),
-    ((1, -1), (-1, 1)),
-)
 
 
 def pack_kernel(panel_ref, even_ref, odd_ref):
@@ -139,16 +114,16 @@
     turned = lax.dot_general(eye, diag, NT, preferred_element_type=F32).astype(BF16)
     bases = (own, lax.rem(own + 2 * lax.rem(y, 2), 4))
     source_x = 2 * lax.rem(y, 2) + z // 2
-    half = lax.rem(x - source_x + 4, 4) // 2
+    swapped = lax.rem(x - source_x + 4, 2)
     for q in range(Q):
         part = turned[q * B : q * B + B, :]
         zero = jnp.zeros_like(part)
         for kind, base in enumerate(bases):
-            slot = lax.rem(q - base + 4, 4)
+            slot = jnp.bitwise_xor(q, base)
             row_w_ref[kind, 0, slot] = jnp.concatenate([part, zero], axis=0)
             row_w_ref[kind, 1, slot] = jnp.concatenate([zero, part], axis=0)
-        other = jnp.where(q % 2 == core, 0, 2)
-        late = jnp.where(q // 2 == half, 0, 1)
+        other = jnp.where(q // 2 == core, 0, 2)
+        late = jnp.bitwise_xor(q % 2, swapped)
         part = diag[:, q * B : q * B + B]
         zero = jnp.zeros_like(part)
         col_w_ref[0, other + late] = jnp.concatenate([part, zero], axis=1)
@@ -196,12 +171,13 @@
     )(front4, diag_inverse, fill_pattern)
 
 
-def column_kernel(g0, g1, g2, g3, col_w_ref, out_ref):
+def column_kernel(near_ref, far_ref, col_w_ref, out_ref):
     col_id = lax.axis_index("y") * 4 + lax.axis_index("z")
     for u in range(2):
         total = jnp.zeros((WIDTH, ROWS), F32)
-        for k, g in enumerate((g0, g1, g2, g3)):
-            total += lax.dot_general(col_w_ref[u, k], g[...], NT, preferred_element_type=F32)
+        for k in range(Q):
+            g = (near_ref, far_ref)[k // 2][k % 2]
+            total += lax.dot_general(col_w_ref[u, k], g, NT, preferred_element_type=F32)
         out_ref[:, u * ROWS : (u + 1) * ROWS] = total.astype(BF16)
 
     @pl.when(col_id < Q)
@@ -218,35 +194,53 @@
     return pl.pallas_call(
         column_kernel,
         out_shape=jax.ShapeDtypeStruct((WIDTH, COLS), BF16),
+        in_specs=[whole] * 3,
+        out_specs=whole,
+        compiler_params=pltpu.CompilerParams(vmem_limit_bytes=16 << 20),
+        cost_estimate=pl.CostEstimate(
+            flops=2 * COLS * 256 * 512, bytes_accessed=2 * COLS * 768, transcendentals=0
+        ),
+    )(*columns, col_w)
+
+
+CHUNK = 512
+
+
+def factor_kernel(own_ref, z_ref, next_ref, prev_ref, row_w_ref, out_ref):
+    y = lax.axis_index("y")
+    fours = (
+        (own_ref[0], own_ref[1], z_ref[1], z_ref[0]),
+        (next_ref[0], next_ref[1], prev_ref[0], prev_ref[1]),
+    )
+    for kind, four in enumerate(fours):
+        parity = lax.rem(y + kind, 2)
+        joined = jnp.concatenate(four, axis=1)
+        for u in range(2):
+            out_ref[parity, u] = jnp.dot(
+                joined,
+                row_w_ref[kind, u].reshape(Q * 128, WIDTH),
+                preferred_element_type=F32,
+            ).astype(BF16)
+
+
+def row_factor(parts, row_w):
+    whole = pl.BlockSpec(memory_space=VMEM)
+    return pl.pallas_call(
+        factor_kernel,
+        out_shape=jax.ShapeDtypeStruct((2, 2, ROWS, WIDTH), BF16),
         in_specs=[whole] * 5,
         out_specs=whole,
         compiler_params=pltpu.CompilerParams(vmem_limit_bytes=16 << 20),
         cost_estimate=pl.CostEstimate(
-            flops=2 * COLS * 256 * 512, bytes_accessed=2 * COLS * 768, transcendentals=0
-        ),
-    )(*columns, col_w)
-
-
-CHUNK = 512
-
-
-def update_kernel(front_ref, *refs):
-    parts, (gt_ref, row_w_ref, mask_ref, out_ref, factor_ref) = refs[:8], refs[8:]
+            flops=2 * 3072 * 256 * 512, bytes_accessed=4 * 3072 * 256, transcendentals=0
+        ),
+    )(*parts, row_w)
+
+
+def update_kernel(front_ref, factor_ref, gt_ref, mask_ref, out_ref):
     parity, u = pl.program_id(0), pl.program_id(1)
-    y, z = lax.axis_index("y"), lax.axis_index("z")
-    owner = y * 4 + z < Q
-    for kind in range(2):
-
-        @pl.when(lax.rem(y + kind, 2) == parity)
-        def _():
-            four = [p[...] for p in parts[4 * kind : 4 * kind + 4]]
-            factor_ref[...] = jnp.dot(
-                jnp.concatenate(four, axis=1),
-                row_w_ref[kind, u].reshape(Q * 128, WIDTH),
-                preferred_element_type=F32,
-            ).astype(BF16)
-
-    factor = factor_ref[...]
+    owner = lax.axis_index("y") * 4 + lax.axis_index("z") < Q
+    factor = factor_ref[parity, u]
     lane = lax.broadcasted_iota(jnp.int32, (B, 128), 1)
     for c in range(COLS // CHUNK):
         product = jnp.dot(
@@ -265,20 +259,19 @@
                 out_ref[b, 0, :, cols] = new.astype(BF16)
 
 
-def update(front4, parts, columns, row_w, mask):
+def update(front4, factor, columns, mask):
     whole = pl.BlockSpec(memory_space=VMEM)
     return pl.pallas_call(
         update_kernel,
         grid=(2, 2),
         out_shape=jax.ShapeDtypeStruct((PAIRS, 2, B, COLS), BF16),
-        in_specs=[whole] * 12,
-        scratch_shapes=[VMEM((ROWS, WIDTH), BF16)],
+        in_specs=[whole] * 4,
         out_specs=pl.BlockSpec((HALF, 1, B, COLS), lambda p, u: (u, p, 0, 0)),
         compiler_params=pltpu.CompilerParams(vmem_limit_bytes=20 << 20),
         cost_estimate=pl.CostEstimate(
             flops=2 * 3072 * 1536 * 256, bytes_accessed=4 * 3072 * 1536, transcendentals=0
         ),
-    )(front4, *parts, columns, row_w, mask)
+    )(front4, factor, columns, mask)
 
 
 def body(front, diag_inverse, fill_pattern):
@@ -289,14 +282,16 @@
         lax.ppermute(part, ALL, spread_perm(k)) for k, part in enumerate((odd, even, odd))
     ]
     own = choose(even, *spread)
-    g0 = lax.ppermute(own, ALL, column_perm(0))
-    g1 = lax.ppermute(own, ALL, column_perm(1))
-    parts = [own] + [lax.ppermute(own, ALL, shift_perm(*offsets)) for offsets in OFFSETS]
-    swap = [(0, 1), (1, 0)]
-    g2 = lax.ppermute(g0, "core", swap)
-    g3 = lax.ppermute(g1, "core", swap)
-    columns = column_factor((g0, g1, g2, g3), col_w)
-    out = update(stay, parts, columns, row_w, mask)
+    mate = lax.ppermute(own, "z", [(0, 1), (1, 0), (2, 3), (3, 2)])
+    pair = jnp.stack([own, mate])
+    near = lax.ppermute(pair, ALL, column_perm())
+    z_pair = lax.ppermute(pair, "z", [(1, 2), (2, 1), (3, 0), (0, 3)])
+    y_next = lax.ppermute(pair, "y", [((i + 1) % 4, i) for i in range(4)])
+    y_prev = lax.ppermute(pair, "y", [(i, (i + 1) % 4) for i in range(4)])
+    far = lax.ppermute(near, "core", [(0, 1), (1, 0)])
+    factor = row_factor((pair, z_pair, y_next, y_prev), row_w)
+    columns = column_factor((near, far), col_w)
+    out = update(stay, factor, columns, mask)
     return out.reshape(front.shape)
 
 

time: 59 us -> 57.9 us (0.981)
  the two profiles are of different devices: /device:TPU:5 before, /device:TPU:7 now
where the time goes in v5:
time: 57.9 us; the launch traced here: 57.7 us
  starting transfers between devices  26 us (45%)
  waiting for transfers between devices  17.1 us (30%)
  Pallas kernels  11.3 us (20%)
  local copies, waits for them, and re-layouts  3.15 us (5%)
    ppermute x3, starting transfers between devices, body(): lax.ppermute(part, ALL, spread_perm(k))  10.7 us
    ppermute x1, waiting for transfers between devices, body(): near = lax.ppermute(pair, ALL, column_perm())  7.82 us
    ppermute x1, starting transfers between devices, body(): near = lax.ppermute(pair, ALL, column_perm())  6.61 us
    pallas_call x1, Pallas kernels, update(): pl.pallas_call(update_kernel, grid=(2, 2), out_shape=jax.ShapeDtypeStruct...  5.21 us
    ppermute x3, waiting for transfers between devices, body(): lax.ppermute(part, ALL, spread_perm(k))  5.13 us
    ppermute x1, starting transfers between devices, body(): far = lax.ppermute(near, 'core', [(0, 1), (1, 0)])  5.04 us
    ppermute x1, waiting for transfers between devices, body(): mate = lax.ppermute(own, 'z', [(0, 1), (1, 0), (2, 3), (3, 2)])  4.11 us
    pallas_call x1, Pallas kernels, prepare(): pl.pallas_call(prepare_kernel, out_shape=(jax.ShapeDtypeStruct((2, 2, Q,...  3.97 us
  transfers between devices with their start and end apart: 9, of which 5 were waited for; matrix products, arithmetic and copies ran while one was open for 0% of the time, Pallas kernels for 9%

profile of v5, /device:TPU:7, one launch (start us, length us, event | category | flops | bytes accessed | tf_op | source)
XLA Modules:
  0.0 57.7 jit_solution(7692436209127977971)
XLA Ops:
  0.0 1.2 %slice.3 = bf16[3072,128]{1,0:T(8,128)(2,1)S(1)} slice(bf16[3072,1536]{1,0:T(8,128)(2,1)} %param.3), slice={[0:3072], [0:128]} | slice | bytes 1572864 | tf_op jit(solution)/shard_map/slice | solution.py:279
  1.2 0.2 shard_map.38
  1.4 8.1 %collective-permute-start.1 = (bf16[768,128]{1,0:T(8,128)(2,1)S(1)}, bf16[768,128]{1,0:T(8,128)(2,1)S(1)}, u32[]{:S(2)}, u32[]{:S(2)}) collective-permute-start(bf16[768,128]{1,0:T(8,128)(2,1)S(1)} %get-tuple-element.12.a_ref), channel_id=1, source_target_pairs={{0,10},{1,11},{2,8},{3,9},{16,26},{17,27},{18,24},{19,25},{32,42},... | collective-permute-start | bytes 589832 | tf_op jit(solution)/shard_map/ppermute | solution.py:282
  9.5 1.3 %collective-permute-start.2 = (bf16[768,128]{1,0:T(8,128)(2,1)S(1)}, bf16[768,128]{1,0:T(8,128)(2,1)S(1)}, u32[]{:S(2)}, u32[]{:S(2)}) collective-permute-start(bf16[768,128]{1,0:T(8,128)(2,1)S(1)} %get-tuple-element.13), channel_id=1, source_target_pairs={{0,14},{1,15},{2,12},{3,13},{16,30},{17,31},{18,28},{19,29},{32,46... | collective-permute-start | bytes 589832 | tf_op jit(solution)/shard_map/ppermute | solution.py:282
  10.8 1.3 %collective-permute-start = (bf16[768,128]{1,0:T(8,128)(2,1)S(1)}, bf16[768,128]{1,0:T(8,128)(2,1)S(1)}, u32[]{:S(2)}, u32[]{:S(2)}) collective-permute-start(bf16[768,128]{1,0:T(8,128)(2,1)S(1)} %get-tuple-element.13), channel_id=1, source_target_pairs={{0,4},{1,5},{2,6},{3,7},{16,20},{17,21},{18,22},{19,23},{32,36},{3... | collective-permute-start | bytes 589832 | tf_op jit(solution)/shard_map/ppermute | solution.py:282
  12.1 0.9 %collective-permute-done.1.c_ref = bf16[768,128]{1,0:T(8,128)(2,1)S(1)} collective-permute-done((bf16[768,128]{1,0:T(8,128)(2,1)S(1)}, bf16[768,128]{1,0:T(8,128)(2,1)S(1)}, u32[]{:S(2)}, u32[]{:S(2)}) %collective-permute-start.1) | collective-permute-done | bytes 196640 | tf_op jit(solution)/shard_map/ppermute | solution.py:282
  13.1 1.3 %collective-permute-done.2.d_ref = bf16[768,128]{1,0:T(8,128)(2,1)S(1)} collective-permute-done((bf16[768,128]{1,0:T(8,128)(2,1)S(1)}, bf16[768,128]{1,0:T(8,128)(2,1)S(1)}, u32[]{:S(2)}, u32[]{:S(2)}) %collective-permute-start.2) | collective-permute-done | bytes 196640 | tf_op jit(solution)/shard_map/ppermute | solution.py:282
  14.4 2.9 %collective-permute-done.b_ref = bf16[768,128]{1,0:T(8,128)(2,1)S(1)} collective-permute-done((bf16[768,128]{1,0:T(8,128)(2,1)S(1)}, bf16[768,128]{1,0:T(8,128)(2,1)S(1)}, u32[]{:S(2)}, u32[]{:S(2)}) %collective-permute-start) | collective-permute-done | bytes 196640 | tf_op jit(solution)/shard_map/ppermute | solution.py:282
  17.3 0.8 %collective-permute-start.3 = (bf16[768,128]{1,0:T(8,128)(2,1)S(1)}, bf16[768,128]{1,0:T(8,128)(2,1)S(1)}, u32[]{:S(2)}, u32[]{:S(2)}) collective-permute-start(bf16[768,128]{1,0:T(8,128)(2,1)S(1)} %shard_map.39), channel_id=1, source_target_pairs={{0,1},{1,0},{2,3},{3,2},{4,5},{5,4},{6,7},{7,6},{8,9},{9,8},{10,11... | collective-permute-start | bytes 589832 | tf_op jit(solution)/shard_map/ppermute | solution.py:285
  18.1 4.1 %collective-permute-done.3 = bf16[768,128]{1,0:T(8,128)(2,1)S(1)} collective-permute-done((bf16[768,128]{1,0:T(8,128)(2,1)S(1)}, bf16[768,128]{1,0:T(8,128)(2,1)S(1)}, u32[]{:S(2)}, u32[]{:S(2)}) %collective-permute-start.3) | collective-permute-done | bytes 196640 | tf_op jit(solution)/shard_map/ppermute | solution.py:285
  22.3 6.6 %collective-permute-start.7 = (bf16[2,768,128]{2,1,0:T(8,128)(2,1)S(1)}, bf16[2,768,128]{2,1,0:T(8,128)(2,1)S(1)}, u32[]{:S(2)}, u32[]{:S(2)}) collective-permute-start(bf16[2,768,128]{2,1,0:T(8,128)(2,1)S(1)} %pad_maximum_fusion.own_ref), channel_id=1, source_target_pairs={{0,0},{1,32},{2,16},{3,48},{4,8},{5,40},{6,24},{7,56},{8,80},{9,11... | collective-permute-start | bytes 1179656 | tf_op jit(solution)/shard_map/ppermute | solution.py:287
  28.9 1.4 %collective-permute-start.6 = (bf16[2,768,128]{2,1,0:T(8,128)(2,1)S(1)}, bf16[2,768,128]{2,1,0:T(8,128)(2,1)S(1)}, u32[]{:S(2)}, u32[]{:S(2)}) collective-permute-start(bf16[2,768,128]{2,1,0:T(8,128)(2,1)S(1)} %pad_maximum_fusion.own_ref), channel_id=1, source_target_pairs={{0,4},{4,8},{8,12},{12,0},{1,5},{5,9},{9,13},{13,1},{2,6},{6,10},{... | collective-permute-start | bytes 1179656 | tf_op jit(solution)/shard_map/ppermute | solution.py:290
  30.2 1.4 %collective-permute-start.5 = (bf16[2,768,128]{2,1,0:T(8,128)(2,1)S(1)}, bf16[2,768,128]{2,1,0:T(8,128)(2,1)S(1)}, u32[]{:S(2)}, u32[]{:S(2)}) collective-permute-start(bf16[2,768,128]{2,1,0:T(8,128)(2,1)S(1)} %pad_maximum_fusion.own_ref), channel_id=1, source_target_pairs={{4,0},{8,4},{12,8},{0,12},{5,1},{9,5},{13,9},{1,13},{6,2},{10,6},{... | collective-permute-start | bytes 1179656 | tf_op jit(solution)/shard_map/ppermute | solution.py:289
  31.6 0.0 collective-permute-start.4
  31.6 7.8 %collective-permute-done.7.near_ref = bf16[2,768,128]{2,1,0:T(8,128)(2,1)S(1)} collective-permute-done((bf16[2,768,128]{2,1,0:T(8,128)(2,1)S(1)}, bf16[2,768,128]{2,1,0:T(8,128)(2,1)S(1)}, u32[]{:S(2)}, u32[]{:S(2)}) %collective-permute-start.7) | collective-permute-done | bytes 393248 | tf_op jit(solution)/shard_map/ppermute | solution.py:287
  39.4 5.0 %collective-permute-start.8 = (bf16[2,768,128]{2,1,0:T(8,128)(2,1)S(1)}, bf16[2,768,128]{2,1,0:T(8,128)(2,1)S(1)}, u32[]{:S(2)}, u32[]{:S(2)}) collective-permute-start(bf16[2,768,128]{2,1,0:T(8,128)(2,1)S(1)} %collective-permute-done.7.near_ref), channel_id=1, source_target_pairs={{0,16},{16,0},{1,17},{17,1},{2,18},{18,2},{3,19},{19,3},{4,20},{20... | collective-permute-start | bytes 1179656 | tf_op jit(solution)/shard_map/ppermute | solution.py:291
  44.5 0.0 copy-start
  44.5 1.1 %copy-done = s32[384,384]{1,0:T(8,128)S(1)} copy-done((s32[384,384]{1,0:T(8,128)S(1)}, s32[384,384]{1,0:T(8,128)}, u32[]{:S(2)}) %copy-start) | copy-done | bytes 589848
  45.5 0.0 copy-start.1
  45.6 0.9 %copy-done.1 = bf16[256,256]{1,0:T(8,128)(2,1)S(1)} copy-done((bf16[256,256]{1,0:T(8,128)(2,1)S(1)}, bf16[256,256]{1,0:T(8,128)(2,1)}, u32[]{:S(2)}) %copy-start.1) | copy-done | bytes 131096
  46.5 4.0 %shard_map.37 = (bf16[2,2,4,128,256]{4,3,2,1,0:T(8,128)(2,1)S(1)}, bf16[2,4,256,128]{3,2,1,0:T(8,128)(2,1)S(1)}, f32[48,1536]{1,0:T(8,128)S(1)}, bf16[24,2,64,1536]{3,2,1,0:T(8,128)(2,1)S(1)}) custom-call(bf16[24,2,64,1536]{3,2,1,0:T(8,128)(2,1)} %bitcast.7, bf16[256,256]{1,0:T(8,128)(2,1)S(1)} %copy-done.1, s32[384,384]{1,0:T(8,128)S(1)} %copy-done), custom_call_target="tpu_custom_call" | custom-call | bytes 18874368 | tf_op jit(solution)/shard_map/pallas_call | solution.py:156
  50.4 0.0 collective-permute-done.6.prev_ref
  50.4 0.0 collective-permute-done.5.next_ref
  50.5 0.0 collective-permute-done.4.z_ref
  50.5 1.0 %shard_map.40.factor_ref = bf16[2,2,768,256]{3,2,1,0:T(8,128)(2,1)S(1)} custom-call(bf16[2,768,128]{2,1,0:T(8,128)(2,1)S(1)} %pad_maximum_fusion.own_ref, bf16[2,768,128]{2,1,0:T(8,128)(2,1)S(1)} %collective-permute-done.4.z_ref, bf16[2,768,128]{2,1,0:T(8,128)(2,1)S(1)} %collective-permute-done.5.next_ref, ...), custom_call_target="tpu_custom_call" | custom-call | flops 805306368 | bytes 3145728 | tf_op jit(solution)/shard_map/pallas_call | solution.py:228
  51.4 0.0 collective-permute-done.8.far_ref
  51.5 1.0 %shard_map.41.gt_ref = bf16[256,1536]{1,0:T(8,128)(2,1)S(1)} custom-call(bf16[2,768,128]{2,1,0:T(8,128)(2,1)S(1)} %collective-permute-done.7.near_ref, bf16[2,768,128]{2,1,0:T(8,128)(2,1)S(1)} %collective-permute-done.8.far_ref, bf16[2,4,256,128]{3,2,1,0:T(8,128)(2,1)S(1)} %get-tuple-element.15.col_w_ref), custom_call_target="tpu_custom_call" | custom-call | flops 402653184 | bytes 2359296 | tf_op jit(solution)/shard_map/pallas_call | solution.py:194
  52.5 5.2 %shard_map.42 = bf16[24,2,64,1536]{3,2,1,0:T(8,128)(2,1)} custom-call(bf16[24,2,64,1536]{3,2,1,0:T(8,128)(2,1)S(1)} %get-tuple-element.11.front_ref, bf16[2,2,768,256]{3,2,1,0:T(8,128)(2,1)S(1)} %shard_map.40.factor_ref, bf16[256,1536]{1,0:T(8,128)(2,1)S(1)} %shard_map.41.gt_ref, f32[48,1536]{1,0:T(8,128)S(1)} %get-tuple-element.16.mask_ref), custom_call_target="tpu_custom_call" | custom-call | flops 2415919104 | bytes 18874368 | tf_op jit(solution)/shard_map/pallas_call | solution.py:264
  (2 shorter events, 0.1 us)
Async XLA Ops:
  1.4 11.7 %collective-permute-start.1 = (bf16[768,128]{1,0:T(8,128)(2,1)S(1)}, bf16[768,128]{1,0:T(8,128)(2,1)S(1)}, u32[]{:S(2)}, u32[]{:S(2)}) collective-permute-start(bf16[768,128]{1,0:T(8,128)(2,1)S(1)} %get-tuple-element.12.a_ref), channel_id=1, source_target_pairs={{0,10},{1,11},{2,8},{3,9},{16,26},{17,27},{18,24},{19,25},{32,42},... | collective-permute-start | bytes 589832 | tf_op jit(solution)/shard_map/ppermute | solution.py:282
  9.5 4.8 %collective-permute-start.2 = (bf16[768,128]{1,0:T(8,128)(2,1)S(1)}, bf16[768,128]{1,0:T(8,128)(2,1)S(1)}, u32[]{:S(2)}, u32[]{:S(2)}) collective-permute-start(bf16[768,128]{1,0:T(8,128)(2,1)S(1)} %get-tuple-element.13), channel_id=1, source_target_pairs={{0,14},{1,15},{2,12},{3,13},{16,30},{17,31},{18,28},{19,29},{32,46... | collective-permute-start | bytes 589832 | tf_op jit(solution)/shard_map/ppermute | solution.py:282
  10.8 6.4 %collective-permute-start = (bf16[768,128]{1,0:T(8,128)(2,1)S(1)}, bf16[768,128]{1,0:T(8,128)(2,1)S(1)}, u32[]{:S(2)}, u32[]{:S(2)}) collective-permute-start(bf16[768,128]{1,0:T(8,128)(2,1)S(1)} %get-tuple-element.13), channel_id=1, source_target_pairs={{0,4},{1,5},{2,6},{3,7},{16,20},{17,21},{18,22},{19,23},{32,36},{3... | collective-permute-start | bytes 589832 | tf_op jit(solution)/shard_map/ppermute | solution.py:282
  17.3 4.9 %collective-permute-start.3 = (bf16[768,128]{1,0:T(8,128)(2,1)S(1)}, bf16[768,128]{1,0:T(8,128)(2,1)S(1)}, u32[]{:S(2)}, u32[]{:S(2)}) collective-permute-start(bf16[768,128]{1,0:T(8,128)(2,1)S(1)} %shard_map.39), channel_id=1, source_target_pairs={{0,1},{1,0},{2,3},{3,2},{4,5},{5,4},{6,7},{7,6},{8,9},{9,8},{10,11... | collective-permute-start | bytes 589832 | tf_op jit(solution)/shard_map/ppermute | solution.py:285
  22.3 17.2 %collective-permute-start.7 = (bf16[2,768,128]{2,1,0:T(8,128)(2,1)S(1)}, bf16[2,768,128]{2,1,0:T(8,128)(2,1)S(1)}, u32[]{:S(2)}, u32[]{:S(2)}) collective-permute-start(bf16[2,768,128]{2,1,0:T(8,128)(2,1)S(1)} %pad_maximum_fusion.own_ref), channel_id=1, source_target_pairs={{0,0},{1,32},{2,16},{3,48},{4,8},{5,40},{6,24},{7,56},{8,80},{9,11... | collective-permute-start | bytes 1179656 | tf_op jit(solution)/shard_map/ppermute | solution.py:287
  28.9 21.6 %collective-permute-start.6 = (bf16[2,768,128]{2,1,0:T(8,128)(2,1)S(1)}, bf16[2,768,128]{2,1,0:T(8,128)(2,1)S(1)}, u32[]{:S(2)}, u32[]{:S(2)}) collective-permute-start(bf16[2,768,128]{2,1,0:T(8,128)(2,1)S(1)} %pad_maximum_fusion.own_ref), channel_id=1, source_target_pairs={{0,4},{4,8},{8,12},{12,0},{1,5},{5,9},{9,13},{13,1},{2,6},{6,10},{... | collective-permute-start | bytes 1179656 | tf_op jit(solution)/shard_map/ppermute | solution.py:290
  30.2 20.2 %collective-permute-start.5 = (bf16[2,768,128]{2,1,0:T(8,128)(2,1)S(1)}, bf16[2,768,128]{2,1,0:T(8,128)(2,1)S(1)}, u32[]{:S(2)}, u32[]{:S(2)}) collective-permute-start(bf16[2,768,128]{2,1,0:T(8,128)(2,1)S(1)} %pad_maximum_fusion.own_ref), channel_id=1, source_target_pairs={{4,0},{8,4},{12,8},{0,12},{5,1},{9,5},{13,9},{1,13},{6,2},{10,6},{... | collective-permute-start | bytes 1179656 | tf_op jit(solution)/shard_map/ppermute | solution.py:289
  31.6 18.8 %collective-permute-start.4 = (bf16[2,768,128]{2,1,0:T(8,128)(2,1)S(1)}, bf16[2,768,128]{2,1,0:T(8,128)(2,1)S(1)}, u32[]{:S(2)}, u32[]{:S(2)}) collective-permute-start(bf16[2,768,128]{2,1,0:T(8,128)(2,1)S(1)} %pad_maximum_fusion.own_ref), channel_id=1, source_target_pairs={{1,2},{2,1},{3,0},{0,3},{5,6},{6,5},{7,4},{4,7},{9,10},{10,9},{11,... | collective-permute-start | bytes 1179656 | tf_op jit(solution)/shard_map/ppermute | solution.py:288
  39.4 12.0 %collective-permute-start.8 = (bf16[2,768,128]{2,1,0:T(8,128)(2,1)S(1)}, bf16[2,768,128]{2,1,0:T(8,128)(2,1)S(1)}, u32[]{:S(2)}, u32[]{:S(2)}) collective-permute-start(bf16[2,768,128]{2,1,0:T(8,128)(2,1)S(1)} %collective-permute-done.7.near_ref), channel_id=1, source_target_pairs={{0,16},{16,0},{1,17},{17,1},{2,18},{18,2},{3,19},{19,3},{4,20},{20... | collective-permute-start | bytes 1179656 | tf_op jit(solution)/shard_map/ppermute | solution.py:291
  44.5 1.1 %copy-start = (s32[384,384]{1,0:T(8,128)S(1)}, s32[384,384]{1,0:T(8,128)}, u32[]{:S(2)}) copy-start(s32[384,384]{1,0:T(8,128)} %pattern_ref.1) | copy-start | bytes 1769476
  45.5 0.9 %copy-start.1 = (bf16[256,256]{1,0:T(8,128)(2,1)S(1)}, bf16[256,256]{1,0:T(8,128)(2,1)}, u32[]{:S(2)}) copy-start(bf16[256,256]{1,0:T(8,128)(2,1)} %diag_ref.1) | copy-start | bytes 393220

commit v6 on v5

--- a/solution.py
+++ b/solution.py
@@ -274,6 +274,22 @@
     )(front4, factor, columns, mask)
 
 
+def hand_on_kernel(in_ref, after_ref, out_ref):
+    del after_ref
+    out_ref[...] = in_ref[...]
+
+
+def hand_on(message, after):
+    whole = pl.BlockSpec(memory_space=VMEM)
+    return pl.pallas_call(
+        hand_on_kernel,
+        out_shape=jax.ShapeDtypeStruct(message.shape, BF16),
+        in_specs=[whole, pl.BlockSpec(memory_space=pl.ANY)],
+        out_specs=whole,
+        compiler_params=pltpu.CompilerParams(vmem_limit_bytes=8 << 20),
+    )(message, after)
+
+
 def body(front, diag_inverse, fill_pattern):
     front4 = front.reshape(PAIRS, 2, B, COLS)
     even, odd = pack(lax.slice(front, (0, 0), (front.shape[0], 128)).reshape(PAIRS, 2, B, 128))
@@ -288,7 +304,7 @@
     z_pair = lax.ppermute(pair, "z", [(1, 2), (2, 1), (3, 0), (0, 3)])
     y_next = lax.ppermute(pair, "y", [((i + 1) % 4, i) for i in range(4)])
     y_prev = lax.ppermute(pair, "y", [(i, (i + 1) % 4) for i in range(4)])
-    far = lax.ppermute(near, "core", [(0, 1), (1, 0)])
+    far = lax.ppermute(hand_on(near, mask), "core", [(0, 1), (1, 0)])
     factor = row_factor((pair, z_pair, y_next, y_prev), row_w)
     columns = column_factor((near, far), col_w)
     out = update(stay, factor, columns, mask)

time: 57.9 us -> 55.7 us (0.962)
  waiting for transfers between devices: 17.1 us -> 14.5 us
    ppermute x1, waiting for transfers between devices: 7.82 us -> 1.87 us  [body(): near = lax.ppermute(pair, ALL, column_perm())]
    ppermute x1, waiting for transfers between devices: 0.01 us -> 3.23 us  [body(): y_prev = lax.ppermute(pair, 'y', [(i, (i + 1) % 4) for i in range(4)])]
  transfers between devices with their start and end apart: 9 -> 9, of which waited for: 5 -> 7; matrix products, arithmetic and copies ran while one was open for 0% -> 0% of each run, Pallas kernels for 9% -> 9%
where the time goes in v6:
time: 55.7 us; the launch traced here: 55.2 us
  starting transfers between devices  26 us (47%)
  waiting for transfers between devices  14.5 us (26%)
  Pallas kernels  11.4 us (20%)
  local copies, waits for them, and re-layouts  3.15 us (6%)
    ppermute x3, starting transfers between devices, body(): lax.ppermute(part, ALL, spread_perm(k))  10.7 us
    ppermute x1, starting transfers between devices, body(): near = lax.ppermute(pair, ALL, column_perm())  6.61 us
    pallas_call x1, Pallas kernels, update(): pl.pallas_call(update_kernel, grid=(2, 2), out_shape=jax.ShapeDtypeStruct...  5.21 us
    ppermute x3, waiting for transfers between devices, body(): lax.ppermute(part, ALL, spread_perm(k))  5.13 us
    ppermute x1, starting transfers between devices, body(): far = lax.ppermute(hand_on(near, mask), 'core', [(0, 1), (1, 0)])  5.11 us
    ppermute x1, waiting for transfers between devices, body(): mate = lax.ppermute(own, 'z', [(0, 1), (1, 0), (2, 3), (3, 2)])  4.11 us
    pallas_call x1, Pallas kernels, prepare(): pl.pallas_call(prepare_kernel, out_shape=(jax.ShapeDtypeStruct((2, 2, Q,...  3.97 us
    ppermute x1, waiting for transfers between devices, body(): y_prev = lax.ppermute(pair, 'y', [(i, (i + 1) % 4) for i in range(4)])  3.23 us
  transfers between devices with their start and end apart: 9, of which 7 were waited for; matrix products, arithmetic and copies ran while one was open for 0% of the time, Pallas kernels for 9%

profile of v6, /device:TPU:7, one launch (start us, length us, event | category | flops | bytes accessed | tf_op | source)
XLA Modules:
  0.0 55.2 jit_solution(12150125751375530315)
XLA Ops:
  0.0 1.2 %slice.3 = bf16[3072,128]{1,0:T(8,128)(2,1)S(1)} slice(bf16[3072,1536]{1,0:T(8,128)(2,1)} %param.3), slice={[0:3072], [0:128]} | slice | bytes 1572864 | tf_op jit(solution)/shard_map/slice | solution.py:295
  1.2 0.2 shard_map.38
  1.4 8.1 %collective-permute-start.1 = (bf16[768,128]{1,0:T(8,128)(2,1)S(1)}, bf16[768,128]{1,0:T(8,128)(2,1)S(1)}, u32[]{:S(2)}, u32[]{:S(2)}) collective-permute-start(bf16[768,128]{1,0:T(8,128)(2,1)S(1)} %get-tuple-element.12.a_ref), channel_id=1, source_target_pairs={{0,10},{1,11},{2,8},{3,9},{16,26},{17,27},{18,24},{19,25},{32,42},... | collective-permute-start | bytes 589832 | tf_op jit(solution)/shard_map/ppermute | solution.py:298
  9.5 1.3 %collective-permute-start.2 = (bf16[768,128]{1,0:T(8,128)(2,1)S(1)}, bf16[768,128]{1,0:T(8,128)(2,1)S(1)}, u32[]{:S(2)}, u32[]{:S(2)}) collective-permute-start(bf16[768,128]{1,0:T(8,128)(2,1)S(1)} %get-tuple-element.13), channel_id=1, source_target_pairs={{0,14},{1,15},{2,12},{3,13},{16,30},{17,31},{18,28},{19,29},{32,46... | collective-permute-start | bytes 589832 | tf_op jit(solution)/shard_map/ppermute | solution.py:298
  10.8 1.3 %collective-permute-start = (bf16[768,128]{1,0:T(8,128)(2,1)S(1)}, bf16[768,128]{1,0:T(8,128)(2,1)S(1)}, u32[]{:S(2)}, u32[]{:S(2)}) collective-permute-start(bf16[768,128]{1,0:T(8,128)(2,1)S(1)} %get-tuple-element.13), channel_id=1, source_target_pairs={{0,4},{1,5},{2,6},{3,7},{16,20},{17,21},{18,22},{19,23},{32,36},{3... | collective-permute-start | bytes 589832 | tf_op jit(solution)/shard_map/ppermute | solution.py:298
  12.1 0.9 %collective-permute-done.1.c_ref = bf16[768,128]{1,0:T(8,128)(2,1)S(1)} collective-permute-done((bf16[768,128]{1,0:T(8,128)(2,1)S(1)}, bf16[768,128]{1,0:T(8,128)(2,1)S(1)}, u32[]{:S(2)}, u32[]{:S(2)}) %collective-permute-start.1) | collective-permute-done | bytes 196640 | tf_op jit(solution)/shard_map/ppermute | solution.py:298
  13.1 1.3 %collective-permute-done.2.d_ref = bf16[768,128]{1,0:T(8,128)(2,1)S(1)} collective-permute-done((bf16[768,128]{1,0:T(8,128)(2,1)S(1)}, bf16[768,128]{1,0:T(8,128)(2,1)S(1)}, u32[]{:S(2)}, u32[]{:S(2)}) %collective-permute-start.2) | collective-permute-done | bytes 196640 | tf_op jit(solution)/shard_map/ppermute | solution.py:298
  14.4 2.9 %collective-permute-done.b_ref = bf16[768,128]{1,0:T(8,128)(2,1)S(1)} collective-permute-done((bf16[768,128]{1,0:T(8,128)(2,1)S(1)}, bf16[768,128]{1,0:T(8,128)(2,1)S(1)}, u32[]{:S(2)}, u32[]{:S(2)}) %collective-permute-start) | collective-permute-done | bytes 196640 | tf_op jit(solution)/shard_map/ppermute | solution.py:298
  17.3 0.8 %collective-permute-start.3 = (bf16[768,128]{1,0:T(8,128)(2,1)S(1)}, bf16[768,128]{1,0:T(8,128)(2,1)S(1)}, u32[]{:S(2)}, u32[]{:S(2)}) collective-permute-start(bf16[768,128]{1,0:T(8,128)(2,1)S(1)} %shard_map.39), channel_id=1, source_target_pairs={{0,1},{1,0},{2,3},{3,2},{4,5},{5,4},{6,7},{7,6},{8,9},{9,8},{10,11... | collective-permute-start | bytes 589832 | tf_op jit(solution)/shard_map/ppermute | solution.py:301
  18.1 4.1 %collective-permute-done.3 = bf16[768,128]{1,0:T(8,128)(2,1)S(1)} collective-permute-done((bf16[768,128]{1,0:T(8,128)(2,1)S(1)}, bf16[768,128]{1,0:T(8,128)(2,1)S(1)}, u32[]{:S(2)}, u32[]{:S(2)}) %collective-permute-start.3) | collective-permute-done | bytes 196640 | tf_op jit(solution)/shard_map/ppermute | solution.py:301
  22.3 6.6 %collective-permute-start.7 = (bf16[2,768,128]{2,1,0:T(8,128)(2,1)S(1)}, bf16[2,768,128]{2,1,0:T(8,128)(2,1)S(1)}, u32[]{:S(2)}, u32[]{:S(2)}) collective-permute-start(bf16[2,768,128]{2,1,0:T(8,128)(2,1)S(1)} %pad_maximum_fusion.own_ref), channel_id=1, source_target_pairs={{0,0},{1,32},{2,16},{3,48},{4,8},{5,40},{6,24},{7,56},{8,80},{9,11... | collective-permute-start | bytes 1179656 | tf_op jit(solution)/shard_map/ppermute | solution.py:303
  28.9 1.4 %collective-permute-start.6 = (bf16[2,768,128]{2,1,0:T(8,128)(2,1)S(1)}, bf16[2,768,128]{2,1,0:T(8,128)(2,1)S(1)}, u32[]{:S(2)}, u32[]{:S(2)}) collective-permute-start(bf16[2,768,128]{2,1,0:T(8,128)(2,1)S(1)} %pad_maximum_fusion.own_ref), channel_id=1, source_target_pairs={{0,4},{4,8},{8,12},{12,0},{1,5},{5,9},{9,13},{13,1},{2,6},{6,10},{... | collective-permute-start | bytes 1179656 | tf_op jit(solution)/shard_map/ppermute | solution.py:306
  30.2 1.4 %collective-permute-start.5 = (bf16[2,768,128]{2,1,0:T(8,128)(2,1)S(1)}, bf16[2,768,128]{2,1,0:T(8,128)(2,1)S(1)}, u32[]{:S(2)}, u32[]{:S(2)}) collective-permute-start(bf16[2,768,128]{2,1,0:T(8,128)(2,1)S(1)} %pad_maximum_fusion.own_ref), channel_id=1, source_target_pairs={{4,0},{8,4},{12,8},{0,12},{5,1},{9,5},{13,9},{1,13},{6,2},{10,6},{... | collective-permute-start | bytes 1179656 | tf_op jit(solution)/shard_map/ppermute | solution.py:305
  31.6 0.0 collective-permute-start.4
  31.6 0.0 copy-start
  31.6 1.1 %copy-done = s32[384,384]{1,0:T(8,128)S(1)} copy-done((s32[384,384]{1,0:T(8,128)S(1)}, s32[384,384]{1,0:T(8,128)}, u32[]{:S(2)}) %copy-start) | copy-done | bytes 589848
  32.7 0.0 copy-start.1
  32.7 0.9 %copy-done.1 = bf16[256,256]{1,0:T(8,128)(2,1)S(1)} copy-done((bf16[256,256]{1,0:T(8,128)(2,1)S(1)}, bf16[256,256]{1,0:T(8,128)(2,1)}, u32[]{:S(2)}) %copy-start.1) | copy-done | bytes 131096
  33.6 4.0 %shard_map.37 = (bf16[2,2,4,128,256]{4,3,2,1,0:T(8,128)(2,1)S(1)}, bf16[2,4,256,128]{3,2,1,0:T(8,128)(2,1)S(1)}, f32[48,1536]{1,0:T(8,128)S(1)}, bf16[24,2,64,1536]{3,2,1,0:T(8,128)(2,1)S(1)}) custom-call(bf16[24,2,64,1536]{3,2,1,0:T(8,128)(2,1)} %bitcast.7, bf16[256,256]{1,0:T(8,128)(2,1)S(1)} %copy-done.1, s32[384,384]{1,0:T(8,128)S(1)} %copy-done), custom_call_target="tpu_custom_call" | custom-call | bytes 18874368 | tf_op jit(solution)/shard_map/pallas_call | solution.py:156
  37.6 1.9 %collective-permute-done.7.in_ref.near_ref = bf16[2,768,128]{2,1,0:T(8,128)(2,1)S(1)} collective-permute-done((bf16[2,768,128]{2,1,0:T(8,128)(2,1)S(1)}, bf16[2,768,128]{2,1,0:T(8,128)(2,1)S(1)}, u32[]{:S(2)}, u32[]{:S(2)}) %collective-permute-start.7) | collective-permute-done | bytes 393248 | tf_op jit(solution)/shard_map/ppermute | solution.py:303
  39.5 5.1 %collective-permute-start.8 = (bf16[2,768,128]{2,1,0:T(8,128)(2,1)S(1)}, bf16[2,768,128]{2,1,0:T(8,128)(2,1)S(1)}, u32[]{:S(2)}, u32[]{:S(2)}) collective-permute-start(bf16[2,768,128]{2,1,0:T(8,128)(2,1)S(1)} %shard_map.41), channel_id=1, source_target_pairs={{0,16},{16,0},{1,17},{17,1},{2,18},{18,2},{3,19},{19,3},{4,20},{20... | collective-permute-start | bytes 1179656 | tf_op jit(solution)/shard_map/ppermute | solution.py:307
  44.6 3.2 %collective-permute-done.6.prev_ref = bf16[2,768,128]{2,1,0:T(8,128)(2,1)S(1)} collective-permute-done((bf16[2,768,128]{2,1,0:T(8,128)(2,1)S(1)}, bf16[2,768,128]{2,1,0:T(8,128)(2,1)S(1)}, u32[]{:S(2)}, u32[]{:S(2)}) %collective-permute-start.6) | collective-permute-done | bytes 393248 | tf_op jit(solution)/shard_map/ppermute | solution.py:306
  47.8 0.1 collective-permute-done.5.next_ref
  48.0 0.0 collective-permute-done.4.z_ref
  48.0 1.0 %shard_map.40.factor_ref = bf16[2,2,768,256]{3,2,1,0:T(8,128)(2,1)S(1)} custom-call(bf16[2,768,128]{2,1,0:T(8,128)(2,1)S(1)} %pad_maximum_fusion.own_ref, bf16[2,768,128]{2,1,0:T(8,128)(2,1)S(1)} %collective-permute-done.4.z_ref, bf16[2,768,128]{2,1,0:T(8,128)(2,1)S(1)} %collective-permute-done.5.next_ref, ...), custom_call_target="tpu_custom_call" | custom-call | flops 805306368 | bytes 3145728 | tf_op jit(solution)/shard_map/pallas_call | solution.py:228
  48.9 0.0 collective-permute-done.8.far_ref
  49.0 1.0 %shard_map.42.gt_ref = bf16[256,1536]{1,0:T(8,128)(2,1)S(1)} custom-call(bf16[2,768,128]{2,1,0:T(8,128)(2,1)S(1)} %collective-permute-done.7.in_ref.near_ref, bf16[2,768,128]{2,1,0:T(8,128)(2,1)S(1)} %collective-permute-done.8.far_ref, bf16[2,4,256,128]{3,2,1,0:T(8,128)(2,1)S(1)} %get-tuple-element.16.col_w_ref), custom_call_target="tpu_custom_call" | custom-call | flops 402653184 | bytes 2359296 | tf_op jit(solution)/shard_map/pallas_call | solution.py:194
  49.9 5.2 %shard_map.43 = bf16[24,2,64,1536]{3,2,1,0:T(8,128)(2,1)} custom-call(bf16[24,2,64,1536]{3,2,1,0:T(8,128)(2,1)S(1)} %get-tuple-element.11.front_ref, bf16[2,2,768,256]{3,2,1,0:T(8,128)(2,1)S(1)} %shard_map.40.factor_ref, bf16[256,1536]{1,0:T(8,128)(2,1)S(1)} %shard_map.42.gt_ref, f32[48,1536]{1,0:T(8,128)S(1)} %get-tuple-element.15.after_ref.mask_ref), custom_call_target="tpu_custom_call" | custom-call | flops 2415919104 | bytes 18874368 | tf_op jit(solution)/shard_map/pallas_call | solution.py:264
  (3 shorter events, 0.1 us)
Async XLA Ops:
  1.4 11.7 %collective-permute-start.1 = (bf16[768,128]{1,0:T(8,128)(2,1)S(1)}, bf16[768,128]{1,0:T(8,128)(2,1)S(1)}, u32[]{:S(2)}, u32[]{:S(2)}) collective-permute-start(bf16[768,128]{1,0:T(8,128)(2,1)S(1)} %get-tuple-element.12.a_ref), channel_id=1, source_target_pairs={{0,10},{1,11},{2,8},{3,9},{16,26},{17,27},{18,24},{19,25},{32,42},... | collective-permute-start | bytes 589832 | tf_op jit(solution)/shard_map/ppermute | solution.py:298
  9.5 4.8 %collective-permute-start.2 = (bf16[768,128]{1,0:T(8,128)(2,1)S(1)}, bf16[768,128]{1,0:T(8,128)(2,1)S(1)}, u32[]{:S(2)}, u32[]{:S(2)}) collective-permute-start(bf16[768,128]{1,0:T(8,128)(2,1)S(1)} %get-tuple-element.13), channel_id=1, source_target_pairs={{0,14},{1,15},{2,12},{3,13},{16,30},{17,31},{18,28},{19,29},{32,46... | collective-permute-start | bytes 589832 | tf_op jit(solution)/shard_map/ppermute | solution.py:298
  10.8 6.4 %collective-permute-start = (bf16[768,128]{1,0:T(8,128)(2,1)S(1)}, bf16[768,128]{1,0:T(8,128)(2,1)S(1)}, u32[]{:S(2)}, u32[]{:S(2)}) collective-permute-start(bf16[768,128]{1,0:T(8,128)(2,1)S(1)} %get-tuple-element.13), channel_id=1, source_target_pairs={{0,4},{1,5},{2,6},{3,7},{16,20},{17,21},{18,22},{19,23},{32,36},{3... | collective-permute-start | bytes 589832 | tf_op jit(solution)/shard_map/ppermute | solution.py:298
  17.3 4.9 %collective-permute-start.3 = (bf16[768,128]{1,0:T(8,128)(2,1)S(1)}, bf16[768,128]{1,0:T(8,128)(2,1)S(1)}, u32[]{:S(2)}, u32[]{:S(2)}) collective-permute-start(bf16[768,128]{1,0:T(8,128)(2,1)S(1)} %shard_map.39), channel_id=1, source_target_pairs={{0,1},{1,0},{2,3},{3,2},{4,5},{5,4},{6,7},{7,6},{8,9},{9,8},{10,11... | collective-permute-start | bytes 589832 | tf_op jit(solution)/shard_map/ppermute | solution.py:301
  22.3 17.2 %collective-permute-start.7 = (bf16[2,768,128]{2,1,0:T(8,128)(2,1)S(1)}, bf16[2,768,128]{2,1,0:T(8,128)(2,1)S(1)}, u32[]{:S(2)}, u32[]{:S(2)}) collective-permute-start(bf16[2,768,128]{2,1,0:T(8,128)(2,1)S(1)} %pad_maximum_fusion.own_ref), channel_id=1, source_target_pairs={{0,0},{1,32},{2,16},{3,48},{4,8},{5,40},{6,24},{7,56},{8,80},{9,11... | collective-permute-start | bytes 1179656 | tf_op jit(solution)/shard_map/ppermute | solution.py:303
  28.9 18.9 %collective-permute-start.6 = (bf16[2,768,128]{2,1,0:T(8,128)(2,1)S(1)}, bf16[2,768,128]{2,1,0:T(8,128)(2,1)S(1)}, u32[]{:S(2)}, u32[]{:S(2)}) collective-permute-start(bf16[2,768,128]{2,1,0:T(8,128)(2,1)S(1)} %pad_maximum_fusion.own_ref), channel_id=1, source_target_pairs={{0,4},{4,8},{8,12},{12,0},{1,5},{5,9},{9,13},{13,1},{2,6},{6,10},{... | collective-permute-start | bytes 1179656 | tf_op jit(solution)/shard_map/ppermute | solution.py:306
  30.2 17.7 %collective-permute-start.5 = (bf16[2,768,128]{2,1,0:T(8,128)(2,1)S(1)}, bf16[2,768,128]{2,1,0:T(8,128)(2,1)S(1)}, u32[]{:S(2)}, u32[]{:S(2)}) collective-permute-start(bf16[2,768,128]{2,1,0:T(8,128)(2,1)S(1)} %pad_maximum_fusion.own_ref), channel_id=1, source_target_pairs={{4,0},{8,4},{12,8},{0,12},{5,1},{9,5},{13,9},{1,13},{6,2},{10,6},{... | collective-permute-start | bytes 1179656 | tf_op jit(solution)/shard_map/ppermute | solution.py:305
  31.6 16.3 %collective-permute-start.4 = (bf16[2,768,128]{2,1,0:T(8,128)(2,1)S(1)}, bf16[2,768,128]{2,1,0:T(8,128)(2,1)S(1)}, u32[]{:S(2)}, u32[]{:S(2)}) collective-permute-start(bf16[2,768,128]{2,1,0:T(8,128)(2,1)S(1)} %pad_maximum_fusion.own_ref), channel_id=1, source_target_pairs={{1,2},{2,1},{3,0},{0,3},{5,6},{6,5},{7,4},{4,7},{9,10},{10,9},{11,... | collective-permute-start | bytes 1179656 | tf_op jit(solution)/shard_map/ppermute | solution.py:304
  31.6 1.1 %copy-start = (s32[384,384]{1,0:T(8,128)S(1)}, s32[384,384]{1,0:T(8,128)}, u32[]{:S(2)}) copy-start(s32[384,384]{1,0:T(8,128)} %pattern_ref.1) | copy-start | bytes 1769476
  32.7 0.9 %copy-start.1 = (bf16[256,256]{1,0:T(8,128)(2,1)S(1)}, bf16[256,256]{1,0:T(8,128)(2,1)}, u32[]{:S(2)}) copy-start(bf16[256,256]{1,0:T(8,128)(2,1)} %diag_ref.1) | copy-start | bytes 393220
  39.5 9.5 %collective-permute-start.8 = (bf16[2,768,128]{2,1,0:T(8,128)(2,1)S(1)}, bf16[2,768,128]{2,1,0:T(8,128)(2,1)S(1)}, u32[]{:S(2)}, u32[]{:S(2)}) collective-permute-start(bf16[2,768,128]{2,1,0:T(8,128)(2,1)S(1)} %shard_map.41), channel_id=1, source_target_pairs={{0,16},{16,0},{1,17},{17,1},{2,18},{18,2},{3,19},{19,3},{4,20},{20... | collective-permute-start | bytes 1179656 | tf_op jit(solution)/shard_map/ppermute | solution.py:307

commit v7 on v6

--- a/solution.py
+++ b/solution.py
@@ -45,7 +45,7 @@
             r = 2 * x + core
             for y in range(4):
                 for z in range(4):
-                    to_x = (x + 2 * (y // 2) + z % 2) % 4
+                    to_x = (x - 2 * (y // 2) - z % 2) % 4
                     target = linear(to_x, quarter_of(y, z) // 2, 2 * (y % 2) + r // 4, r % 4)
                     pairs.append((linear(x, core, y, z), target))
     return pairs

time: 55.7 us -> 55.7 us (level)
  starting transfers between devices: 26 us -> 21.8 us
  waiting for transfers between devices: 14.5 us -> 18.7 us
    ppermute x1, waiting for transfers between devices: 3.23 us -> 8 us  [body(): y_prev = lax.ppermute(pair, 'y', [(i, (i + 1) % 4) for i in range(4)])]
    ppermute x1, starting transfers between devices: 5.11 us -> 0.9 us  [body(): far = lax.ppermute(hand_on(near, mask), 'core', [(0, 1), (1, 0)])]
    ppermute x1, waiting for transfers between devices: 1.87 us -> 1.31 us  [body(): near = lax.ppermute(pair, ALL, column_perm())]
where the time goes in v7:
time: 55.7 us; the launch traced here: 55.2 us
  starting transfers between devices  21.8 us (39%)
  waiting for transfers between devices  18.7 us (34%)
  Pallas kernels  11.4 us (20%)
  local copies, waits for them, and re-layouts  3.15 us (6%)
    ppermute x3, starting transfers between devices, body(): lax.ppermute(part, ALL, spread_perm(k))  10.7 us
    ppermute x1, waiting for transfers between devices, body(): y_prev = lax.ppermute(pair, 'y', [(i, (i + 1) % 4) for i in range(4)])  8 us
    ppermute x1, starting transfers between devices, body(): near = lax.ppermute(pair, ALL, column_perm())  6.61 us
    pallas_call x1, Pallas kernels, update(): pl.pallas_call(update_kernel, grid=(2, 2), out_shape=jax.ShapeDtypeStruct...  5.21 us
    ppermute x3, waiting for transfers between devices, body(): lax.ppermute(part, ALL, spread_perm(k))  5.13 us
    ppermute x1, waiting for transfers between devices, body(): mate = lax.ppermute(own, 'z', [(0, 1), (1, 0), (2, 3), (3, 2)])  4.11 us
    pallas_call x1, Pallas kernels, prepare(): pl.pallas_call(prepare_kernel, out_shape=(jax.ShapeDtypeStruct((2, 2, Q,...  3.97 us
    unnamed x4, local copies, waits for them, and re-layouts  1.97 us
  transfers between devices with their start and end apart: 9, of which 7 were waited for; matrix products, arithmetic and copies ran while one was open for 0% of the time, Pallas kernels for 9%

profile of v7, /device:TPU:7, one launch (start us, length us, event | category | flops | bytes accessed | tf_op | source)
XLA Modules:
  0.0 55.2 jit_solution(14804787640633002803)
XLA Ops:
  0.0 1.2 %slice.3 = bf16[3072,128]{1,0:T(8,128)(2,1)S(1)} slice(bf16[3072,1536]{1,0:T(8,128)(2,1)} %param.3), slice={[0:3072], [0:128]} | slice | bytes 1572864 | tf_op jit(solution)/shard_map/slice | solution.py:295
  1.2 0.2 shard_map.38
  1.4 8.1 %collective-permute-start.1 = (bf16[768,128]{1,0:T(8,128)(2,1)S(1)}, bf16[768,128]{1,0:T(8,128)(2,1)S(1)}, u32[]{:S(2)}, u32[]{:S(2)}) collective-permute-start(bf16[768,128]{1,0:T(8,128)(2,1)S(1)} %get-tuple-element.12.a_ref), channel_id=1, source_target_pairs={{0,10},{1,11},{2,8},{3,9},{16,26},{17,27},{18,24},{19,25},{32,42},... | collective-permute-start | bytes 589832 | tf_op jit(solution)/shard_map/ppermute | solution.py:298
  9.5 1.3 %collective-permute-start.2 = (bf16[768,128]{1,0:T(8,128)(2,1)S(1)}, bf16[768,128]{1,0:T(8,128)(2,1)S(1)}, u32[]{:S(2)}, u32[]{:S(2)}) collective-permute-start(bf16[768,128]{1,0:T(8,128)(2,1)S(1)} %get-tuple-element.13), channel_id=1, source_target_pairs={{0,14},{1,15},{2,12},{3,13},{16,30},{17,31},{18,28},{19,29},{32,46... | collective-permute-start | bytes 589832 | tf_op jit(solution)/shard_map/ppermute | solution.py:298
  10.8 1.3 %collective-permute-start = (bf16[768,128]{1,0:T(8,128)(2,1)S(1)}, bf16[768,128]{1,0:T(8,128)(2,1)S(1)}, u32[]{:S(2)}, u32[]{:S(2)}) collective-permute-start(bf16[768,128]{1,0:T(8,128)(2,1)S(1)} %get-tuple-element.13), channel_id=1, source_target_pairs={{0,4},{1,5},{2,6},{3,7},{16,20},{17,21},{18,22},{19,23},{32,36},{3... | collective-permute-start | bytes 589832 | tf_op jit(solution)/shard_map/ppermute | solution.py:298
  12.1 0.9 %collective-permute-done.1.c_ref = bf16[768,128]{1,0:T(8,128)(2,1)S(1)} collective-permute-done((bf16[768,128]{1,0:T(8,128)(2,1)S(1)}, bf16[768,128]{1,0:T(8,128)(2,1)S(1)}, u32[]{:S(2)}, u32[]{:S(2)}) %collective-permute-start.1) | collective-permute-done | bytes 196640 | tf_op jit(solution)/shard_map/ppermute | solution.py:298
  13.1 1.3 %collective-permute-done.2.d_ref = bf16[768,128]{1,0:T(8,128)(2,1)S(1)} collective-permute-done((bf16[768,128]{1,0:T(8,128)(2,1)S(1)}, bf16[768,128]{1,0:T(8,128)(2,1)S(1)}, u32[]{:S(2)}, u32[]{:S(2)}) %collective-permute-start.2) | collective-permute-done | bytes 196640 | tf_op jit(solution)/shard_map/ppermute | solution.py:298
  14.4 2.9 %collective-permute-done.b_ref = bf16[768,128]{1,0:T(8,128)(2,1)S(1)} collective-permute-done((bf16[768,128]{1,0:T(8,128)(2,1)S(1)}, bf16[768,128]{1,0:T(8,128)(2,1)S(1)}, u32[]{:S(2)}, u32[]{:S(2)}) %collective-permute-start) | collective-permute-done | bytes 196640 | tf_op jit(solution)/shard_map/ppermute | solution.py:298
  17.3 0.8 %collective-permute-start.3 = (bf16[768,128]{1,0:T(8,128)(2,1)S(1)}, bf16[768,128]{1,0:T(8,128)(2,1)S(1)}, u32[]{:S(2)}, u32[]{:S(2)}) collective-permute-start(bf16[768,128]{1,0:T(8,128)(2,1)S(1)} %shard_map.39), channel_id=1, source_target_pairs={{0,1},{1,0},{2,3},{3,2},{4,5},{5,4},{6,7},{7,6},{8,9},{9,8},{10,11... | collective-permute-start | bytes 589832 | tf_op jit(solution)/shard_map/ppermute | solution.py:301
  18.1 4.1 %collective-permute-done.3 = bf16[768,128]{1,0:T(8,128)(2,1)S(1)} collective-permute-done((bf16[768,128]{1,0:T(8,128)(2,1)S(1)}, bf16[768,128]{1,0:T(8,128)(2,1)S(1)}, u32[]{:S(2)}, u32[]{:S(2)}) %collective-permute-start.3) | collective-permute-done | bytes 196640 | tf_op jit(solution)/shard_map/ppermute | solution.py:301
  22.3 6.6 %collective-permute-start.7 = (bf16[2,768,128]{2,1,0:T(8,128)(2,1)S(1)}, bf16[2,768,128]{2,1,0:T(8,128)(2,1)S(1)}, u32[]{:S(2)}, u32[]{:S(2)}) collective-permute-start(bf16[2,768,128]{2,1,0:T(8,128)(2,1)S(1)} %pad_maximum_fusion.own_ref), channel_id=1, source_target_pairs={{0,0},{1,96},{2,16},{3,112},{4,8},{5,104},{6,24},{7,120},{8,80},{9... | collective-permute-start | bytes 1179656 | tf_op jit(solution)/shard_map/ppermute | solution.py:303
  28.9 1.4 %collective-permute-start.6 = (bf16[2,768,128]{2,1,0:T(8,128)(2,1)S(1)}, bf16[2,768,128]{2,1,0:T(8,128)(2,1)S(1)}, u32[]{:S(2)}, u32[]{:S(2)}) collective-permute-start(bf16[2,768,128]{2,1,0:T(8,128)(2,1)S(1)} %pad_maximum_fusion.own_ref), channel_id=1, source_target_pairs={{0,4},{4,8},{8,12},{12,0},{1,5},{5,9},{9,13},{13,1},{2,6},{6,10},{... | collective-permute-start | bytes 1179656 | tf_op jit(solution)/shard_map/ppermute | solution.py:306
  30.2 1.4 %collective-permute-start.5 = (bf16[2,768,128]{2,1,0:T(8,128)(2,1)S(1)}, bf16[2,768,128]{2,1,0:T(8,128)(2,1)S(1)}, u32[]{:S(2)}, u32[]{:S(2)}) collective-permute-start(bf16[2,768,128]{2,1,0:T(8,128)(2,1)S(1)} %pad_maximum_fusion.own_ref), channel_id=1, source_target_pairs={{4,0},{8,4},{12,8},{0,12},{5,1},{9,5},{13,9},{1,13},{6,2},{10,6},{... | collective-permute-start | bytes 1179656 | tf_op jit(solution)/shard_map/ppermute | solution.py:305
  31.6 0.0 collective-permute-start.4
  31.6 0.0 copy-start
  31.6 1.1 %copy-done = s32[384,384]{1,0:T(8,128)S(1)} copy-done((s32[384,384]{1,0:T(8,128)S(1)}, s32[384,384]{1,0:T(8,128)}, u32[]{:S(2)}) %copy-start) | copy-done | bytes 589848
  32.7 0.0 copy-start.1
  32.7 0.9 %copy-done.1 = bf16[256,256]{1,0:T(8,128)(2,1)S(1)} copy-done((bf16[256,256]{1,0:T(8,128)(2,1)S(1)}, bf16[256,256]{1,0:T(8,128)(2,1)}, u32[]{:S(2)}) %copy-start.1) | copy-done | bytes 131096
  33.6 4.0 %shard_map.37 = (bf16[2,2,4,128,256]{4,3,2,1,0:T(8,128)(2,1)S(1)}, bf16[2,4,256,128]{3,2,1,0:T(8,128)(2,1)S(1)}, f32[48,1536]{1,0:T(8,128)S(1)}, bf16[24,2,64,1536]{3,2,1,0:T(8,128)(2,1)S(1)}) custom-call(bf16[24,2,64,1536]{3,2,1,0:T(8,128)(2,1)} %bitcast.7, bf16[256,256]{1,0:T(8,128)(2,1)S(1)} %copy-done.1, s32[384,384]{1,0:T(8,128)S(1)} %copy-done), custom_call_target="tpu_custom_call" | custom-call | bytes 18874368 | tf_op jit(solution)/shard_map/pallas_call | solution.py:156
  37.6 1.3 %collective-permute-done.7.in_ref.near_ref = bf16[2,768,128]{2,1,0:T(8,128)(2,1)S(1)} collective-permute-done((bf16[2,768,128]{2,1,0:T(8,128)(2,1)S(1)}, bf16[2,768,128]{2,1,0:T(8,128)(2,1)S(1)}, u32[]{:S(2)}, u32[]{:S(2)}) %collective-permute-start.7) | collective-permute-done | bytes 393248 | tf_op jit(solution)/shard_map/ppermute | solution.py:303
  38.9 0.9 %collective-permute-start.8 = (bf16[2,768,128]{2,1,0:T(8,128)(2,1)S(1)}, bf16[2,768,128]{2,1,0:T(8,128)(2,1)S(1)}, u32[]{:S(2)}, u32[]{:S(2)}) collective-permute-start(bf16[2,768,128]{2,1,0:T(8,128)(2,1)S(1)} %shard_map.41), channel_id=1, source_target_pairs={{0,16},{16,0},{1,17},{17,1},{2,18},{18,2},{3,19},{19,3},{4,20},{20... | collective-permute-start | bytes 1179656 | tf_op jit(solution)/shard_map/ppermute | solution.py:307
  39.8 8.0 %collective-permute-done.6.prev_ref = bf16[2,768,128]{2,1,0:T(8,128)(2,1)S(1)} collective-permute-done((bf16[2,768,128]{2,1,0:T(8,128)(2,1)S(1)}, bf16[2,768,128]{2,1,0:T(8,128)(2,1)S(1)}, u32[]{:S(2)}, u32[]{:S(2)}) %collective-permute-start.6) | collective-permute-done | bytes 393248 | tf_op jit(solution)/shard_map/ppermute | solution.py:306
  47.8 0.1 collective-permute-done.5.next_ref
  48.0 0.0 collective-permute-done.4.z_ref
  48.0 1.0 %shard_map.40.factor_ref = bf16[2,2,768,256]{3,2,1,0:T(8,128)(2,1)S(1)} custom-call(bf16[2,768,128]{2,1,0:T(8,128)(2,1)S(1)} %pad_maximum_fusion.own_ref, bf16[2,768,128]{2,1,0:T(8,128)(2,1)S(1)} %collective-permute-done.4.z_ref, bf16[2,768,128]{2,1,0:T(8,128)(2,1)S(1)} %collective-permute-done.5.next_ref, ...), custom_call_target="tpu_custom_call" | custom-call | flops 805306368 | bytes 3145728 | tf_op jit(solution)/shard_map/pallas_call | solution.py:228
  48.9 0.0 collective-permute-done.8.far_ref
  49.0 1.0 %shard_map.42.gt_ref = bf16[256,1536]{1,0:T(8,128)(2,1)S(1)} custom-call(bf16[2,768,128]{2,1,0:T(8,128)(2,1)S(1)} %collective-permute-done.7.in_ref.near_ref, bf16[2,768,128]{2,1,0:T(8,128)(2,1)S(1)} %collective-permute-done.8.far_ref, bf16[2,4,256,128]{3,2,1,0:T(8,128)(2,1)S(1)} %get-tuple-element.16.col_w_ref), custom_call_target="tpu_custom_call" | custom-call | flops 402653184 | bytes 2359296 | tf_op jit(solution)/shard_map/pallas_call | solution.py:194
  49.9 5.2 %shard_map.43 = bf16[24,2,64,1536]{3,2,1,0:T(8,128)(2,1)} custom-call(bf16[24,2,64,1536]{3,2,1,0:T(8,128)(2,1)S(1)} %get-tuple-element.11.front_ref, bf16[2,2,768,256]{3,2,1,0:T(8,128)(2,1)S(1)} %shard_map.40.factor_ref, bf16[256,1536]{1,0:T(8,128)(2,1)S(1)} %shard_map.42.gt_ref, f32[48,1536]{1,0:T(8,128)S(1)} %get-tuple-element.15.after_ref.mask_ref), custom_call_target="tpu_custom_call" | custom-call | flops 2415919104 | bytes 18874368 | tf_op jit(solution)/shard_map/pallas_call | solution.py:264
  (3 shorter events, 0.1 us)
Async XLA Ops:
  1.4 11.7 %collective-permute-start.1 = (bf16[768,128]{1,0:T(8,128)(2,1)S(1)}, bf16[768,128]{1,0:T(8,128)(2,1)S(1)}, u32[]{:S(2)}, u32[]{:S(2)}) collective-permute-start(bf16[768,128]{1,0:T(8,128)(2,1)S(1)} %get-tuple-element.12.a_ref), channel_id=1, source_target_pairs={{0,10},{1,11},{2,8},{3,9},{16,26},{17,27},{18,24},{19,25},{32,42},... | collective-permute-start | bytes 589832 | tf_op jit(solution)/shard_map/ppermute | solution.py:298
  9.5 4.8 %collective-permute-start.2 = (bf16[768,128]{1,0:T(8,128)(2,1)S(1)}, bf16[768,128]{1,0:T(8,128)(2,1)S(1)}, u32[]{:S(2)}, u32[]{:S(2)}) collective-permute-start(bf16[768,128]{1,0:T(8,128)(2,1)S(1)} %get-tuple-element.13), channel_id=1, source_target_pairs={{0,14},{1,15},{2,12},{3,13},{16,30},{17,31},{18,28},{19,29},{32,46... | collective-permute-start | bytes 589832 | tf_op jit(solution)/shard_map/ppermute | solution.py:298
  10.8 6.4 %collective-permute-start = (bf16[768,128]{1,0:T(8,128)(2,1)S(1)}, bf16[768,128]{1,0:T(8,128)(2,1)S(1)}, u32[]{:S(2)}, u32[]{:S(2)}) collective-permute-start(bf16[768,128]{1,0:T(8,128)(2,1)S(1)} %get-tuple-element.13), channel_id=1, source_target_pairs={{0,4},{1,5},{2,6},{3,7},{16,20},{17,21},{18,22},{19,23},{32,36},{3... | collective-permute-start | bytes 589832 | tf_op jit(solution)/shard_map/ppermute | solution.py:298
  17.3 4.9 %collective-permute-start.3 = (bf16[768,128]{1,0:T(8,128)(2,1)S(1)}, bf16[768,128]{1,0:T(8,128)(2,1)S(1)}, u32[]{:S(2)}, u32[]{:S(2)}) collective-permute-start(bf16[768,128]{1,0:T(8,128)(2,1)S(1)} %shard_map.39), channel_id=1, source_target_pairs={{0,1},{1,0},{2,3},{3,2},{4,5},{5,4},{6,7},{7,6},{8,9},{9,8},{10,11... | collective-permute-start | bytes 589832 | tf_op jit(solution)/shard_map/ppermute | solution.py:301
  22.3 16.6 %collective-permute-start.7 = (bf16[2,768,128]{2,1,0:T(8,128)(2,1)S(1)}, bf16[2,768,128]{2,1,0:T(8,128)(2,1)S(1)}, u32[]{:S(2)}, u32[]{:S(2)}) collective-permute-start(bf16[2,768,128]{2,1,0:T(8,128)(2,1)S(1)} %pad_maximum_fusion.own_ref), channel_id=1, source_target_pairs={{0,0},{1,96},{2,16},{3,112},{4,8},{5,104},{6,24},{7,120},{8,80},{9... | collective-permute-start | bytes 1179656 | tf_op jit(solution)/shard_map/ppermute | solution.py:303
  28.9 18.9 %collective-permute-start.6 = (bf16[2,768,128]{2,1,0:T(8,128)(2,1)S(1)}, bf16[2,768,128]{2,1,0:T(8,128)(2,1)S(1)}, u32[]{:S(2)}, u32[]{:S(2)}) collective-permute-start(bf16[2,768,128]{2,1,0:T(8,128)(2,1)S(1)} %pad_maximum_fusion.own_ref), channel_id=1, source_target_pairs={{0,4},{4,8},{8,12},{12,0},{1,5},{5,9},{9,13},{13,1},{2,6},{6,10},{... | collective-permute-start | bytes 1179656 | tf_op jit(solution)/shard_map/ppermute | solution.py:306
  30.2 17.7 %collective-permute-start.5 = (bf16[2,768,128]{2,1,0:T(8,128)(2,1)S(1)}, bf16[2,768,128]{2,1,0:T(8,128)(2,1)S(1)}, u32[]{:S(2)}, u32[]{:S(2)}) collective-permute-start(bf16[2,768,128]{2,1,0:T(8,128)(2,1)S(1)} %pad_maximum_fusion.own_ref), channel_id=1, source_target_pairs={{4,0},{8,4},{12,8},{0,12},{5,1},{9,5},{13,9},{1,13},{6,2},{10,6},{... | collective-permute-start | bytes 1179656 | tf_op jit(solution)/shard_map/ppermute | solution.py:305
  31.6 16.3 %collective-permute-start.4 = (bf16[2,768,128]{2,1,0:T(8,128)(2,1)S(1)}, bf16[2,768,128]{2,1,0:T(8,128)(2,1)S(1)}, u32[]{:S(2)}, u32[]{:S(2)}) collective-permute-start(bf16[2,768,128]{2,1,0:T(8,128)(2,1)S(1)} %pad_maximum_fusion.own_ref), channel_id=1, source_target_pairs={{1,2},{2,1},{3,0},{0,3},{5,6},{6,5},{7,4},{4,7},{9,10},{10,9},{11,... | collective-permute-start | bytes 1179656 | tf_op jit(solution)/shard_map/ppermute | solution.py:304
  31.6 1.1 %copy-start = (s32[384,384]{1,0:T(8,128)S(1)}, s32[384,384]{1,0:T(8,128)}, u32[]{:S(2)}) copy-start(s32[384,384]{1,0:T(8,128)} %pattern_ref.1) | copy-start | bytes 1769476
  32.7 0.9 %copy-start.1 = (bf16[256,256]{1,0:T(8,128)(2,1)S(1)}, bf16[256,256]{1,0:T(8,128)(2,1)}, u32[]{:S(2)}) copy-start(bf16[256,256]{1,0:T(8,128)(2,1)} %diag_ref.1) | copy-start | bytes 393220
  38.9 10.0 %collective-permute-start.8 = (bf16[2,768,128]{2,1,0:T(8,128)(2,1)S(1)}, bf16[2,768,128]{2,1,0:T(8,128)(2,1)S(1)}, u32[]{:S(2)}, u32[]{:S(2)}) collective-permute-start(bf16[2,768,128]{2,1,0:T(8,128)(2,1)S(1)} %shard_map.41), channel_id=1, source_target_pairs={{0,16},{16,0},{1,17},{17,1},{2,18},{18,2},{3,19},{19,3},{4,20},{20... | collective-permute-start | bytes 1179656 | tf_op jit(solution)/shard_map/ppermute | solution.py:307
